TPU v7x, 32 devices: a whole 2x2x4 slice. The times are simulated.
32 devices in a mesh: fibre: 8 (over z, x), seg: 4 (over y, core).
Axes of the slice: x: 2, y: 2, z: 4, core: 2. Of those that a mesh axis runs over, the one named last changes fastest.
Arguments:
- strain: float32 [768, 2048], P(('fibre', 'seg')), may hold values from -500 to 500
- fir_taps: float32 [64], replicated, may hold values from -0.75 to 0.75
- space_taps: float32 [31], replicated, may hold values from -1.2 to 1.2
- sources: int32 [3, 4], replicated, may hold values from 0 to 767, as said below
Outputs:
- correlations: float32 [3, 4, 768, 256], P(None, None, ('fibre', 'seg'))
Inputs may be any that keep to these rules, and one draw needn't show every extreme that they name: `sources`: virtual-source channel indices; repeats are allowed.
All inputs are finite; a program needn't handle non-finite values.
Results may differ from a plain program's by a relative error of at most 0.0028.
Values may be sent and summed in bfloat16 or wider, within the bound.
No kernel may reach another device: no remote copies, remote signals or barrier semaphores. Data moves between devices by JAX's collectives and lax.ppermute only.
A program may use at most 64 MiB of HBM per device.

v0:
```python
import functools

import jax
import jax.numpy as jnp
from jax import lax
from jax.experimental import pallas as pl
from jax.experimental.pallas import tpu as pltpu
from jax.sharding import PartitionSpec as P

RUN = 64
LAGS = 256
PANELS = 3
SRC = 4
AXES = ("fibre", "seg")
LANES = 128
STEP = 16
HALO = 16
ROWS = PANELS * SRC
HALF_ROWS = ROWS // 2
VMEM = pl.BlockSpec(memory_space=pltpu.VMEM)
SMEM = pl.BlockSpec(memory_space=pltpu.SMEM)
BF16 = jnp.bfloat16
F32 = jnp.float32


def split(x):
    high = x.astype(BF16)
    return high, (x - high.astype(F32)).astype(BF16)


def split_rows(x):
    high = x.astype(BF16).astype(F32)
    return jnp.concatenate([high, x - high, high], axis=0).astype(BF16)


def split_columns(x):
    high = x.astype(BF16).astype(F32)
    return jnp.concatenate([high, high, x - high], axis=1).astype(BF16)


def taps_at(taps_ref, index):
    total = jnp.zeros(index.shape, F32)
    for j in range(taps_ref.shape[0]):
        total = jnp.where(index == j, taps_ref[j], total)
    return total


def fir_matrix(fir_ref):
    lane = lax.broadcasted_iota(jnp.int32, (8, LANES), 1)
    row = lax.broadcasted_iota(jnp.int32, (8, LANES), 0)
    first = taps_at(fir_ref, lane - row)
    first = jnp.concatenate([first, jnp.zeros_like(first)], axis=1)
    return jnp.concatenate(
        [first if g == 0 else pltpu.roll(first, 8 * g, 1) for g in range(LANES // 8)], axis=0
    )


def to_blocks(x):
    return jnp.concatenate(
        [x[:, k : k + LANES] for k in range(0, x.shape[1], LANES)], axis=0
    )


def from_blocks(x, rows):
    return jnp.concatenate([x[k : k + rows] for k in range(0, x.shape[0], rows)], axis=1)


def earlier(x, rows):
    return jnp.concatenate([jnp.zeros((rows, x.shape[1]), x.dtype), x[:-rows]], axis=0)


def later(x, rows):
    return jnp.concatenate([x[rows:], jnp.zeros((rows, x.shape[1]), x.dtype)], axis=0)


def filter_and_norm(x, fir_both, fir_low):
    rows, samples = x.shape
    high, low = split(to_blocks(x))
    dot = functools.partial(jnp.dot, preferred_element_type=F32)
    full = dot(jnp.concatenate([high, low], axis=1), fir_both) + dot(high, fir_low)
    smooth = full[:, :LANES] + earlier(full[:, LANES:], rows)
    high, low = split(jnp.abs(smooth))
    u = lax.broadcasted_iota(jnp.int32, (2 * LANES, LANES), 0) % LANES
    t = lax.broadcasted_iota(jnp.int32, (2 * LANES, LANES), 1)
    bands = [jnp.abs(u - t) <= RUN, u - t >= LANES - RUN, t - u >= LANES - RUN]
    window = jnp.concatenate([jnp.where(b, 1.0, 0.0).astype(BF16) for b in bands], axis=1)
    sums = dot(jnp.concatenate([high, low], axis=1), window)
    total = (
        sums[:, :LANES]
        + earlier(sums[:, LANES : 2 * LANES], rows)
        + later(sums[:, 2 * LANES :], rows)
    )
    shape = total.shape
    where = lax.broadcasted_iota(jnp.int32, shape, 0) // rows * LANES
    where = where + lax.broadcasted_iota(jnp.int32, shape, 1)
    count = jnp.minimum(where, RUN) + jnp.minimum(samples - 1 - where, RUN) + 1
    level = total / count.astype(F32)
    return from_blocks(smooth / (level + 1e-5), rows)


def pack(x):
    width = x.shape[1] // 4
    tail = x[:, 3 * width :]
    more = [
        jnp.concatenate([tail[k : k + 1] for k in range(3 * g, 3 * g + 3)], axis=1)
        for g in range(2)
    ]
    return jnp.concatenate([x[:, : 3 * width]] + more, axis=0)


def unpack(x):
    width = x.shape[1] // 3
    tail = [x[6 + k // 3 : 7 + k // 3, k % 3 * width : (k % 3 + 1) * width] for k in range(6)]
    return jnp.concatenate([x[:6], jnp.concatenate(tail, axis=0)], axis=1)


def share_kernel(strain_ref, space_ref, sources_ref, keep_ref, send_ref, first_ref, last_ref):
    channels = strain_ref.shape[0]
    me = lax.axis_index(AXES)
    core = me % 2
    half_span = (space_ref.shape[0] - 1) // 2
    x = strain_ref[...]
    first_ref[...] = x[:HALO]
    last_ref[...] = x[channels - HALO :]
    row = lax.broadcasted_iota(jnp.int32, (16, channels), 0)
    lane = lax.broadcasted_iota(jnp.int32, (16, channels), 1)
    source = jnp.full((16, channels), -(1 << 20), jnp.int32)
    for k in range(ROWS):
        half = core if k < HALF_ROWS else 1 - core
        number = half * HALF_ROWS + k % HALF_ROWS
        place = k if k < HALF_ROWS else k - HALF_ROWS + 8
        source = jnp.where(row == place, sources_ref[number // SRC, number % SRC], source)
    matrix = taps_at(space_ref, lane + me * channels - source + half_span)
    share = jnp.dot(split_columns(matrix), split_rows(x), preferred_element_type=F32)
    keep_ref[...] = pack(share[:HALF_ROWS])
    send_ref[...] = pack(share[8 : 8 + HALF_ROWS])


def channels_kernel(
    strain_ref, before_ref, after_ref, fir_ref, space_ref, shifted_ref, both_ref, low_ref
):
    channels, samples = strain_ref.shape
    half_span = (space_ref.shape[0] - 1) // 2
    x = jnp.concatenate([before_ref[...], strain_ref[...], after_ref[...]], axis=0)
    wide = x.shape[0]
    row = lax.broadcasted_iota(jnp.int32, (channels, wide), 0)
    column = lax.broadcasted_iota(jnp.int32, (channels, wide), 1)
    matrix = taps_at(space_ref, column - HALO - row + half_span)
    spaced = jnp.dot(split_columns(matrix), split_rows(x), preferred_element_type=F32)
    high, low = split(fir_matrix(fir_ref))
    both = jnp.concatenate([high, high], axis=0)
    both_ref[...] = both
    low_ref[...] = low
    normed = filter_and_norm(spaced, both, low)
    length = shifted_ref.shape[1]
    padded = jnp.concatenate(
        [
            jnp.zeros((channels, LANES), F32),
            normed,
            jnp.zeros((channels, 2 * LANES), F32),
        ],
        axis=1,
    )
    per_tile = LANES // STEP
    for q in range(0, per_tile, 2):
        turned = [
            padded if k == 0 else pltpu.roll(padded, padded.shape[1] - STEP * k, 1)
            for k in (q, q + 1)
        ]
        pair = jnp.concatenate(turned, axis=0).astype(BF16)
        for h in range(LAGS // LANES):
            at = (h * per_tile + q) * channels
            shifted_ref[at : at + 2 * channels, :] = pair[:, h * LANES : h * LANES + length]


def swap(upper, lower, distance, lane):
    near = (lane // distance) % 2 == 0
    return (
        jnp.where(near, upper, pltpu.roll(lower, distance, 1)),
        jnp.where(near, pltpu.roll(upper, LANES - distance, 1), lower),
    )


def correlate_kernel(mine_ref, other_ref, shifted_ref, both_ref, low_ref, out_ref):
    channels = out_ref.shape[2]
    core = lax.axis_index(AXES) % 2
    mine = unpack(mine_ref[...])
    other = unpack(other_ref[...])
    samples = mine.shape[1]
    even = core == 0
    spaced = jnp.concatenate(
        [
            jnp.where(even, mine, other),
            jnp.where(even, other, mine),
            jnp.zeros((16 - ROWS, samples), F32),
        ],
        axis=0,
    )
    normed = filter_and_norm(spaced, both_ref[...], low_ref[...])
    normed = normed.astype(BF16).astype(F32)
    padded = jnp.concatenate([normed, jnp.zeros((16, LANES), F32)], axis=1)
    lane = lax.broadcasted_iota(jnp.int32, (STEP, LANES), 1)
    row = lax.broadcasted_iota(jnp.int32, (STEP, LANES), 0)
    straight = lane >= row
    records = []
    for k in range(ROWS):
        one = jnp.broadcast_to(padded[k : k + 1], (STEP, padded.shape[1]))
        tiles = [
            pltpu.roll(one[:, j : j + LANES], 0, 1, stride=1, stride_axis=0)
            for j in range(0, padded.shape[1], LANES)
        ]
        previous = [tiles[-1]] + tiles[:-1]
        records.append(
            jnp.concatenate(
                [jnp.where(straight, b, a) for a, b in zip(previous, tiles)], axis=1
            ).astype(BF16)
        )
    records = jnp.concatenate(records, axis=0)
    result = lax.dot_general(
        shifted_ref[...], records, (((1,), (1,)), ((), ())), preferred_element_type=F32
    )
    result = result * float(samples) ** -0.5
    result = jnp.concatenate(
        [result, jnp.zeros((result.shape[0], 2 * LANES - result.shape[1]), F32)], axis=1
    )
    per_tile = LANES // STEP
    lane = lax.broadcasted_iota(jnp.int32, (channels, LANES), 1)
    for h in range(LAGS // LANES):
        for tile in range(2):
            parts = [
                result[
                    (h * per_tile + q) * channels : (h * per_tile + q + 1) * channels,
                    tile * LANES : (tile + 1) * LANES,
                ]
                for q in range(per_tile)
            ]
            for distance in (4, 2, 1):
                for q in range(per_tile):
                    if q & distance == 0:
                        parts[q], parts[q + distance] = swap(
                            parts[q], parts[q + distance], distance * STEP, lane
                        )
            for q in range(per_tile):
                number = tile * per_tile + q
                if number < ROWS:
                    out_ref[number // SRC, number % SRC, :, h * LANES : (h + 1) * LANES] = parts[q]


def local(strain, fir_taps, space_taps, sources):
    channels, samples = strain.shape
    devices = lax.axis_size(AXES)
    packed = jax.ShapeDtypeStruct((8, samples * 3 // 4), F32)
    edge = jax.ShapeDtypeStruct((HALO, samples), F32)
    keep, send, first, last = pl.pallas_call(
        share_kernel,
        out_shape=[packed, packed, edge, edge],
        in_specs=[VMEM, SMEM, SMEM],
        out_specs=[VMEM] * 4,
        name="share",
    )(strain, space_taps, sources)

    def partner(x, distance):
        return lax.ppermute(x, AXES, [(i, i ^ distance) for i in range(devices)])

    total = keep + partner(send, 1)
    up = [(i, i + 1) for i in range(devices - 1)]
    before = lax.ppermute(last, AXES, up)
    after = lax.ppermute(first, AXES, [(j, i) for i, j in up])
    distance = 2
    while distance < devices:
        total = total + partner(total, distance)
        distance *= 2
    other = partner(total, 1)
    length = samples + LANES
    shifted, both, low = pl.pallas_call(
        channels_kernel,
        out_shape=[
            jax.ShapeDtypeStruct((LAGS // STEP * channels, length), BF16),
            jax.ShapeDtypeStruct((2 * LANES, 2 * LANES), BF16),
            jax.ShapeDtypeStruct((LANES, 2 * LANES), BF16),
        ],
        in_specs=[VMEM, VMEM, VMEM, SMEM, SMEM],
        out_specs=[VMEM] * 3,
        name="channels",
    )(strain, before, after, fir_taps, space_taps)
    return pl.pallas_call(
        correlate_kernel,
        out_shape=jax.ShapeDtypeStruct((PANELS, SRC, channels, LAGS), F32),
        in_specs=[VMEM] * 5,
        out_specs=VMEM,
        name="correlate",
    )(total, other, shifted, both, low)


def solution(mesh):
    return jax.shard_map(
        local,
        mesh=mesh,
        in_specs=(P(AXES, None), P(), P(), P()),
        out_specs=P(None, None, AXES, None),
        check_vma=False,
    )
```

profile of v0, /device:TPU:0, one launch (start us, length us, event | category | flops | bytes accessed | tf_op | source)
XLA Modules:
  0.0 38.7 jit_solution(5850880501185613746)
XLA Ops:
  0.0 2.0 %share.1 = (f32[8,1536]{1,0:T(8,128)}, f32[8,1536]{1,0:T(8,128)}, f32[16,2048]{1,0:T(8,128)}, f32[16,2048]{1,0:T(8,128)}) custom-call(f32[24,2048]{1,0:T(8,128)} %strain_ref.3, f32[31]{0:T(128)} %space_ref.3, s32[3,4]{1,0:T(4,128)} %sources_ref.1), custom_call_target="tpu_custom_call" | custom-call | tf_op jit(solution)/shard_map/share/pallas_call | solution.py:254
  2.0 0.5 %collective-permute-start = (f32[8,1536]{1,0:T(8,128)}, f32[8,1536]{1,0:T(8,128)S(1)}, u32[]{:S(2)}, u32[]{:S(2)}) collective-permute-start(f32[8,1536]{1,0:T(8,128)} %get-tuple-element.13), channel_id=1, source_target_pairs={{0,1},{1,0},{2,3},{3,2},{4,5},{5,4},{6,7},{7,6},{8,9},{9,8},{10,11... | collective-permute-start | bytes 147464 | tf_op jit(solution)/shard_map/ppermute | solution.py:263
  2.4 1.1 %collective-permute-done = f32[8,1536]{1,0:T(8,128)S(1)} collective-permute-done((f32[8,1536]{1,0:T(8,128)}, f32[8,1536]{1,0:T(8,128)S(1)}, u32[]{:S(2)}, u32[]{:S(2)}) %collective-permute-start) | collective-permute-done | bytes 49184 | tf_op jit(solution)/shard_map/ppermute | solution.py:263
  3.5 0.8 %add.15 = f32[8,1536]{1,0:T(8,128)S(1)} add(f32[8,1536]{1,0:T(8,128)} %get-tuple-element.12, f32[8,1536]{1,0:T(8,128)S(1)} %collective-permute-done) | non-fusion elementwise | flops 12288 | bytes 147456 | tf_op jit(solution)/shard_map/add | solution.py:265
  4.3 2.9 %collective-permute-start.1 = (f32[8,1536]{1,0:T(8,128)S(1)}, f32[8,1536]{1,0:T(8,128)S(1)}, u32[]{:S(2)}, u32[]{:S(2)}) collective-permute-start(f32[8,1536]{1,0:T(8,128)S(1)} %add.15), channel_id=1, source_target_pairs={{0,2},{1,3},{2,0},{3,1},{4,6},{5,7},{6,4},{7,5},{8,10},{9,11},{10,... | collective-permute-start | bytes 147464 | tf_op jit(solution)/shard_map/ppermute | solution.py:263
  7.2 2.1 %collective-permute-done.1 = f32[8,1536]{1,0:T(8,128)S(1)} collective-permute-done((f32[8,1536]{1,0:T(8,128)S(1)}, f32[8,1536]{1,0:T(8,128)S(1)}, u32[]{:S(2)}, u32[]{:S(2)}) %collective-permute-start.1) | collective-permute-done | bytes 49184 | tf_op jit(solution)/shard_map/ppermute | solution.py:263
  9.3 2.1 %collective-permute-start.2 = (f32[8,1536]{1,0:T(8,128)S(1)}, f32[8,1536]{1,0:T(8,128)S(1)}, u32[]{:S(2)}, u32[]{:S(2)}) collective-permute-start(f32[8,1536]{1,0:T(8,128)S(1)} %add.16), channel_id=1, source_target_pairs={{0,4},{1,5},{2,6},{3,7},{4,0},{5,1},{6,2},{7,3},{8,12},{9,13},{10,... | collective-permute-start | bytes 147464 | tf_op jit(solution)/shard_map/ppermute | solution.py:263
  11.3 2.1 %collective-permute-done.2 = f32[8,1536]{1,0:T(8,128)S(1)} collective-permute-done((f32[8,1536]{1,0:T(8,128)S(1)}, f32[8,1536]{1,0:T(8,128)S(1)}, u32[]{:S(2)}, u32[]{:S(2)}) %collective-permute-start.2) | collective-permute-done | bytes 49184 | tf_op jit(solution)/shard_map/ppermute | solution.py:263
  13.4 2.1 %collective-permute-start.3 = (f32[8,1536]{1,0:T(8,128)S(1)}, f32[8,1536]{1,0:T(8,128)S(1)}, u32[]{:S(2)}, u32[]{:S(2)}) collective-permute-start(f32[8,1536]{1,0:T(8,128)S(1)} %add.17), channel_id=1, source_target_pairs={{0,8},{1,9},{2,10},{3,11},{4,12},{5,13},{6,14},{7,15},{8,0},{9,1},... | collective-permute-start | bytes 147464 | tf_op jit(solution)/shard_map/ppermute | solution.py:263
  15.6 1.3 %collective-permute-start.6 = (f32[16,2048]{1,0:T(8,128)}, f32[16,2048]{1,0:T(8,128)S(1)}, u32[]{:S(2)}, u32[]{:S(2)}) collective-permute-start(f32[16,2048]{1,0:T(8,128)} %get-tuple-element.14), channel_id=1, source_target_pairs={{0,1},{1,2},{2,3},{3,4},{4,5},{5,6},{6,7},{7,8},{8,9},{9,10},{10,1... | collective-permute-start | bytes 393224 | tf_op jit(solution)/shard_map/ppermute | solution.py:267
  16.9 1.3 %collective-permute-start.7 = (f32[16,2048]{1,0:T(8,128)}, f32[16,2048]{1,0:T(8,128)S(1)}, u32[]{:S(2)}, u32[]{:S(2)}) collective-permute-start(f32[16,2048]{1,0:T(8,128)} %get-tuple-element.15), channel_id=1, source_target_pairs={{1,0},{2,1},{3,2},{4,3},{5,4},{6,5},{7,6},{8,7},{9,8},{10,9},{11,1... | collective-permute-start | bytes 393224 | tf_op jit(solution)/shard_map/ppermute | solution.py:268
  18.2 0.0 collective-permute-done.3
  18.2 7.4 %collective-permute-start.4 = (f32[8,1536]{1,0:T(8,128)S(1)}, f32[8,1536]{1,0:T(8,128)S(1)}, u32[]{:S(2)}, u32[]{:S(2)}) collective-permute-start(f32[8,1536]{1,0:T(8,128)S(1)} %add.18), channel_id=1, source_target_pairs={{0,16},{1,17},{2,18},{3,19},{4,20},{5,21},{6,22},{7,23},{8,24},{9,... | collective-permute-start | bytes 147464 | tf_op jit(solution)/shard_map/ppermute | solution.py:263
  25.6 4.1 %collective-permute-done.4 = f32[8,1536]{1,0:T(8,128)S(1)} collective-permute-done((f32[8,1536]{1,0:T(8,128)S(1)}, f32[8,1536]{1,0:T(8,128)S(1)}, u32[]{:S(2)}, u32[]{:S(2)}) %collective-permute-start.4) | collective-permute-done | bytes 49184 | tf_op jit(solution)/shard_map/ppermute | solution.py:263
  29.7 0.0 copy-start
  29.7 0.1 collective-permute-start.5
  29.8 0.0 collective-permute-done.6.before_ref
  29.8 0.0 copy-start.1
  29.8 0.0 collective-permute-done.7.after_ref
  29.8 0.6 %copy-done.1 = f32[16,2048]{1,0:T(8,128)} copy-done((f32[16,2048]{1,0:T(8,128)}, f32[16,2048]{1,0:T(8,128)S(1)}, u32[]{:S(2)}) %copy-start.1) | copy-done | bytes 131096
  30.5 0.0 copy-start.2
  30.5 0.7 %copy-done.2 = f32[16,2048]{1,0:T(8,128)} copy-done((f32[16,2048]{1,0:T(8,128)}, f32[16,2048]{1,0:T(8,128)S(1)}, u32[]{:S(2)}) %copy-start.2) | copy-done | bytes 131096
  31.1 3.2 %channels.1 = (bf16[384,2176]{1,0:T(8,128)(2,1)}, bf16[256,256]{1,0:T(8,128)(2,1)}, bf16[128,256]{1,0:T(8,128)(2,1)}) custom-call(f32[24,2048]{1,0:T(8,128)} %strain_ref.3, f32[16,2048]{1,0:T(8,128)} %copy-done.1, f32[16,2048]{1,0:T(8,128)} %copy-done.2, f32[64]{0:T(128)} %fir_ref.1, f32[31]{0:T(128)} %space_ref.3), custom_call_target="tpu_custom_call" | custom-call | tf_op jit(solution)/shard_map/channels/pallas_call | solution.py:275
  34.4 0.0 collective-permute-done.5.other_ref
  34.4 0.0 copy-start.3
  34.4 0.0 copy-done
  34.4 0.6 %copy-done.3 = f32[8,1536]{1,0:T(8,128)} copy-done((f32[8,1536]{1,0:T(8,128)}, f32[8,1536]{1,0:T(8,128)S(1)}, u32[]{:S(2)}) %copy-start.3) | copy-done | bytes 49176
  35.0 3.7 %correlate.1 = f32[3,4,24,256]{3,2,1,0:T(8,128)} custom-call(f32[8,1536]{1,0:T(8,128)} %copy-done, f32[8,1536]{1,0:T(8,128)} %copy-done.3, bf16[384,2176]{1,0:T(8,128)(2,1)} %get-tuple-element.16.shifted_ref, bf16[256,256]{1,0:T(8,128)(2,1)} %get-tuple-element.17.both_ref, bf16[128,256]{1,0:T(8,128)(2,1)} %get-tuple-element.18.low_ref), custom_call_target="tpu_custom_call" | custom-call | tf_op jit(solution)/shard_map/correlate/pallas_call | solution.py:286
  (4 shorter events, 0.0 us)
Async XLA Ops:
  2.0 1.5 %collective-permute-start = (f32[8,1536]{1,0:T(8,128)}, f32[8,1536]{1,0:T(8,128)S(1)}, u32[]{:S(2)}, u32[]{:S(2)}) collective-permute-start(f32[8,1536]{1,0:T(8,128)} %get-tuple-element.13), channel_id=1, source_target_pairs={{0,1},{1,0},{2,3},{3,2},{4,5},{5,4},{6,7},{7,6},{8,9},{9,8},{10,11... | collective-permute-start | bytes 147464 | tf_op jit(solution)/shard_map/ppermute | solution.py:263
  4.3 4.9 %collective-permute-start.1 = (f32[8,1536]{1,0:T(8,128)S(1)}, f32[8,1536]{1,0:T(8,128)S(1)}, u32[]{:S(2)}, u32[]{:S(2)}) collective-permute-start(f32[8,1536]{1,0:T(8,128)S(1)} %add.15), channel_id=1, source_target_pairs={{0,2},{1,3},{2,0},{3,1},{4,6},{5,7},{6,4},{7,5},{8,10},{9,11},{10,... | collective-permute-start | bytes 147464 | tf_op jit(solution)/shard_map/ppermute | solution.py:263
  9.3 4.2 %collective-permute-start.2 = (f32[8,1536]{1,0:T(8,128)S(1)}, f32[8,1536]{1,0:T(8,128)S(1)}, u32[]{:S(2)}, u32[]{:S(2)}) collective-permute-start(f32[8,1536]{1,0:T(8,128)S(1)} %add.16), channel_id=1, source_target_pairs={{0,4},{1,5},{2,6},{3,7},{4,0},{5,1},{6,2},{7,3},{8,12},{9,13},{10,... | collective-permute-start | bytes 147464 | tf_op jit(solution)/shard_map/ppermute | solution.py:263
  13.4 4.7 %collective-permute-start.3 = (f32[8,1536]{1,0:T(8,128)S(1)}, f32[8,1536]{1,0:T(8,128)S(1)}, u32[]{:S(2)}, u32[]{:S(2)}) collective-permute-start(f32[8,1536]{1,0:T(8,128)S(1)} %add.17), channel_id=1, source_target_pairs={{0,8},{1,9},{2,10},{3,11},{4,12},{5,13},{6,14},{7,15},{8,0},{9,1},... | collective-permute-start | bytes 147464 | tf_op jit(solution)/shard_map/ppermute | solution.py:263
  15.6 14.2 %collective-permute-start.6 = (f32[16,2048]{1,0:T(8,128)}, f32[16,2048]{1,0:T(8,128)S(1)}, u32[]{:S(2)}, u32[]{:S(2)}) collective-permute-start(f32[16,2048]{1,0:T(8,128)} %get-tuple-element.14), channel_id=1, source_target_pairs={{0,1},{1,2},{2,3},{3,4},{4,5},{5,6},{6,7},{7,8},{8,9},{9,10},{10,1... | collective-permute-start | bytes 393224 | tf_op jit(solution)/shard_map/ppermute | solution.py:267
  16.9 13.0 %collective-permute-start.7 = (f32[16,2048]{1,0:T(8,128)}, f32[16,2048]{1,0:T(8,128)S(1)}, u32[]{:S(2)}, u32[]{:S(2)}) collective-permute-start(f32[16,2048]{1,0:T(8,128)} %get-tuple-element.15), channel_id=1, source_target_pairs={{1,0},{2,1},{3,2},{4,3},{5,4},{6,5},{7,6},{8,7},{9,8},{10,9},{11,1... | collective-permute-start | bytes 393224 | tf_op jit(solution)/shard_map/ppermute | solution.py:268
  18.2 11.5 %collective-permute-start.4 = (f32[8,1536]{1,0:T(8,128)S(1)}, f32[8,1536]{1,0:T(8,128)S(1)}, u32[]{:S(2)}, u32[]{:S(2)}) collective-permute-start(f32[8,1536]{1,0:T(8,128)S(1)} %add.18), channel_id=1, source_target_pairs={{0,16},{1,17},{2,18},{3,19},{4,20},{5,21},{6,22},{7,23},{8,24},{9,... | collective-permute-start | bytes 147464 | tf_op jit(solution)/shard_map/ppermute | solution.py:263
  29.7 4.6 %copy-start = (f32[8,1536]{1,0:T(8,128)}, f32[8,1536]{1,0:T(8,128)S(1)}, u32[]{:S(2)}) copy-start(f32[8,1536]{1,0:T(8,128)S(1)} %add.19.mine_ref) | copy-start | bytes 147460
  29.7 4.6 %collective-permute-start.5 = (f32[8,1536]{1,0:T(8,128)S(1)}, f32[8,1536]{1,0:T(8,128)S(1)}, u32[]{:S(2)}, u32[]{:S(2)}) collective-permute-start(f32[8,1536]{1,0:T(8,128)S(1)} %add.19.mine_ref), channel_id=1, source_target_pairs={{0,1},{1,0},{2,3},{3,2},{4,5},{5,4},{6,7},{7,6},{8,9},{9,8},{10,11... | collective-permute-start | bytes 147464 | tf_op jit(solution)/shard_map/ppermute | solution.py:263
  29.8 0.7 %copy-start.1 = (f32[16,2048]{1,0:T(8,128)}, f32[16,2048]{1,0:T(8,128)S(1)}, u32[]{:S(2)}) copy-start(f32[16,2048]{1,0:T(8,128)S(1)} %collective-permute-done.6.before_ref) | copy-start | bytes 393220
  30.5 0.7 %copy-start.2 = (f32[16,2048]{1,0:T(8,128)}, f32[16,2048]{1,0:T(8,128)S(1)}, u32[]{:S(2)}) copy-start(f32[16,2048]{1,0:T(8,128)S(1)} %collective-permute-done.7.after_ref) | copy-start | bytes 393220
  34.4 0.6 %copy-start.3 = (f32[8,1536]{1,0:T(8,128)}, f32[8,1536]{1,0:T(8,128)S(1)}, u32[]{:S(2)}) copy-start(f32[8,1536]{1,0:T(8,128)S(1)} %collective-permute-done.5.other_ref) | copy-start | bytes 147460
where the time goes:
time: 39 us; the launch traced here: 38.7 us
  starting transfers between devices  17.6 us (45%)
  waiting for transfers between devices  9.35 us (24%)
  Pallas kernels  8.92 us (23%)
  local copies, waits for them, and re-layouts  1.9 us (5%)
  other arithmetic  0.84 us (2%)
    ppermute x6, starting transfers between devices, partner(): return lax.ppermute(x, AXES, [(i, i ^ distance) for i in range(devices)])  15 us
    ppermute x6, waiting for transfers between devices, partner(): return lax.ppermute(x, AXES, [(i, i ^ distance) for i in range(devices)])  9.35 us
    pallas_call x1, Pallas kernels, local(): pl.pallas_call(correlate_kernel, out_shape=jax.ShapeDtypeStruct((PANELS,...  3.71 us
    pallas_call x1, Pallas kernels, local(): pl.pallas_call(channels_kernel, out_shape=[jax.ShapeDtypeStruct((LAGS //...  3.23 us
    pallas_call x1, Pallas kernels, local(): pl.pallas_call(share_kernel, out_shape=[packed, packed, edge, edge], in_s...  1.98 us
    unnamed x8, local copies, waits for them, and re-layouts  1.9 us
    ppermute x1, starting transfers between devices, local(): after = lax.ppermute(first, AXES, [(j, i) for i, j in up])  1.29 us
    ppermute x1, starting transfers between devices, local(): before = lax.ppermute(last, AXES, up)  1.28 us
  transfers between devices with their start and end apart: 8, of which 4 were waited for; matrix products, arithmetic and copies ran while one was open for 0% of the time, Pallas kernels for 8%

commit v1 on v0

--- a/solution.py
+++ b/solution.py
@@ -18,7 +18,8 @@
 ROWS = PANELS * SRC
 HALF_ROWS = ROWS // 2
 VMEM = pl.BlockSpec(memory_space=pltpu.VMEM)
-SMEM = pl.BlockSpec(memory_space=pltpu.SMEM)
+HBM = pl.BlockSpec(memory_space=pltpu.HBM)
+SMALL = pltpu.CompilerParams(vmem_limit_bytes=16 * 2**20)
 BF16 = jnp.bfloat16
 F32 = jnp.float32
 
@@ -114,14 +115,35 @@
     return jnp.concatenate([x[:6], jnp.concatenate(tail, axis=0)], axis=1)
 
 
-def share_kernel(strain_ref, space_ref, sources_ref, keep_ref, send_ref, first_ref, last_ref):
+def fetch(pairs, sems):
+    copies = [pltpu.make_async_copy(a, b, sems.at[i]) for i, (a, b) in enumerate(pairs)]
+    for copy in copies:
+        copy.start()
+    return copies
+
+
+def share_kernel(
+    strain_hbm,
+    space_hbm,
+    sources_hbm,
+    keep_ref,
+    send_ref,
+    inner_ref,
+    outer_ref,
+    strain_ref,
+    space_ref,
+    sources_ref,
+    sems,
+):
+    copies = fetch(
+        [(sources_hbm, sources_ref), (space_hbm, space_ref), (strain_hbm, strain_ref)], sems
+    )
     channels = strain_ref.shape[0]
     me = lax.axis_index(AXES)
     core = me % 2
     half_span = (space_ref.shape[0] - 1) // 2
-    x = strain_ref[...]
-    first_ref[...] = x[:HALO]
-    last_ref[...] = x[channels - HALO :]
+    even = core == 0
+    copies[0].wait()
     row = lax.broadcasted_iota(jnp.int32, (16, channels), 0)
     lane = lax.broadcasted_iota(jnp.int32, (16, channels), 1)
     source = jnp.full((16, channels), -(1 << 20), jnp.int32)
@@ -130,23 +152,44 @@
         number = half * HALF_ROWS + k % HALF_ROWS
         place = k if k < HALF_ROWS else k - HALF_ROWS + 8
         source = jnp.where(row == place, sources_ref[number // SRC, number % SRC], source)
+    copies[1].wait()
     matrix = taps_at(space_ref, lane + me * channels - source + half_span)
+    copies[2].wait()
+    x = strain_ref[...]
+    inner_ref[...] = jnp.where(even, x[channels - HALO :], x[:HALO])
+    outer_ref[...] = jnp.where(even, x[:HALO], x[channels - HALO :])
     share = jnp.dot(split_columns(matrix), split_rows(x), preferred_element_type=F32)
     keep_ref[...] = pack(share[:HALF_ROWS])
     send_ref[...] = pack(share[8 : 8 + HALF_ROWS])
 
 
 def channels_kernel(
-    strain_ref, before_ref, after_ref, fir_ref, space_ref, shifted_ref, both_ref, low_ref
+    strain_ref,
+    inner_ref,
+    outer_ref,
+    fir_hbm,
+    space_hbm,
+    shifted_ref,
+    both_ref,
+    low_ref,
+    fir_ref,
+    space_ref,
+    sems,
 ):
+    copies = fetch([(space_hbm, space_ref), (fir_hbm, fir_ref)], sems)
     channels, samples = strain_ref.shape
     half_span = (space_ref.shape[0] - 1) // 2
-    x = jnp.concatenate([before_ref[...], strain_ref[...], after_ref[...]], axis=0)
+    even = lax.axis_index(AXES) % 2 == 0
+    inner, outer = inner_ref[...], outer_ref[...]
+    before, after = jnp.where(even, outer, inner), jnp.where(even, inner, outer)
+    x = jnp.concatenate([before, strain_ref[...], after], axis=0)
     wide = x.shape[0]
     row = lax.broadcasted_iota(jnp.int32, (channels, wide), 0)
     column = lax.broadcasted_iota(jnp.int32, (channels, wide), 1)
+    copies[0].wait()
     matrix = taps_at(space_ref, column - HALO - row + half_span)
     spaced = jnp.dot(split_columns(matrix), split_rows(x), preferred_element_type=F32)
+    copies[1].wait()
     high, low = split(fir_matrix(fir_ref))
     both = jnp.concatenate([high, high], axis=0)
     both_ref[...] = both
@@ -246,31 +289,38 @@
                     out_ref[number // SRC, number % SRC, :, h * LANES : (h + 1) * LANES] = parts[q]
 
 
+def in_hbm(x):
+    return pltpu.with_memory_space_constraint(x, pltpu.HBM)
+
+
 def local(strain, fir_taps, space_taps, sources):
     channels, samples = strain.shape
     devices = lax.axis_size(AXES)
     packed = jax.ShapeDtypeStruct((8, samples * 3 // 4), F32)
     edge = jax.ShapeDtypeStruct((HALO, samples), F32)
-    keep, send, first, last = pl.pallas_call(
+    near = jax.ShapeDtypeStruct(strain.shape, F32)
+    keep, send, inner, outer, near = pl.pallas_call(
         share_kernel,
-        out_shape=[packed, packed, edge, edge],
-        in_specs=[VMEM, SMEM, SMEM],
-        out_specs=[VMEM] * 4,
+        out_shape=[packed, packed, edge, edge, near],
+        in_specs=[HBM] * 3,
+        out_specs=[VMEM] * 5,
+        scratch_shapes=[
+            pltpu.SMEM(space_taps.shape, F32),
+            pltpu.SMEM(sources.shape, jnp.int32),
+            pltpu.SemaphoreType.DMA((3,)),
+        ],
+        compiler_params=SMALL,
         name="share",
-    )(strain, space_taps, sources)
+    )(*[in_hbm(x) for x in (strain, space_taps, sources)])
 
     def partner(x, distance):
         return lax.ppermute(x, AXES, [(i, i ^ distance) for i in range(devices)])
 
     total = keep + partner(send, 1)
-    up = [(i, i + 1) for i in range(devices - 1)]
-    before = lax.ppermute(last, AXES, up)
-    after = lax.ppermute(first, AXES, [(j, i) for i, j in up])
-    distance = 2
-    while distance < devices:
-        total = total + partner(total, distance)
-        distance *= 2
-    other = partner(total, 1)
+    total, inner, outer = lax.optimization_barrier((total, inner, outer))
+    inner = partner(inner, 1)
+    across = [(i, i + 1) for i in range(1, devices - 1, 2)]
+    outer = lax.ppermute(outer, AXES, across + [(j, i) for i, j in across])
     length = samples + LANES
     shifted, both, low = pl.pallas_call(
         channels_kernel,
@@ -279,15 +329,29 @@
             jax.ShapeDtypeStruct((2 * LANES, 2 * LANES), BF16),
             jax.ShapeDtypeStruct((LANES, 2 * LANES), BF16),
         ],
-        in_specs=[VMEM, VMEM, VMEM, SMEM, SMEM],
+        in_specs=[VMEM] * 3 + [HBM] * 2,
         out_specs=[VMEM] * 3,
+        scratch_shapes=[
+            pltpu.SMEM(fir_taps.shape, F32),
+            pltpu.SMEM(space_taps.shape, F32),
+            pltpu.SemaphoreType.DMA((2,)),
+        ],
+        compiler_params=SMALL,
         name="channels",
-    )(strain, before, after, fir_taps, space_taps)
+    )(near, inner, outer, in_hbm(fir_taps), in_hbm(space_taps))
+    distance = 2
+    while distance < devices:
+        if distance == 16:
+            total, shifted, both, low = lax.optimization_barrier((total, shifted, both, low))
+        total = total + partner(total, distance)
+        distance *= 2
+    other = partner(total, 1)
     return pl.pallas_call(
         correlate_kernel,
         out_shape=jax.ShapeDtypeStruct((PANELS, SRC, channels, LAGS), F32),
         in_specs=[VMEM] * 5,
         out_specs=VMEM,
+        compiler_params=SMALL,
         name="correlate",
     )(total, other, shifted, both, low)
 

time: 39 us -> 25.9 us (0.66)
  starting transfers between devices: 17.6 us -> 10.8 us
  Pallas kernels: 8.92 us -> 5.17 us
  local copies, waits for them, and re-layouts: 1.9 us -> 0 us
  other arithmetic: 0.84 us -> 0.04 us
    ppermute x6 -> x7, starting transfers between devices: 15 us -> 10.1 us  [partner(): return lax.ppermute(x, AXES, [(i, i ^ distance) for i in range(devices)])]
    ppermute x2 -> x1, starting transfers between devices: 2.58 us -> 0.66 us  [local(): outer = lax.ppermute(outer, AXES, across + [(j, i) for i, j in across])]
    unnamed x8 -> x0, local copies, waits for them, and re-layouts: 1.9 us -> none
    pallas_call x1, Pallas kernels: 3.71 us -> 2.13 us  [local(): pl.pallas_call(correlate_kernel, out_shape=jax.ShapeDtypeStruct((PANELS,...]
    pallas_call x1, Pallas kernels: 3.23 us -> 1.86 us  [local(): pl.pallas_call(channels_kernel, out_shape=[jax.ShapeDtypeStruct((LAGS //...]
    add x1, other arithmetic: 0.81 us -> 0.01 us  [local(): total = keep + partner(send, 1)]
    pallas_call x1, Pallas kernels: 1.98 us -> 1.19 us  [local(): pl.pallas_call(share_kernel, out_shape=[packed, packed, edge, edge, near]...]
    ppermute x6 -> x7, waiting for transfers between devices: 9.35 us -> 9.67 us  [partner(): return lax.ppermute(x, AXES, [(i, i ^ distance) for i in range(devices)])]
  transfers between devices with their start and end apart: 8 -> 8, of which waited for: 4 -> 6; matrix products, arithmetic and copies ran while one was open for 0% -> 0% of each run, Pallas kernels for 8% -> 7%
where the time goes in v1:
time: 25.9 us; the launch traced here: 25.7 us
  starting transfers between devices  10.8 us (42%)
  waiting for transfers between devices  9.67 us (37%)
  Pallas kernels  5.17 us (20%)
    ppermute x7, starting transfers between devices, partner(): return lax.ppermute(x, AXES, [(i, i ^ distance) for i in range(devices)])  10.1 us
    ppermute x7, waiting for transfers between devices, partner(): return lax.ppermute(x, AXES, [(i, i ^ distance) for i in range(devices)])  9.67 us
    pallas_call x1, Pallas kernels, local(): pl.pallas_call(correlate_kernel, out_shape=jax.ShapeDtypeStruct((PANELS,...  2.13 us
    pallas_call x1, Pallas kernels, local(): pl.pallas_call(channels_kernel, out_shape=[jax.ShapeDtypeStruct((LAGS //...  1.86 us
    pallas_call x1, Pallas kernels, local(): pl.pallas_call(share_kernel, out_shape=[packed, packed, edge, edge, near]...  1.19 us
    ppermute x1, starting transfers between devices, local(): outer = lax.ppermute(outer, AXES, across + [(j, i) for i, j in across])  0.66 us
  transfers between devices with their start and end apart: 8, of which 6 were waited for; matrix products, arithmetic and copies ran while one was open for 0% of the time, Pallas kernels for 7%

profile of v1, /device:TPU:0, one launch (start us, length us, event | category | flops | bytes accessed | tf_op | source)
XLA Modules:
  0.0 25.7 jit_solution(12526384558701581164)
XLA Ops:
  0.0 1.2 %share.1 = (f32[8,1536]{1,0:T(8,128)S(1)}, f32[8,1536]{1,0:T(8,128)S(1)}, f32[16,2048]{1,0:T(8,128)S(1)}, f32[16,2048]{1,0:T(8,128)S(1)}, f32[24,2048]{1,0:T(8,128)S(1)}) custom-call(f32[24,2048]{1,0:T(8,128)} %strain_hbm.1, f32[31]{0:T(128)} %space_hbm.3, s32[3,4]{1,0:T(4,128)} %sources_hbm.1), custom_call_target="tpu_custom_call" | custom-call | tf_op jit(solution)/shard_map/share/pallas_call | solution.py:302
  1.2 0.5 %collective-permute-start = (f32[8,1536]{1,0:T(8,128)S(1)}, f32[8,1536]{1,0:T(8,128)S(1)}, u32[]{:S(2)}, u32[]{:S(2)}) collective-permute-start(f32[8,1536]{1,0:T(8,128)S(1)} %get-tuple-element.21), channel_id=1, source_target_pairs={{0,1},{1,0},{2,3},{3,2},{4,5},{5,4},{6,7},{7,6},{8,9},{9,8},{10,11... | collective-permute-start | bytes 147464 | tf_op jit(solution)/shard_map/ppermute | solution.py:317
  1.7 0.9 %collective-permute-done = f32[8,1536]{1,0:T(8,128)S(1)} collective-permute-done((f32[8,1536]{1,0:T(8,128)S(1)}, f32[8,1536]{1,0:T(8,128)S(1)}, u32[]{:S(2)}, u32[]{:S(2)}) %collective-permute-start) | collective-permute-done | bytes 49184 | tf_op jit(solution)/shard_map/ppermute | solution.py:317
  2.6 2.9 %collective-permute-start.1 = (f32[8,1536]{1,0:T(8,128)S(1)}, f32[8,1536]{1,0:T(8,128)S(1)}, u32[]{:S(2)}, u32[]{:S(2)}) collective-permute-start(f32[8,1536]{1,0:T(8,128)S(1)} %add.15), channel_id=1, source_target_pairs={{0,2},{1,3},{2,0},{3,1},{4,6},{5,7},{6,4},{7,5},{8,10},{9,11},{10,... | collective-permute-start | bytes 147464 | tf_op jit(solution)/shard_map/ppermute | solution.py:317
  5.5 0.0 collective-permute-start.4
  5.5 0.7 %collective-permute-start.5 = (f32[16,2048]{1,0:T(8,128)S(1)}, f32[16,2048]{1,0:T(8,128)S(1)}, u32[]{:S(2)}, u32[]{:S(2)}) collective-permute-start(f32[16,2048]{1,0:T(8,128)S(1)} %get-tuple-element.27), channel_id=1, source_target_pairs={{1,2},{3,4},{5,6},{7,8},{9,10},{11,12},{13,14},{15,16},{17,18},{19... | collective-permute-start | bytes 393224 | tf_op jit(solution)/shard_map/ppermute | solution.py:323
  6.2 1.4 %collective-permute-done.1 = f32[8,1536]{1,0:T(8,128)S(1)} collective-permute-done((f32[8,1536]{1,0:T(8,128)S(1)}, f32[8,1536]{1,0:T(8,128)S(1)}, u32[]{:S(2)}, u32[]{:S(2)}) %collective-permute-start.1) | collective-permute-done | bytes 49184 | tf_op jit(solution)/shard_map/ppermute | solution.py:317
  7.6 2.1 %collective-permute-start.2 = (f32[8,1536]{1,0:T(8,128)S(1)}, f32[8,1536]{1,0:T(8,128)S(1)}, u32[]{:S(2)}, u32[]{:S(2)}) collective-permute-start(f32[8,1536]{1,0:T(8,128)S(1)} %add.16), channel_id=1, source_target_pairs={{0,4},{1,5},{2,6},{3,7},{4,0},{5,1},{6,2},{7,3},{8,12},{9,13},{10,... | collective-permute-start | bytes 147464 | tf_op jit(solution)/shard_map/ppermute | solution.py:317
  9.7 3.4 %collective-permute-done.2 = f32[8,1536]{1,0:T(8,128)S(1)} collective-permute-done((f32[8,1536]{1,0:T(8,128)S(1)}, f32[8,1536]{1,0:T(8,128)S(1)}, u32[]{:S(2)}, u32[]{:S(2)}) %collective-permute-start.2) | collective-permute-done | bytes 49184 | tf_op jit(solution)/shard_map/ppermute | solution.py:317
  13.1 1.8 %collective-permute-start.3 = (f32[8,1536]{1,0:T(8,128)S(1)}, f32[8,1536]{1,0:T(8,128)S(1)}, u32[]{:S(2)}, u32[]{:S(2)}) collective-permute-start(f32[8,1536]{1,0:T(8,128)S(1)} %add.17), channel_id=1, source_target_pairs={{0,8},{1,9},{2,10},{3,11},{4,12},{5,13},{6,14},{7,15},{8,0},{9,1},... | collective-permute-start | bytes 147464 | tf_op jit(solution)/shard_map/ppermute | solution.py:317
  14.9 0.0 collective-permute-done.4.inner_ref
  14.9 0.0 collective-permute-done.5.outer_ref
  14.9 1.9 %channels.1 = (bf16[384,2176]{1,0:T(8,128)(2,1)S(1)}, bf16[256,256]{1,0:T(8,128)(2,1)S(1)}, bf16[128,256]{1,0:T(8,128)(2,1)S(1)}) custom-call(f32[24,2048]{1,0:T(8,128)S(1)} %get-tuple-element.25.strain_ref, f32[16,2048]{1,0:T(8,128)S(1)} %collective-permute-done.4.inner_ref, f32[16,2048]{1,0:T(8,128)S(1)} %collective-permute-done.5.outer_ref, f32[64]{0:T(128)} %fir_hbm.1, ...), custom_call_target="tpu_custom_call" | custom-call | tf_op jit(solution)/shard_map/channels/pallas_call | solution.py:325
  16.7 0.5 %collective-permute-done.3 = f32[8,1536]{1,0:T(8,128)S(1)} collective-permute-done((f32[8,1536]{1,0:T(8,128)S(1)}, f32[8,1536]{1,0:T(8,128)S(1)}, u32[]{:S(2)}, u32[]{:S(2)}) %collective-permute-start.3) | collective-permute-done | bytes 49184 | tf_op jit(solution)/shard_map/ppermute | solution.py:317
  17.2 2.8 %collective-permute-start.6 = (f32[8,1536]{1,0:T(8,128)S(1)}, f32[8,1536]{1,0:T(8,128)S(1)}, u32[]{:S(2)}, u32[]{:S(2)}) collective-permute-start(f32[8,1536]{1,0:T(8,128)S(1)} %add.18), channel_id=1, source_target_pairs={{0,16},{1,17},{2,18},{3,19},{4,20},{5,21},{6,22},{7,23},{8,24},{9,... | collective-permute-start | bytes 147464 | tf_op jit(solution)/shard_map/ppermute | solution.py:317
  20.0 2.3 %collective-permute-done.6 = f32[8,1536]{1,0:T(8,128)S(1)} collective-permute-done((f32[8,1536]{1,0:T(8,128)S(1)}, f32[8,1536]{1,0:T(8,128)S(1)}, u32[]{:S(2)}, u32[]{:S(2)}) %collective-permute-start.6) | collective-permute-done | bytes 49184 | tf_op jit(solution)/shard_map/ppermute | solution.py:317
  22.3 0.1 collective-permute-start.7
  22.4 1.2 %collective-permute-done.7.other_ref = f32[8,1536]{1,0:T(8,128)S(1)} collective-permute-done((f32[8,1536]{1,0:T(8,128)S(1)}, f32[8,1536]{1,0:T(8,128)S(1)}, u32[]{:S(2)}, u32[]{:S(2)}) %collective-permute-start.7) | collective-permute-done | bytes 49184 | tf_op jit(solution)/shard_map/ppermute | solution.py:317
  23.6 2.1 %correlate.1 = f32[3,4,24,256]{3,2,1,0:T(8,128)} custom-call(f32[8,1536]{1,0:T(8,128)S(1)} %add.19.mine_ref, f32[8,1536]{1,0:T(8,128)S(1)} %collective-permute-done.7.other_ref, bf16[384,2176]{1,0:T(8,128)(2,1)S(1)} %get-tuple-element.32.shifted_ref, bf16[256,256]{1,0:T(8,128)(2,1)S(1)} %get-tuple-element.33.both_ref, ...), custom_call_target="tpu_custom_call" | custom-call | tf_op jit(solution)/shard_map/correlate/pallas_call | solution.py:349
  (5 shorter events, 0.0 us)
Async XLA Ops:
  1.2 1.4 %collective-permute-start = (f32[8,1536]{1,0:T(8,128)S(1)}, f32[8,1536]{1,0:T(8,128)S(1)}, u32[]{:S(2)}, u32[]{:S(2)}) collective-permute-start(f32[8,1536]{1,0:T(8,128)S(1)} %get-tuple-element.21), channel_id=1, source_target_pairs={{0,1},{1,0},{2,3},{3,2},{4,5},{5,4},{6,7},{7,6},{8,9},{9,8},{10,11... | collective-permute-start | bytes 147464 | tf_op jit(solution)/shard_map/ppermute | solution.py:317
  2.6 5.0 %collective-permute-start.1 = (f32[8,1536]{1,0:T(8,128)S(1)}, f32[8,1536]{1,0:T(8,128)S(1)}, u32[]{:S(2)}, u32[]{:S(2)}) collective-permute-start(f32[8,1536]{1,0:T(8,128)S(1)} %add.15), channel_id=1, source_target_pairs={{0,2},{1,3},{2,0},{3,1},{4,6},{5,7},{6,4},{7,5},{8,10},{9,11},{10,... | collective-permute-start | bytes 147464 | tf_op jit(solution)/shard_map/ppermute | solution.py:317
  5.5 9.3 %collective-permute-start.4 = (f32[16,2048]{1,0:T(8,128)S(1)}, f32[16,2048]{1,0:T(8,128)S(1)}, u32[]{:S(2)}, u32[]{:S(2)}) collective-permute-start(f32[16,2048]{1,0:T(8,128)S(1)} %get-tuple-element.26), channel_id=1, source_target_pairs={{0,1},{1,0},{2,3},{3,2},{4,5},{5,4},{6,7},{7,6},{8,9},{9,8},{10,11... | collective-permute-start | bytes 393224 | tf_op jit(solution)/shard_map/ppermute | solution.py:317
  5.5 9.3 %collective-permute-start.5 = (f32[16,2048]{1,0:T(8,128)S(1)}, f32[16,2048]{1,0:T(8,128)S(1)}, u32[]{:S(2)}, u32[]{:S(2)}) collective-permute-start(f32[16,2048]{1,0:T(8,128)S(1)} %get-tuple-element.27), channel_id=1, source_target_pairs={{1,2},{3,4},{5,6},{7,8},{9,10},{11,12},{13,14},{15,16},{17,18},{19... | collective-permute-start | bytes 393224 | tf_op jit(solution)/shard_map/ppermute | solution.py:323
  7.6 5.5 %collective-permute-start.2 = (f32[8,1536]{1,0:T(8,128)S(1)}, f32[8,1536]{1,0:T(8,128)S(1)}, u32[]{:S(2)}, u32[]{:S(2)}) collective-permute-start(f32[8,1536]{1,0:T(8,128)S(1)} %add.16), channel_id=1, source_target_pairs={{0,4},{1,5},{2,6},{3,7},{4,0},{5,1},{6,2},{7,3},{8,12},{9,13},{10,... | collective-permute-start | bytes 147464 | tf_op jit(solution)/shard_map/ppermute | solution.py:317
  13.1 4.2 %collective-permute-start.3 = (f32[8,1536]{1,0:T(8,128)S(1)}, f32[8,1536]{1,0:T(8,128)S(1)}, u32[]{:S(2)}, u32[]{:S(2)}) collective-permute-start(f32[8,1536]{1,0:T(8,128)S(1)} %add.17), channel_id=1, source_target_pairs={{0,8},{1,9},{2,10},{3,11},{4,12},{5,13},{6,14},{7,15},{8,0},{9,1},... | collective-permute-start | bytes 147464 | tf_op jit(solution)/shard_map/ppermute | solution.py:317
  17.2 5.0 %collective-permute-start.6 = (f32[8,1536]{1,0:T(8,128)S(1)}, f32[8,1536]{1,0:T(8,128)S(1)}, u32[]{:S(2)}, u32[]{:S(2)}) collective-permute-start(f32[8,1536]{1,0:T(8,128)S(1)} %add.18), channel_id=1, source_target_pairs={{0,16},{1,17},{2,18},{3,19},{4,20},{5,21},{6,22},{7,23},{8,24},{9,... | collective-permute-start | bytes 147464 | tf_op jit(solution)/shard_map/ppermute | solution.py:317
  22.3 1.3 %collective-permute-start.7 = (f32[8,1536]{1,0:T(8,128)S(1)}, f32[8,1536]{1,0:T(8,128)S(1)}, u32[]{:S(2)}, u32[]{:S(2)}) collective-permute-start(f32[8,1536]{1,0:T(8,128)S(1)} %add.19.mine_ref), channel_id=1, source_target_pairs={{0,1},{1,0},{2,3},{3,2},{4,5},{5,4},{6,7},{7,6},{8,9},{9,8},{10,11... | collective-permute-start | bytes 147464 | tf_op jit(solution)/shard_map/ppermute | solution.py:317

commit v2 on v1

--- a/solution.py
+++ b/solution.py
@@ -115,6 +115,13 @@
     return jnp.concatenate([x[:6], jnp.concatenate(tail, axis=0)], axis=1)
 
 
+def parity(number):
+    total = 0
+    for k in range(16):
+        total = total ^ (number >> k)
+    return total & 1
+
+
 def fetch(pairs, sems):
     copies = [pltpu.make_async_copy(a, b, sems.at[i]) for i, (a, b) in enumerate(pairs)]
     for copy in copies:
@@ -140,15 +147,15 @@
     )
     channels = strain_ref.shape[0]
     me = lax.axis_index(AXES)
-    core = me % 2
+    mine = parity(me)
     half_span = (space_ref.shape[0] - 1) // 2
-    even = core == 0
+    even = me % 2 == 0
     copies[0].wait()
     row = lax.broadcasted_iota(jnp.int32, (16, channels), 0)
     lane = lax.broadcasted_iota(jnp.int32, (16, channels), 1)
     source = jnp.full((16, channels), -(1 << 20), jnp.int32)
     for k in range(ROWS):
-        half = core if k < HALF_ROWS else 1 - core
+        half = mine if k < HALF_ROWS else 1 - mine
         number = half * HALF_ROWS + k % HALF_ROWS
         place = k if k < HALF_ROWS else k - HALF_ROWS + 8
         source = jnp.where(row == place, sources_ref[number // SRC, number % SRC], source)
@@ -179,8 +186,10 @@
     copies = fetch([(space_hbm, space_ref), (fir_hbm, fir_ref)], sems)
     channels, samples = strain_ref.shape
     half_span = (space_ref.shape[0] - 1) // 2
-    even = lax.axis_index(AXES) % 2 == 0
+    me = lax.axis_index(AXES)
+    even = me % 2 == 0
     inner, outer = inner_ref[...], outer_ref[...]
+    outer = jnp.where((me == 0) | (me == lax.axis_size(AXES) - 1), 0.0, outer)
     before, after = jnp.where(even, outer, inner), jnp.where(even, inner, outer)
     x = jnp.concatenate([before, strain_ref[...], after], axis=0)
     wide = x.shape[0]
@@ -226,11 +235,10 @@
 
 def correlate_kernel(mine_ref, other_ref, shifted_ref, both_ref, low_ref, out_ref):
     channels = out_ref.shape[2]
-    core = lax.axis_index(AXES) % 2
     mine = unpack(mine_ref[...])
     other = unpack(other_ref[...])
     samples = mine.shape[1]
-    even = core == 0
+    even = parity(lax.axis_index(AXES)) == 0
     spaced = jnp.concatenate(
         [
             jnp.where(even, mine, other),
@@ -293,6 +301,28 @@
     return pltpu.with_memory_space_constraint(x, pltpu.HBM)
 
 
+def channels_call(near, inner, outer, fir_taps, space_taps):
+    channels, samples = near.shape
+    length = samples + LANES
+    return pl.pallas_call(
+        channels_kernel,
+        out_shape=[
+            jax.ShapeDtypeStruct((LAGS // STEP * channels, length), BF16),
+            jax.ShapeDtypeStruct((2 * LANES, 2 * LANES), BF16),
+            jax.ShapeDtypeStruct((LANES, 2 * LANES), BF16),
+        ],
+        in_specs=[VMEM] * 3 + [HBM] * 2,
+        out_specs=[VMEM] * 3,
+        scratch_shapes=[
+            pltpu.SMEM(fir_taps.shape, F32),
+            pltpu.SMEM(space_taps.shape, F32),
+            pltpu.SemaphoreType.DMA((2,)),
+        ],
+        compiler_params=SMALL,
+        name="channels",
+    )(near, inner, outer, in_hbm(fir_taps), in_hbm(space_taps))
+
+
 def local(strain, fir_taps, space_taps, sources):
     channels, samples = strain.shape
     devices = lax.axis_size(AXES)
@@ -317,34 +347,20 @@
         return lax.ppermute(x, AXES, [(i, i ^ distance) for i in range(devices)])
 
     total = keep + partner(send, 1)
-    total, inner, outer = lax.optimization_barrier((total, inner, outer))
-    inner = partner(inner, 1)
-    across = [(i, i + 1) for i in range(1, devices - 1, 2)]
-    outer = lax.ppermute(outer, AXES, across + [(j, i) for i, j in across])
-    length = samples + LANES
-    shifted, both, low = pl.pallas_call(
-        channels_kernel,
-        out_shape=[
-            jax.ShapeDtypeStruct((LAGS // STEP * channels, length), BF16),
-            jax.ShapeDtypeStruct((2 * LANES, 2 * LANES), BF16),
-            jax.ShapeDtypeStruct((LANES, 2 * LANES), BF16),
-        ],
-        in_specs=[VMEM] * 3 + [HBM] * 2,
-        out_specs=[VMEM] * 3,
-        scratch_shapes=[
-            pltpu.SMEM(fir_taps.shape, F32),
-            pltpu.SMEM(space_taps.shape, F32),
-            pltpu.SemaphoreType.DMA((2,)),
-        ],
-        compiler_params=SMALL,
-        name="channels",
-    )(near, inner, outer, in_hbm(fir_taps), in_hbm(space_taps))
-    distance = 2
-    while distance < devices:
-        if distance == 16:
+    across = [(i, i + 1) for i in range(1, devices - 1, 2)] + [(0, devices - 1)]
+    across = across + [(j, i) for i, j in across]
+    steps = [1 << k for k in range(1, devices.bit_length() - 1)]
+    order = steps[-1:] + steps[1:-1][:1] + steps[:1] + steps[2:-1]
+    for place, distance in enumerate(order):
+        if place == 0:
+            total, inner, outer = lax.optimization_barrier((total, inner, outer))
+            inner = partner(inner, 1)
+            outer = lax.ppermute(outer, AXES, across)
+        if place == 2:
+            shifted, both, low = channels_call(near, inner, outer, fir_taps, space_taps)
+        if place == 3:
             total, shifted, both, low = lax.optimization_barrier((total, shifted, both, low))
-        total = total + partner(total, distance)
-        distance *= 2
+        total = total + partner(total, distance + 1)
     other = partner(total, 1)
     return pl.pallas_call(
         correlate_kernel,

time: 25.9 us -> 24.4 us (0.942)
  waiting for transfers between devices: 9.67 us -> 7.51 us
  starting transfers between devices: 10.8 us -> 11.4 us
    ppermute x1, starting transfers between devices: 0.66 us -> 2.97 us  [local(): outer = lax.ppermute(outer, AXES, across)]
    ppermute x7, waiting for transfers between devices: 9.67 us -> 7.51 us  [partner(): return lax.ppermute(x, AXES, [(i, i ^ distance) for i in range(devices)])]
    ppermute x7, starting transfers between devices: 10.1 us -> 8.41 us  [partner(): return lax.ppermute(x, AXES, [(i, i ^ distance) for i in range(devices)])]
  transfers between devices with their start and end apart: 8 -> 8, of which waited for: 6 -> 4; matrix products, arithmetic and copies ran while one was open for 0% -> 0% of each run, Pallas kernels for 7% -> 8%
where the time goes in v2:
time: 24.4 us; the launch traced here: 24.2 us
  starting transfers between devices  11.4 us (47%)
  waiting for transfers between devices  7.51 us (31%)
  Pallas kernels  5.18 us (21%)
    ppermute x7, starting transfers between devices, partner(): return lax.ppermute(x, AXES, [(i, i ^ distance) for i in range(devices)])  8.41 us
    ppermute x7, waiting for transfers between devices, partner(): return lax.ppermute(x, AXES, [(i, i ^ distance) for i in range(devices)])  7.51 us
    ppermute x1, starting transfers between devices, local(): outer = lax.ppermute(outer, AXES, across)  2.97 us
    pallas_call x1, Pallas kernels, local(): pl.pallas_call(correlate_kernel, out_shape=jax.ShapeDtypeStruct((PANELS,...  2.13 us
    pallas_call x1, Pallas kernels, channels_call(): pl.pallas_call(channels_kernel, out_shape=[jax.ShapeDtypeStruct((LAGS //...  1.86 us
    pallas_call x1, Pallas kernels, local(): pl.pallas_call(share_kernel, out_shape=[packed, packed, edge, edge, near]...  1.19 us
  transfers between devices with their start and end apart: 8, of which 4 were waited for; matrix products, arithmetic and copies ran while one was open for 0% of the time, Pallas kernels for 8%

profile of v2, /device:TPU:0, one launch (start us, length us, event | category | flops | bytes accessed | tf_op | source)
XLA Modules:
  0.0 24.2 jit_solution(5144354197970629516)
XLA Ops:
  0.0 1.2 %share.1 = (f32[8,1536]{1,0:T(8,128)S(1)}, f32[8,1536]{1,0:T(8,128)S(1)}, f32[16,2048]{1,0:T(8,128)S(1)}, f32[16,2048]{1,0:T(8,128)S(1)}, f32[24,2048]{1,0:T(8,128)S(1)}) custom-call(f32[24,2048]{1,0:T(8,128)} %strain_hbm.1, f32[31]{0:T(128)} %space_hbm.3, s32[3,4]{1,0:T(4,128)} %sources_hbm.1), custom_call_target="tpu_custom_call" | custom-call | tf_op jit(solution)/shard_map/share/pallas_call | solution.py:332
  1.2 0.5 %collective-permute-start = (f32[8,1536]{1,0:T(8,128)S(1)}, f32[8,1536]{1,0:T(8,128)S(1)}, u32[]{:S(2)}, u32[]{:S(2)}) collective-permute-start(f32[8,1536]{1,0:T(8,128)S(1)} %get-tuple-element.21), channel_id=1, source_target_pairs={{0,1},{1,0},{2,3},{3,2},{4,5},{5,4},{6,7},{7,6},{8,9},{9,8},{10,11... | collective-permute-start | bytes 147464 | tf_op jit(solution)/shard_map/ppermute | solution.py:347
  1.7 0.9 %collective-permute-done = f32[8,1536]{1,0:T(8,128)S(1)} collective-permute-done((f32[8,1536]{1,0:T(8,128)S(1)}, f32[8,1536]{1,0:T(8,128)S(1)}, u32[]{:S(2)}, u32[]{:S(2)}) %collective-permute-start) | collective-permute-done | bytes 49184 | tf_op jit(solution)/shard_map/ppermute | solution.py:347
  2.6 3.7 %collective-permute-start.1 = (f32[8,1536]{1,0:T(8,128)S(1)}, f32[8,1536]{1,0:T(8,128)S(1)}, u32[]{:S(2)}, u32[]{:S(2)}) collective-permute-start(f32[8,1536]{1,0:T(8,128)S(1)} %add.15), channel_id=1, source_target_pairs={{0,17},{1,16},{2,19},{3,18},{4,21},{5,20},{6,23},{7,22},{8,25},{9,... | collective-permute-start | bytes 147464 | tf_op jit(solution)/shard_map/ppermute | solution.py:347
  6.3 0.4 %collective-permute-start.4 = (f32[16,2048]{1,0:T(8,128)S(1)}, f32[16,2048]{1,0:T(8,128)S(1)}, u32[]{:S(2)}, u32[]{:S(2)}) collective-permute-start(f32[16,2048]{1,0:T(8,128)S(1)} %get-tuple-element.26), channel_id=1, source_target_pairs={{0,1},{1,0},{2,3},{3,2},{4,5},{5,4},{6,7},{7,6},{8,9},{9,8},{10,11... | collective-permute-start | bytes 393224 | tf_op jit(solution)/shard_map/ppermute | solution.py:347
  6.7 3.0 %collective-permute-start.5 = (f32[16,2048]{1,0:T(8,128)S(1)}, f32[16,2048]{1,0:T(8,128)S(1)}, u32[]{:S(2)}, u32[]{:S(2)}) collective-permute-start(f32[16,2048]{1,0:T(8,128)S(1)} %get-tuple-element.27), channel_id=1, source_target_pairs={{1,2},{3,4},{5,6},{7,8},{9,10},{11,12},{13,14},{15,16},{17,18},{19... | collective-permute-start | bytes 393224 | tf_op jit(solution)/shard_map/ppermute | solution.py:358
  9.7 0.0 collective-permute-done.1
  9.7 0.2 %collective-permute-start.2 = (f32[8,1536]{1,0:T(8,128)S(1)}, f32[8,1536]{1,0:T(8,128)S(1)}, u32[]{:S(2)}, u32[]{:S(2)}) collective-permute-start(f32[8,1536]{1,0:T(8,128)S(1)} %add.16), channel_id=1, source_target_pairs={{0,5},{1,4},{2,7},{3,6},{4,1},{5,0},{6,3},{7,2},{8,13},{9,12},{10,... | collective-permute-start | bytes 147464 | tf_op jit(solution)/shard_map/ppermute | solution.py:347
  10.0 3.5 %collective-permute-done.2 = f32[8,1536]{1,0:T(8,128)S(1)} collective-permute-done((f32[8,1536]{1,0:T(8,128)S(1)}, f32[8,1536]{1,0:T(8,128)S(1)}, u32[]{:S(2)}, u32[]{:S(2)}) %collective-permute-start.2) | collective-permute-done | bytes 49184 | tf_op jit(solution)/shard_map/ppermute | solution.py:347
  13.5 1.7 %collective-permute-start.3 = (f32[8,1536]{1,0:T(8,128)S(1)}, f32[8,1536]{1,0:T(8,128)S(1)}, u32[]{:S(2)}, u32[]{:S(2)}) collective-permute-start(f32[8,1536]{1,0:T(8,128)S(1)} %add.17), channel_id=1, source_target_pairs={{0,3},{1,2},{2,1},{3,0},{4,7},{5,6},{6,5},{7,4},{8,11},{9,10},{10,... | collective-permute-start | bytes 147464 | tf_op jit(solution)/shard_map/ppermute | solution.py:347
  15.2 0.0 collective-permute-done.4.inner_ref
  15.2 0.0 collective-permute-done.5.outer_ref
  15.2 1.9 %channels.1 = (bf16[384,2176]{1,0:T(8,128)(2,1)S(1)}, bf16[256,256]{1,0:T(8,128)(2,1)S(1)}, bf16[128,256]{1,0:T(8,128)(2,1)S(1)}) custom-call(f32[24,2048]{1,0:T(8,128)S(1)} %get-tuple-element.25.strain_ref, f32[16,2048]{1,0:T(8,128)S(1)} %collective-permute-done.4.inner_ref, f32[16,2048]{1,0:T(8,128)S(1)} %collective-permute-done.5.outer_ref, f32[64]{0:T(128)} %fir_hbm.1, ...), custom_call_target="tpu_custom_call" | custom-call | tf_op jit(solution)/shard_map/channels/pallas_call | solution.py:307
  17.1 0.0 collective-permute-done.3
  17.1 1.4 %collective-permute-start.6 = (f32[8,1536]{1,0:T(8,128)S(1)}, f32[8,1536]{1,0:T(8,128)S(1)}, u32[]{:S(2)}, u32[]{:S(2)}) collective-permute-start(f32[8,1536]{1,0:T(8,128)S(1)} %add.18), channel_id=1, source_target_pairs={{0,9},{1,8},{2,11},{3,10},{4,13},{5,12},{6,15},{7,14},{8,1},{9,0},... | collective-permute-start | bytes 147464 | tf_op jit(solution)/shard_map/ppermute | solution.py:347
  18.5 2.2 %collective-permute-done.6 = f32[8,1536]{1,0:T(8,128)S(1)} collective-permute-done((f32[8,1536]{1,0:T(8,128)S(1)}, f32[8,1536]{1,0:T(8,128)S(1)}, u32[]{:S(2)}, u32[]{:S(2)}) %collective-permute-start.6) | collective-permute-done | bytes 49184 | tf_op jit(solution)/shard_map/ppermute | solution.py:347
  20.7 0.4 %collective-permute-start.7 = (f32[8,1536]{1,0:T(8,128)S(1)}, f32[8,1536]{1,0:T(8,128)S(1)}, u32[]{:S(2)}, u32[]{:S(2)}) collective-permute-start(f32[8,1536]{1,0:T(8,128)S(1)} %add.19.mine_ref), channel_id=1, source_target_pairs={{0,1},{1,0},{2,3},{3,2},{4,5},{5,4},{6,7},{7,6},{8,9},{9,8},{10,11... | collective-permute-start | bytes 147464 | tf_op jit(solution)/shard_map/ppermute | solution.py:347
  21.1 0.9 %collective-permute-done.7.other_ref = f32[8,1536]{1,0:T(8,128)S(1)} collective-permute-done((f32[8,1536]{1,0:T(8,128)S(1)}, f32[8,1536]{1,0:T(8,128)S(1)}, u32[]{:S(2)}, u32[]{:S(2)}) %collective-permute-start.7) | collective-permute-done | bytes 49184 | tf_op jit(solution)/shard_map/ppermute | solution.py:347
  22.0 2.1 %correlate.1 = f32[3,4,24,256]{3,2,1,0:T(8,128)} custom-call(f32[8,1536]{1,0:T(8,128)S(1)} %add.19.mine_ref, f32[8,1536]{1,0:T(8,128)S(1)} %collective-permute-done.7.other_ref, bf16[384,2176]{1,0:T(8,128)(2,1)S(1)} %get-tuple-element.32.shifted_ref, bf16[256,256]{1,0:T(8,128)(2,1)S(1)} %get-tuple-element.33.both_ref, ...), custom_call_target="tpu_custom_call" | custom-call | tf_op jit(solution)/shard_map/correlate/pallas_call | solution.py:365
  (5 shorter events, 0.0 us)
Async XLA Ops:
  1.2 1.4 %collective-permute-start = (f32[8,1536]{1,0:T(8,128)S(1)}, f32[8,1536]{1,0:T(8,128)S(1)}, u32[]{:S(2)}, u32[]{:S(2)}) collective-permute-start(f32[8,1536]{1,0:T(8,128)S(1)} %get-tuple-element.21), channel_id=1, source_target_pairs={{0,1},{1,0},{2,3},{3,2},{4,5},{5,4},{6,7},{7,6},{8,9},{9,8},{10,11... | collective-permute-start | bytes 147464 | tf_op jit(solution)/shard_map/ppermute | solution.py:347
  2.6 7.1 %collective-permute-start.1 = (f32[8,1536]{1,0:T(8,128)S(1)}, f32[8,1536]{1,0:T(8,128)S(1)}, u32[]{:S(2)}, u32[]{:S(2)}) collective-permute-start(f32[8,1536]{1,0:T(8,128)S(1)} %add.15), channel_id=1, source_target_pairs={{0,17},{1,16},{2,19},{3,18},{4,21},{5,20},{6,23},{7,22},{8,25},{9,... | collective-permute-start | bytes 147464 | tf_op jit(solution)/shard_map/ppermute | solution.py:347
  6.3 8.9 %collective-permute-start.4 = (f32[16,2048]{1,0:T(8,128)S(1)}, f32[16,2048]{1,0:T(8,128)S(1)}, u32[]{:S(2)}, u32[]{:S(2)}) collective-permute-start(f32[16,2048]{1,0:T(8,128)S(1)} %get-tuple-element.26), channel_id=1, source_target_pairs={{0,1},{1,0},{2,3},{3,2},{4,5},{5,4},{6,7},{7,6},{8,9},{9,8},{10,11... | collective-permute-start | bytes 393224 | tf_op jit(solution)/shard_map/ppermute | solution.py:347
  6.7 8.5 %collective-permute-start.5 = (f32[16,2048]{1,0:T(8,128)S(1)}, f32[16,2048]{1,0:T(8,128)S(1)}, u32[]{:S(2)}, u32[]{:S(2)}) collective-permute-start(f32[16,2048]{1,0:T(8,128)S(1)} %get-tuple-element.27), channel_id=1, source_target_pairs={{1,2},{3,4},{5,6},{7,8},{9,10},{11,12},{13,14},{15,16},{17,18},{19... | collective-permute-start | bytes 393224 | tf_op jit(solution)/shard_map/ppermute | solution.py:358
  9.7 3.7 %collective-permute-start.2 = (f32[8,1536]{1,0:T(8,128)S(1)}, f32[8,1536]{1,0:T(8,128)S(1)}, u32[]{:S(2)}, u32[]{:S(2)}) collective-permute-start(f32[8,1536]{1,0:T(8,128)S(1)} %add.16), channel_id=1, source_target_pairs={{0,5},{1,4},{2,7},{3,6},{4,1},{5,0},{6,3},{7,2},{8,13},{9,12},{10,... | collective-permute-start | bytes 147464 | tf_op jit(solution)/shard_map/ppermute | solution.py:347
  13.5 3.6 %collective-permute-start.3 = (f32[8,1536]{1,0:T(8,128)S(1)}, f32[8,1536]{1,0:T(8,128)S(1)}, u32[]{:S(2)}, u32[]{:S(2)}) collective-permute-start(f32[8,1536]{1,0:T(8,128)S(1)} %add.17), channel_id=1, source_target_pairs={{0,3},{1,2},{2,1},{3,0},{4,7},{5,6},{6,5},{7,4},{8,11},{9,10},{10,... | collective-permute-start | bytes 147464 | tf_op jit(solution)/shard_map/ppermute | solution.py:347
  17.1 3.6 %collective-permute-start.6 = (f32[8,1536]{1,0:T(8,128)S(1)}, f32[8,1536]{1,0:T(8,128)S(1)}, u32[]{:S(2)}, u32[]{:S(2)}) collective-permute-start(f32[8,1536]{1,0:T(8,128)S(1)} %add.18), channel_id=1, source_target_pairs={{0,9},{1,8},{2,11},{3,10},{4,13},{5,12},{6,15},{7,14},{8,1},{9,0},... | collective-permute-start | bytes 147464 | tf_op jit(solution)/shard_map/ppermute | solution.py:347
  20.7 1.3 %collective-permute-start.7 = (f32[8,1536]{1,0:T(8,128)S(1)}, f32[8,1536]{1,0:T(8,128)S(1)}, u32[]{:S(2)}, u32[]{:S(2)}) collective-permute-start(f32[8,1536]{1,0:T(8,128)S(1)} %add.19.mine_ref), channel_id=1, source_target_pairs={{0,1},{1,0},{2,3},{3,2},{4,5},{5,4},{6,7},{7,6},{8,9},{9,8},{10,11... | collective-permute-start | bytes 147464 | tf_op jit(solution)/shard_map/ppermute | solution.py:347

commit v3 on v2

--- a/solution.py
+++ b/solution.py
@@ -13,7 +13,7 @@
 SRC = 4
 AXES = ("fibre", "seg")
 LANES = 128
-STEP = 16
+STEP = 32
 HALO = 16
 ROWS = PANELS * SRC
 HALF_ROWS = ROWS // 2
@@ -74,17 +74,20 @@
     return jnp.concatenate([x[rows:], jnp.zeros((rows, x.shape[1]), x.dtype)], axis=0)
 
 
-def filter_and_norm(x, fir_both, fir_low):
+def window_bands():
+    u = lax.broadcasted_iota(jnp.int32, (2 * LANES, LANES), 0) % LANES
+    t = lax.broadcasted_iota(jnp.int32, (2 * LANES, LANES), 1)
+    bands = [jnp.abs(u - t) <= RUN, u - t >= LANES - RUN, t - u >= LANES - RUN]
+    return jnp.concatenate([jnp.where(b, 1.0, 0.0).astype(BF16) for b in bands], axis=1)
+
+
+def filter_and_norm(x, fir_both, fir_low, window):
     rows, samples = x.shape
     high, low = split(to_blocks(x))
     dot = functools.partial(jnp.dot, preferred_element_type=F32)
     full = dot(jnp.concatenate([high, low], axis=1), fir_both) + dot(high, fir_low)
     smooth = full[:, :LANES] + earlier(full[:, LANES:], rows)
     high, low = split(jnp.abs(smooth))
-    u = lax.broadcasted_iota(jnp.int32, (2 * LANES, LANES), 0) % LANES
-    t = lax.broadcasted_iota(jnp.int32, (2 * LANES, LANES), 1)
-    bands = [jnp.abs(u - t) <= RUN, u - t >= LANES - RUN, t - u >= LANES - RUN]
-    window = jnp.concatenate([jnp.where(b, 1.0, 0.0).astype(BF16) for b in bands], axis=1)
     sums = dot(jnp.concatenate([high, low], axis=1), window)
     total = (
         sums[:, :LANES]
@@ -170,40 +173,42 @@
     send_ref[...] = pack(share[8 : 8 + HALF_ROWS])
 
 
+def tables_kernel(
+    fir_hbm, space_hbm, space_matrix_ref, both_ref, low_ref, window_ref, fir_ref, space_ref, sems
+):
+    copies = fetch([(space_hbm, space_ref), (fir_hbm, fir_ref)], sems)
+    window_ref[...] = window_bands()
+    channels = space_matrix_ref.shape[0]
+    half_span = (space_ref.shape[0] - 1) // 2
+    row = lax.broadcasted_iota(jnp.int32, (channels, channels + 2 * HALO), 0)
+    column = lax.broadcasted_iota(jnp.int32, (channels, channels + 2 * HALO), 1)
+    copies[0].wait()
+    space_matrix_ref[...] = split_columns(taps_at(space_ref, column - HALO - row + half_span))
+    copies[1].wait()
+    high, low = split(fir_matrix(fir_ref))
+    both_ref[...] = jnp.concatenate([high, high], axis=0)
+    low_ref[...] = low
+
+
 def channels_kernel(
     strain_ref,
     inner_ref,
     outer_ref,
-    fir_hbm,
-    space_hbm,
-    shifted_ref,
+    space_matrix_ref,
     both_ref,
     low_ref,
-    fir_ref,
-    space_ref,
-    sems,
+    window_ref,
+    shifted_ref,
 ):
-    copies = fetch([(space_hbm, space_ref), (fir_hbm, fir_ref)], sems)
     channels, samples = strain_ref.shape
-    half_span = (space_ref.shape[0] - 1) // 2
     me = lax.axis_index(AXES)
     even = me % 2 == 0
     inner, outer = inner_ref[...], outer_ref[...]
     outer = jnp.where((me == 0) | (me == lax.axis_size(AXES) - 1), 0.0, outer)
     before, after = jnp.where(even, outer, inner), jnp.where(even, inner, outer)
     x = jnp.concatenate([before, strain_ref[...], after], axis=0)
-    wide = x.shape[0]
-    row = lax.broadcasted_iota(jnp.int32, (channels, wide), 0)
-    column = lax.broadcasted_iota(jnp.int32, (channels, wide), 1)
-    copies[0].wait()
-    matrix = taps_at(space_ref, column - HALO - row + half_span)
-    spaced = jnp.dot(split_columns(matrix), split_rows(x), preferred_element_type=F32)
-    copies[1].wait()
-    high, low = split(fir_matrix(fir_ref))
-    both = jnp.concatenate([high, high], axis=0)
-    both_ref[...] = both
-    low_ref[...] = low
-    normed = filter_and_norm(spaced, both, low)
+    spaced = jnp.dot(space_matrix_ref[...], split_rows(x), preferred_element_type=F32)
+    normed = filter_and_norm(spaced, both_ref[...], low_ref[...], window_ref[...])
     length = shifted_ref.shape[1]
     padded = jnp.concatenate(
         [
@@ -233,28 +238,17 @@
     )
 
 
-def correlate_kernel(mine_ref, other_ref, shifted_ref, both_ref, low_ref, out_ref):
-    channels = out_ref.shape[2]
-    mine = unpack(mine_ref[...])
-    other = unpack(other_ref[...])
-    samples = mine.shape[1]
-    even = parity(lax.axis_index(AXES)) == 0
-    spaced = jnp.concatenate(
-        [
-            jnp.where(even, mine, other),
-            jnp.where(even, other, mine),
-            jnp.zeros((16 - ROWS, samples), F32),
-        ],
-        axis=0,
-    )
-    normed = filter_and_norm(spaced, both_ref[...], low_ref[...])
-    normed = normed.astype(BF16).astype(F32)
-    padded = jnp.concatenate([normed, jnp.zeros((16, LANES), F32)], axis=1)
+def lag_sums(shifted_ref, normed):
+    rows = HALF_ROWS
+    samples = normed.shape[1]
+    coarse = LAGS // STEP
+    channels = shifted_ref.shape[0] // coarse
+    padded = jnp.concatenate([normed, jnp.zeros((normed.shape[0], LANES), F32)], axis=1)
     lane = lax.broadcasted_iota(jnp.int32, (STEP, LANES), 1)
     row = lax.broadcasted_iota(jnp.int32, (STEP, LANES), 0)
     straight = lane >= row
     records = []
-    for k in range(ROWS):
+    for k in range(rows):
         one = jnp.broadcast_to(padded[k : k + 1], (STEP, padded.shape[1]))
         tiles = [
             pltpu.roll(one[:, j : j + LANES], 0, 1, stride=1, stride_axis=0)
@@ -271,13 +265,15 @@
         shifted_ref[...], records, (((1,), (1,)), ((), ())), preferred_element_type=F32
     )
     result = result * float(samples) ** -0.5
-    result = jnp.concatenate(
-        [result, jnp.zeros((result.shape[0], 2 * LANES - result.shape[1]), F32)], axis=1
-    )
     per_tile = LANES // STEP
+    tiles = -(-rows // per_tile)
+    short = tiles * LANES - result.shape[1]
+    if short:
+        result = jnp.concatenate([result, jnp.zeros((result.shape[0], short), F32)], axis=1)
     lane = lax.broadcasted_iota(jnp.int32, (channels, LANES), 1)
+    sums = [[None] * (LAGS // LANES) for _ in range(rows)]
     for h in range(LAGS // LANES):
-        for tile in range(2):
+        for tile in range(tiles):
             parts = [
                 result[
                     (h * per_tile + q) * channels : (h * per_tile + q + 1) * channels,
@@ -285,42 +281,57 @@
                 ]
                 for q in range(per_tile)
             ]
-            for distance in (4, 2, 1):
+            for distance in [d for d in (8, 4, 2, 1) if d < per_tile]:
                 for q in range(per_tile):
                     if q & distance == 0:
                         parts[q], parts[q + distance] = swap(
                             parts[q], parts[q + distance], distance * STEP, lane
                         )
             for q in range(per_tile):
-                number = tile * per_tile + q
-                if number < ROWS:
-                    out_ref[number // SRC, number % SRC, :, h * LANES : (h + 1) * LANES] = parts[q]
+                if tile * per_tile + q < rows:
+                    sums[tile * per_tile + q][h] = parts[q]
+    return sums
+
+
+def norm_kernel(total_ref, both_ref, low_ref, window_ref, normed_ref):
+    spaced = unpack(total_ref[...])
+    samples = spaced.shape[1]
+    spaced = jnp.concatenate([spaced, jnp.zeros((8 - HALF_ROWS, samples), F32)], axis=0)
+    normed = filter_and_norm(spaced, both_ref[...], low_ref[...], window_ref[...])
+    normed = jnp.concatenate([normed[:, : samples // 2], normed[:, samples // 2 :]], axis=0)
+    normed_ref[...] = normed.astype(BF16)
+
+
+def rows_of(normed_ref):
+    x = normed_ref[...].astype(F32)
+    return jnp.concatenate([x[:8], x[8:]], axis=1)
+
+
+def first_kernel(normed_ref, shifted_ref, sums_ref):
+    for k, halves in enumerate(lag_sums(shifted_ref, rows_of(normed_ref))):
+        for h, part in enumerate(halves):
+            sums_ref[k, :, h * LANES : (h + 1) * LANES] = part
+
+
+def second_kernel(normed_ref, shifted_ref, sums_ref, out_hbm, more_ref, sems):
+    mine = parity(lax.axis_index(AXES))
+    early = pltpu.make_async_copy(
+        sums_ref, out_hbm.at[pl.ds(mine * HALF_ROWS, HALF_ROWS)], sems.at[0]
+    )
+    early.start()
+    for k, halves in enumerate(lag_sums(shifted_ref, rows_of(normed_ref))):
+        for h, part in enumerate(halves):
+            more_ref[k, :, h * LANES : (h + 1) * LANES] = part
+    late = pltpu.make_async_copy(
+        more_ref, out_hbm.at[pl.ds((1 - mine) * HALF_ROWS, HALF_ROWS)], sems.at[1]
+    )
+    late.start()
+    early.wait()
+    late.wait()
 
 
 def in_hbm(x):
     return pltpu.with_memory_space_constraint(x, pltpu.HBM)
-
-
-def channels_call(near, inner, outer, fir_taps, space_taps):
-    channels, samples = near.shape
-    length = samples + LANES
-    return pl.pallas_call(
-        channels_kernel,
-        out_shape=[
-            jax.ShapeDtypeStruct((LAGS // STEP * channels, length), BF16),
-            jax.ShapeDtypeStruct((2 * LANES, 2 * LANES), BF16),
-            jax.ShapeDtypeStruct((LANES, 2 * LANES), BF16),
-        ],
-        in_specs=[VMEM] * 3 + [HBM] * 2,
-        out_specs=[VMEM] * 3,
-        scratch_shapes=[
-            pltpu.SMEM(fir_taps.shape, F32),
-            pltpu.SMEM(space_taps.shape, F32),
-            pltpu.SemaphoreType.DMA((2,)),
-        ],
-        compiler_params=SMALL,
-        name="channels",
-    )(near, inner, outer, in_hbm(fir_taps), in_hbm(space_taps))
 
 
 def local(strain, fir_taps, space_taps, sources):
@@ -356,20 +367,69 @@
             total, inner, outer = lax.optimization_barrier((total, inner, outer))
             inner = partner(inner, 1)
             outer = lax.ppermute(outer, AXES, across)
+        if place == 1:
+            total, fir_taps, space_taps = lax.optimization_barrier((total, fir_taps, space_taps))
+            tables = pl.pallas_call(
+                tables_kernel,
+                out_shape=[
+                    jax.ShapeDtypeStruct((channels, 3 * (channels + 2 * HALO)), BF16),
+                    jax.ShapeDtypeStruct((2 * LANES, 2 * LANES), BF16),
+                    jax.ShapeDtypeStruct((LANES, 2 * LANES), BF16),
+                    jax.ShapeDtypeStruct((2 * LANES, 3 * LANES), BF16),
+                ],
+                in_specs=[HBM] * 2,
+                out_specs=[VMEM] * 4,
+                scratch_shapes=[
+                    pltpu.SMEM(fir_taps.shape, F32),
+                    pltpu.SMEM(space_taps.shape, F32),
+                    pltpu.SemaphoreType.DMA((2,)),
+                ],
+                compiler_params=SMALL,
+                name="tables",
+            )(in_hbm(fir_taps), in_hbm(space_taps))
         if place == 2:
-            shifted, both, low = channels_call(near, inner, outer, fir_taps, space_taps)
+            total, *tables = lax.optimization_barrier((total, *tables))
+            shifted = pl.pallas_call(
+                channels_kernel,
+                out_shape=jax.ShapeDtypeStruct(
+                    (LAGS // STEP * channels, samples + LANES), BF16
+                ),
+                in_specs=[VMEM] * 7,
+                out_specs=VMEM,
+                compiler_params=SMALL,
+                name="channels",
+            )(near, inner, outer, *tables)
         if place == 3:
-            total, shifted, both, low = lax.optimization_barrier((total, shifted, both, low))
+            total, shifted = lax.optimization_barrier((total, shifted))
         total = total + partner(total, distance + 1)
-    other = partner(total, 1)
-    return pl.pallas_call(
-        correlate_kernel,
-        out_shape=jax.ShapeDtypeStruct((PANELS, SRC, channels, LAGS), F32),
-        in_specs=[VMEM] * 5,
+    mine = pl.pallas_call(
+        norm_kernel,
+        out_shape=jax.ShapeDtypeStruct((16, samples // 2), BF16),
+        in_specs=[VMEM] * 4,
         out_specs=VMEM,
         compiler_params=SMALL,
-        name="correlate",
-    )(total, other, shifted, both, low)
+        name="norm",
+    )(total, *tables[1:])
+    other = partner(mine, 1)
+    sums = jax.ShapeDtypeStruct((HALF_ROWS, channels, LAGS), F32)
+    first = pl.pallas_call(
+        first_kernel,
+        out_shape=sums,
+        in_specs=[VMEM] * 2,
+        out_specs=VMEM,
+        compiler_params=SMALL,
+        name="first",
+    )(mine, shifted)
+    out = pl.pallas_call(
+        second_kernel,
+        out_shape=jax.ShapeDtypeStruct((ROWS, channels, LAGS), F32),
+        in_specs=[VMEM] * 3,
+        out_specs=HBM,
+        scratch_shapes=[pltpu.VMEM(sums.shape, F32), pltpu.SemaphoreType.DMA((2,))],
+        compiler_params=SMALL,
+        name="second",
+    )(other, shifted, first)
+    return out.reshape(PANELS, SRC, channels, LAGS)
 
 
 def solution(mesh):

time: 24.4 us -> 24 us (0.984)
  waiting for transfers between devices: 7.51 us -> 6.76 us
    ppermute x7, waiting for transfers between devices: 7.51 us -> 6.76 us  [partner(): return lax.ppermute(x, AXES, [(i, i ^ distance) for i in range(devices)])]
    pallas_call x2 -> x5, Pallas kernels: 3.99 us -> 4.19 us  [the longest x1 1.38 us: local(): pl.pallas_call(second_kernel, out_shape=jax.ShapeDtypeStruct((ROWS, chann...]
  transfers between devices with their start and end apart: 8 -> 8, of which waited for: 4 -> 5; matrix products, arithmetic and copies ran while one was open for 0% -> 0% of each run, Pallas kernels for 8% -> 10%
where the time goes in v3:
time: 24 us; the launch traced here: 23.7 us
  starting transfers between devices  11.4 us (48%)
  waiting for transfers between devices  6.76 us (28%)
  Pallas kernels  5.38 us (22%)
    ppermute x7, starting transfers between devices, partner(): return lax.ppermute(x, AXES, [(i, i ^ distance) for i in range(devices)])  8.45 us
    ppermute x7, waiting for transfers between devices, partner(): return lax.ppermute(x, AXES, [(i, i ^ distance) for i in range(devices)])  6.76 us
    ppermute x1, starting transfers between devices, local(): outer = lax.ppermute(outer, AXES, across)  2.97 us
    pallas_call x1, Pallas kernels, local(): pl.pallas_call(second_kernel, out_shape=jax.ShapeDtypeStruct((ROWS, chann...  1.38 us
    pallas_call x1, Pallas kernels, local(): pl.pallas_call(share_kernel, out_shape=[packed, packed, edge, edge, near]...  1.19 us
    pallas_call x1, Pallas kernels, local(): pl.pallas_call(tables_kernel, out_shape=[jax.ShapeDtypeStruct((channels,...  0.94 us
    pallas_call x1, Pallas kernels, local(): pl.pallas_call(channels_kernel, out_shape=jax.ShapeDtypeStruct((LAGS // S...  0.81 us
    pallas_call x1, Pallas kernels, local(): pl.pallas_call(first_kernel, out_shape=sums, in_specs=[VMEM] * 2, out_spe...  0.7 us
  transfers between devices with their start and end apart: 8, of which 5 were waited for; matrix products, arithmetic and copies ran while one was open for 0% of the time, Pallas kernels for 10%

profile of v3, /device:TPU:0, one launch (start us, length us, event | category | flops | bytes accessed | tf_op | source)
XLA Modules:
  0.0 23.7 jit_solution(14571848854563694075)
XLA Ops:
  0.0 1.2 %share.1 = (f32[8,1536]{1,0:T(8,128)S(1)}, f32[8,1536]{1,0:T(8,128)S(1)}, f32[16,2048]{1,0:T(8,128)S(1)}, f32[16,2048]{1,0:T(8,128)S(1)}, f32[24,2048]{1,0:T(8,128)S(1)}) custom-call(f32[24,2048]{1,0:T(8,128)} %strain_hbm.1, f32[31]{0:T(128)} %space_hbm.2, s32[3,4]{1,0:T(4,128)} %sources_hbm.1), custom_call_target="tpu_custom_call" | custom-call | tf_op jit(solution)/shard_map/share/pallas_call | solution.py:343
  1.2 0.5 %collective-permute-start = (f32[8,1536]{1,0:T(8,128)S(1)}, f32[8,1536]{1,0:T(8,128)S(1)}, u32[]{:S(2)}, u32[]{:S(2)}) collective-permute-start(f32[8,1536]{1,0:T(8,128)S(1)} %get-tuple-element.28), channel_id=1, source_target_pairs={{0,1},{1,0},{2,3},{3,2},{4,5},{5,4},{6,7},{7,6},{8,9},{9,8},{10,11... | collective-permute-start | bytes 147464 | tf_op jit(solution)/shard_map/ppermute | solution.py:358
  1.7 0.9 %collective-permute-done = f32[8,1536]{1,0:T(8,128)S(1)} collective-permute-done((f32[8,1536]{1,0:T(8,128)S(1)}, f32[8,1536]{1,0:T(8,128)S(1)}, u32[]{:S(2)}, u32[]{:S(2)}) %collective-permute-start) | collective-permute-done | bytes 49184 | tf_op jit(solution)/shard_map/ppermute | solution.py:358
  2.6 3.7 %collective-permute-start.1 = (f32[8,1536]{1,0:T(8,128)S(1)}, f32[8,1536]{1,0:T(8,128)S(1)}, u32[]{:S(2)}, u32[]{:S(2)}) collective-permute-start(f32[8,1536]{1,0:T(8,128)S(1)} %add.15), channel_id=1, source_target_pairs={{0,17},{1,16},{2,19},{3,18},{4,21},{5,20},{6,23},{7,22},{8,25},{9,... | collective-permute-start | bytes 147464 | tf_op jit(solution)/shard_map/ppermute | solution.py:358
  6.3 0.4 %collective-permute-start.4 = (f32[16,2048]{1,0:T(8,128)S(1)}, f32[16,2048]{1,0:T(8,128)S(1)}, u32[]{:S(2)}, u32[]{:S(2)}) collective-permute-start(f32[16,2048]{1,0:T(8,128)S(1)} %get-tuple-element.41), channel_id=1, source_target_pairs={{0,1},{1,0},{2,3},{3,2},{4,5},{5,4},{6,7},{7,6},{8,9},{9,8},{10,11... | collective-permute-start | bytes 393224 | tf_op jit(solution)/shard_map/ppermute | solution.py:358
  6.7 3.0 %collective-permute-start.5 = (f32[16,2048]{1,0:T(8,128)S(1)}, f32[16,2048]{1,0:T(8,128)S(1)}, u32[]{:S(2)}, u32[]{:S(2)}) collective-permute-start(f32[16,2048]{1,0:T(8,128)S(1)} %get-tuple-element.42), channel_id=1, source_target_pairs={{1,2},{3,4},{5,6},{7,8},{9,10},{11,12},{13,14},{15,16},{17,18},{19... | collective-permute-start | bytes 393224 | tf_op jit(solution)/shard_map/ppermute | solution.py:369
  9.7 0.0 collective-permute-done.1
  9.7 0.2 %collective-permute-start.2 = (f32[8,1536]{1,0:T(8,128)S(1)}, f32[8,1536]{1,0:T(8,128)S(1)}, u32[]{:S(2)}, u32[]{:S(2)}) collective-permute-start(f32[8,1536]{1,0:T(8,128)S(1)} %add.16), channel_id=1, source_target_pairs={{0,5},{1,4},{2,7},{3,6},{4,1},{5,0},{6,3},{7,2},{8,13},{9,12},{10,... | collective-permute-start | bytes 147464 | tf_op jit(solution)/shard_map/ppermute | solution.py:358
  10.0 0.9 %tables.1 = (bf16[24,168]{1,0:T(8,128)(2,1)S(1)}, bf16[256,256]{1,0:T(8,128)(2,1)S(1)}, bf16[128,256]{1,0:T(8,128)(2,1)S(1)}, bf16[256,384]{1,0:T(8,128)(2,1)S(1)}) custom-call(f32[64]{0:T(128)} %fir_hbm, f32[31]{0:T(128)} %space_hbm.2), custom_call_target="tpu_custom_call" | custom-call | tf_op jit(solution)/shard_map/tables/pallas_call | solution.py:372
  10.9 2.5 %collective-permute-done.2 = f32[8,1536]{1,0:T(8,128)S(1)} collective-permute-done((f32[8,1536]{1,0:T(8,128)S(1)}, f32[8,1536]{1,0:T(8,128)S(1)}, u32[]{:S(2)}, u32[]{:S(2)}) %collective-permute-start.2) | collective-permute-done | bytes 49184 | tf_op jit(solution)/shard_map/ppermute | solution.py:358
  13.5 1.7 %collective-permute-start.3 = (f32[8,1536]{1,0:T(8,128)S(1)}, f32[8,1536]{1,0:T(8,128)S(1)}, u32[]{:S(2)}, u32[]{:S(2)}) collective-permute-start(f32[8,1536]{1,0:T(8,128)S(1)} %add.17), channel_id=1, source_target_pairs={{0,3},{1,2},{2,1},{3,0},{4,7},{5,6},{6,5},{7,4},{8,11},{9,10},{10,... | collective-permute-start | bytes 147464 | tf_op jit(solution)/shard_map/ppermute | solution.py:358
  15.2 0.0 collective-permute-done.4.inner_ref
  15.2 0.0 collective-permute-done.5.outer_ref
  15.2 0.8 %channels.1.shifted_ref = bf16[192,2176]{1,0:T(8,128)(2,1)S(1)} custom-call(f32[24,2048]{1,0:T(8,128)S(1)} %get-tuple-element.40.strain_ref, f32[16,2048]{1,0:T(8,128)S(1)} %collective-permute-done.4.inner_ref, f32[16,2048]{1,0:T(8,128)S(1)} %collective-permute-done.5.outer_ref, bf16[24,168]{1,0:T(8,128)(2,1)S(1)} %get-tuple-element.43.space_matrix_ref, ...), custom_call_target="tpu_custom_call" | custom-call | tf_op jit(solution)/shard_map/channels/pallas_call | solution.py:392
  16.0 1.0 %collective-permute-done.3 = f32[8,1536]{1,0:T(8,128)S(1)} collective-permute-done((f32[8,1536]{1,0:T(8,128)S(1)}, f32[8,1536]{1,0:T(8,128)S(1)}, u32[]{:S(2)}, u32[]{:S(2)}) %collective-permute-start.3) | collective-permute-done | bytes 49184 | tf_op jit(solution)/shard_map/ppermute | solution.py:358
  17.0 1.4 %collective-permute-start.6 = (f32[8,1536]{1,0:T(8,128)S(1)}, f32[8,1536]{1,0:T(8,128)S(1)}, u32[]{:S(2)}, u32[]{:S(2)}) collective-permute-start(f32[8,1536]{1,0:T(8,128)S(1)} %add.18), channel_id=1, source_target_pairs={{0,9},{1,8},{2,11},{3,10},{4,13},{5,12},{6,15},{7,14},{8,1},{9,0},... | collective-permute-start | bytes 147464 | tf_op jit(solution)/shard_map/ppermute | solution.py:358
  18.5 2.2 %collective-permute-done.6 = f32[8,1536]{1,0:T(8,128)S(1)} collective-permute-done((f32[8,1536]{1,0:T(8,128)S(1)}, f32[8,1536]{1,0:T(8,128)S(1)}, u32[]{:S(2)}, u32[]{:S(2)}) %collective-permute-start.6) | collective-permute-done | bytes 49184 | tf_op jit(solution)/shard_map/ppermute | solution.py:358
  20.6 0.4 %norm.1.normed_ref = bf16[16,1024]{1,0:T(8,128)(2,1)S(1)} custom-call(f32[8,1536]{1,0:T(8,128)S(1)} %add.19.total_ref, bf16[256,256]{1,0:T(8,128)(2,1)S(1)} %get-tuple-element.44.both_ref, bf16[128,256]{1,0:T(8,128)(2,1)S(1)} %get-tuple-element.45.low_ref, bf16[256,384]{1,0:T(8,128)(2,1)S(1)} %get-tuple-element.46.window_ref), custom_call_target="tpu_custom_call" | custom-call | tf_op jit(solution)/shard_map/norm/pallas_call | solution.py:405
  21.0 0.4 %collective-permute-start.7 = (bf16[16,1024]{1,0:T(8,128)(2,1)S(1)}, bf16[16,1024]{1,0:T(8,128)(2,1)S(1)}, u32[]{:S(2)}, u32[]{:S(2)}) collective-permute-start(bf16[16,1024]{1,0:T(8,128)(2,1)S(1)} %norm.1.normed_ref), channel_id=1, source_target_pairs={{0,1},{1,0},{2,3},{3,2},{4,5},{5,4},{6,7},{7,6},{8,9},{9,8},{10,11... | collective-permute-start | bytes 98312 | tf_op jit(solution)/shard_map/ppermute | solution.py:358
  21.4 0.7 %first.1.sums_ref = f32[6,24,256]{2,1,0:T(8,128)S(1)} custom-call(bf16[16,1024]{1,0:T(8,128)(2,1)S(1)} %norm.1.normed_ref, bf16[192,2176]{1,0:T(8,128)(2,1)S(1)} %channels.1.shifted_ref), custom_call_target="tpu_custom_call" | custom-call | tf_op jit(solution)/shard_map/first/pallas_call | solution.py:415
  22.1 0.2 collective-permute-done.7.normed_ref
  22.3 1.4 %second.1 = f32[12,24,256]{2,1,0:T(8,128)} custom-call(bf16[16,1024]{1,0:T(8,128)(2,1)S(1)} %collective-permute-done.7.normed_ref, bf16[192,2176]{1,0:T(8,128)(2,1)S(1)} %channels.1.shifted_ref, f32[6,24,256]{2,1,0:T(8,128)S(1)} %first.1.sums_ref), custom_call_target="tpu_custom_call" | custom-call | tf_op jit(solution)/shard_map/second/pallas_call | solution.py:423
  (5 shorter events, 0.0 us)
Async XLA Ops:
  1.2 1.4 %collective-permute-start = (f32[8,1536]{1,0:T(8,128)S(1)}, f32[8,1536]{1,0:T(8,128)S(1)}, u32[]{:S(2)}, u32[]{:S(2)}) collective-permute-start(f32[8,1536]{1,0:T(8,128)S(1)} %get-tuple-element.28), channel_id=1, source_target_pairs={{0,1},{1,0},{2,3},{3,2},{4,5},{5,4},{6,7},{7,6},{8,9},{9,8},{10,11... | collective-permute-start | bytes 147464 | tf_op jit(solution)/shard_map/ppermute | solution.py:358
  2.6 7.1 %collective-permute-start.1 = (f32[8,1536]{1,0:T(8,128)S(1)}, f32[8,1536]{1,0:T(8,128)S(1)}, u32[]{:S(2)}, u32[]{:S(2)}) collective-permute-start(f32[8,1536]{1,0:T(8,128)S(1)} %add.15), channel_id=1, source_target_pairs={{0,17},{1,16},{2,19},{3,18},{4,21},{5,20},{6,23},{7,22},{8,25},{9,... | collective-permute-start | bytes 147464 | tf_op jit(solution)/shard_map/ppermute | solution.py:358
  6.3 8.9 %collective-permute-start.4 = (f32[16,2048]{1,0:T(8,128)S(1)}, f32[16,2048]{1,0:T(8,128)S(1)}, u32[]{:S(2)}, u32[]{:S(2)}) collective-permute-start(f32[16,2048]{1,0:T(8,128)S(1)} %get-tuple-element.41), channel_id=1, source_target_pairs={{0,1},{1,0},{2,3},{3,2},{4,5},{5,4},{6,7},{7,6},{8,9},{9,8},{10,11... | collective-permute-start | bytes 393224 | tf_op jit(solution)/shard_map/ppermute | solution.py:358
  6.7 8.5 %collective-permute-start.5 = (f32[16,2048]{1,0:T(8,128)S(1)}, f32[16,2048]{1,0:T(8,128)S(1)}, u32[]{:S(2)}, u32[]{:S(2)}) collective-permute-start(f32[16,2048]{1,0:T(8,128)S(1)} %get-tuple-element.42), channel_id=1, source_target_pairs={{1,2},{3,4},{5,6},{7,8},{9,10},{11,12},{13,14},{15,16},{17,18},{19... | collective-permute-start | bytes 393224 | tf_op jit(solution)/shard_map/ppermute | solution.py:369
  9.7 3.7 %collective-permute-start.2 = (f32[8,1536]{1,0:T(8,128)S(1)}, f32[8,1536]{1,0:T(8,128)S(1)}, u32[]{:S(2)}, u32[]{:S(2)}) collective-permute-start(f32[8,1536]{1,0:T(8,128)S(1)} %add.16), channel_id=1, source_target_pairs={{0,5},{1,4},{2,7},{3,6},{4,1},{5,0},{6,3},{7,2},{8,13},{9,12},{10,... | collective-permute-start | bytes 147464 | tf_op jit(solution)/shard_map/ppermute | solution.py:358
  13.5 3.6 %collective-permute-start.3 = (f32[8,1536]{1,0:T(8,128)S(1)}, f32[8,1536]{1,0:T(8,128)S(1)}, u32[]{:S(2)}, u32[]{:S(2)}) collective-permute-start(f32[8,1536]{1,0:T(8,128)S(1)} %add.17), channel_id=1, source_target_pairs={{0,3},{1,2},{2,1},{3,0},{4,7},{5,6},{6,5},{7,4},{8,11},{9,10},{10,... | collective-permute-start | bytes 147464 | tf_op jit(solution)/shard_map/ppermute | solution.py:358
  17.0 3.6 %collective-permute-start.6 = (f32[8,1536]{1,0:T(8,128)S(1)}, f32[8,1536]{1,0:T(8,128)S(1)}, u32[]{:S(2)}, u32[]{:S(2)}) collective-permute-start(f32[8,1536]{1,0:T(8,128)S(1)} %add.18), channel_id=1, source_target_pairs={{0,9},{1,8},{2,11},{3,10},{4,13},{5,12},{6,15},{7,14},{8,1},{9,0},... | collective-permute-start | bytes 147464 | tf_op jit(solution)/shard_map/ppermute | solution.py:358
  21.0 1.3 %collective-permute-start.7 = (bf16[16,1024]{1,0:T(8,128)(2,1)S(1)}, bf16[16,1024]{1,0:T(8,128)(2,1)S(1)}, u32[]{:S(2)}, u32[]{:S(2)}) collective-permute-start(bf16[16,1024]{1,0:T(8,128)(2,1)S(1)} %norm.1.normed_ref), channel_id=1, source_target_pairs={{0,1},{1,0},{2,3},{3,2},{4,5},{5,4},{6,7},{7,6},{8,9},{9,8},{10,11... | collective-permute-start | bytes 98312 | tf_op jit(solution)/shard_map/ppermute | solution.py:358

commit v4 on v3

--- a/solution.py
+++ b/solution.py
@@ -361,11 +361,12 @@
     across = [(i, i + 1) for i in range(1, devices - 1, 2)] + [(0, devices - 1)]
     across = across + [(j, i) for i, j in across]
     steps = [1 << k for k in range(1, devices.bit_length() - 1)]
-    order = steps[-1:] + steps[1:-1][:1] + steps[:1] + steps[2:-1]
-    for place, distance in enumerate(order):
+    order = [(distance + 1,) for distance in steps[:1:-1]] + [(5, 3, 6)]
+    for place, masks in enumerate(order):
         if place == 0:
-            total, inner, outer = lax.optimization_barrier((total, inner, outer))
+            total, inner = lax.optimization_barrier((total, inner))
             inner = partner(inner, 1)
+            total, outer = lax.optimization_barrier((total, outer))
             outer = lax.ppermute(outer, AXES, across)
         if place == 1:
             total, fir_taps, space_taps = lax.optimization_barrier((total, fir_taps, space_taps))
@@ -387,7 +388,7 @@
                 compiler_params=SMALL,
                 name="tables",
             )(in_hbm(fir_taps), in_hbm(space_taps))
-        if place == 2:
+        if place == len(order) - 1:
             total, *tables = lax.optimization_barrier((total, *tables))
             shifted = pl.pallas_call(
                 channels_kernel,
@@ -399,9 +400,8 @@
                 compiler_params=SMALL,
                 name="channels",
             )(near, inner, outer, *tables)
-        if place == 3:
-            total, shifted = lax.optimization_barrier((total, shifted))
-        total = total + partner(total, distance + 1)
+        total = sum([partner(total, mask) for mask in masks], total)
+    total, shifted = lax.optimization_barrier((total, shifted))
     mine = pl.pallas_call(
         norm_kernel,
         out_shape=jax.ShapeDtypeStruct((16, samples // 2), BF16),

time: 24 us -> 23.2 us (0.967)
  waiting for transfers between devices: 6.76 us -> 5.82 us
  starting transfers between devices: 11.4 us -> 11.8 us
    ppermute x7 -> x8, waiting for transfers between devices: 6.76 us -> 5.82 us  [partner(): return lax.ppermute(x, AXES, [(i, i ^ distance) for i in range(devices)])]
    ppermute x1, starting transfers between devices: 2.97 us -> 3.25 us  [local(): outer = lax.ppermute(outer, AXES, across)]
    ppermute x7 -> x8, starting transfers between devices: 8.45 us -> 8.52 us  [partner(): return lax.ppermute(x, AXES, [(i, i ^ distance) for i in range(devices)])]
  transfers between devices with their start and end apart: 8 -> 9, of which waited for: 5 -> 5; matrix products, arithmetic and copies ran while one was open for 0% -> 0% of each run, Pallas kernels for 10% -> 11%
where the time goes in v4:
time: 23.2 us; the launch traced here: 23.1 us
  starting transfers between devices  11.8 us (51%)
  waiting for transfers between devices  5.82 us (25%)
  Pallas kernels  5.38 us (23%)
    ppermute x8, starting transfers between devices, partner(): return lax.ppermute(x, AXES, [(i, i ^ distance) for i in range(devices)])  8.52 us
    ppermute x8, waiting for transfers between devices, partner(): return lax.ppermute(x, AXES, [(i, i ^ distance) for i in range(devices)])  5.82 us
    ppermute x1, starting transfers between devices, local(): outer = lax.ppermute(outer, AXES, across)  3.25 us
    pallas_call x1, Pallas kernels, local(): pl.pallas_call(second_kernel, out_shape=jax.ShapeDtypeStruct((ROWS, chann...  1.38 us
    pallas_call x1, Pallas kernels, local(): pl.pallas_call(share_kernel, out_shape=[packed, packed, edge, edge, near]...  1.19 us
    pallas_call x1, Pallas kernels, local(): pl.pallas_call(tables_kernel, out_shape=[jax.ShapeDtypeStruct((channels,...  0.94 us
    pallas_call x1, Pallas kernels, local(): pl.pallas_call(channels_kernel, out_shape=jax.ShapeDtypeStruct((LAGS // S...  0.81 us
    pallas_call x1, Pallas kernels, local(): pl.pallas_call(first_kernel, out_shape=sums, in_specs=[VMEM] * 2, out_spe...  0.7 us
  transfers between devices with their start and end apart: 9, of which 5 were waited for; matrix products, arithmetic and copies ran while one was open for 0% of the time, Pallas kernels for 11%

profile of v4, /device:TPU:0, one launch (start us, length us, event | category | flops | bytes accessed | tf_op | source)
XLA Modules:
  0.0 23.1 jit_solution(16178824873763328736)
XLA Ops:
  0.0 1.2 %share.1 = (f32[8,1536]{1,0:T(8,128)S(1)}, f32[8,1536]{1,0:T(8,128)S(1)}, f32[16,2048]{1,0:T(8,128)S(1)}, f32[16,2048]{1,0:T(8,128)S(1)}, f32[24,2048]{1,0:T(8,128)S(1)}) custom-call(f32[24,2048]{1,0:T(8,128)} %strain_hbm.1, f32[31]{0:T(128)} %space_hbm.2, s32[3,4]{1,0:T(4,128)} %sources_hbm.1), custom_call_target="tpu_custom_call" | custom-call | tf_op jit(solution)/shard_map/share/pallas_call | solution.py:343
  1.2 0.5 %collective-permute-start = (f32[8,1536]{1,0:T(8,128)S(1)}, f32[8,1536]{1,0:T(8,128)S(1)}, u32[]{:S(2)}, u32[]{:S(2)}) collective-permute-start(f32[8,1536]{1,0:T(8,128)S(1)} %get-tuple-element.29), channel_id=1, source_target_pairs={{0,1},{1,0},{2,3},{3,2},{4,5},{5,4},{6,7},{7,6},{8,9},{9,8},{10,11... | collective-permute-start | bytes 147464 | tf_op jit(solution)/shard_map/ppermute | solution.py:358
  1.7 0.9 %collective-permute-done = f32[8,1536]{1,0:T(8,128)S(1)} collective-permute-done((f32[8,1536]{1,0:T(8,128)S(1)}, f32[8,1536]{1,0:T(8,128)S(1)}, u32[]{:S(2)}, u32[]{:S(2)}) %collective-permute-start) | collective-permute-done | bytes 49184 | tf_op jit(solution)/shard_map/ppermute | solution.py:358
  2.6 3.7 %collective-permute-start.1 = (f32[8,1536]{1,0:T(8,128)S(1)}, f32[8,1536]{1,0:T(8,128)S(1)}, u32[]{:S(2)}, u32[]{:S(2)}) collective-permute-start(f32[8,1536]{1,0:T(8,128)S(1)} %add.18), channel_id=1, source_target_pairs={{0,17},{1,16},{2,19},{3,18},{4,21},{5,20},{6,23},{7,22},{8,25},{9,... | collective-permute-start | bytes 147464 | tf_op jit(solution)/shard_map/ppermute | solution.py:358
  6.3 3.2 %collective-permute-start.7 = (f32[16,2048]{1,0:T(8,128)S(1)}, f32[16,2048]{1,0:T(8,128)S(1)}, u32[]{:S(2)}, u32[]{:S(2)}) collective-permute-start(f32[16,2048]{1,0:T(8,128)S(1)} %get-tuple-element.44), channel_id=1, source_target_pairs={{1,2},{3,4},{5,6},{7,8},{9,10},{11,12},{13,14},{15,16},{17,18},{19... | collective-permute-start | bytes 393224 | tf_op jit(solution)/shard_map/ppermute | solution.py:370
  9.6 0.0 collective-permute-start.6
  9.6 0.0 collective-permute-done.1
  9.6 0.9 %collective-permute-start.2 = (f32[8,1536]{1,0:T(8,128)S(1)}, f32[8,1536]{1,0:T(8,128)S(1)}, u32[]{:S(2)}, u32[]{:S(2)}) collective-permute-start(f32[8,1536]{1,0:T(8,128)S(1)} %add.19), channel_id=1, source_target_pairs={{0,9},{1,8},{2,11},{3,10},{4,13},{5,12},{6,15},{7,14},{8,1},{9,0},... | collective-permute-start | bytes 147464 | tf_op jit(solution)/shard_map/ppermute | solution.py:358
  10.4 0.9 %tables.1 = (bf16[24,168]{1,0:T(8,128)(2,1)S(1)}, bf16[256,256]{1,0:T(8,128)(2,1)S(1)}, bf16[128,256]{1,0:T(8,128)(2,1)S(1)}, bf16[256,384]{1,0:T(8,128)(2,1)S(1)}) custom-call(f32[64]{0:T(128)} %fir_hbm, f32[31]{0:T(128)} %space_hbm.2), custom_call_target="tpu_custom_call" | custom-call | tf_op jit(solution)/shard_map/tables/pallas_call | solution.py:373
  11.4 2.3 %collective-permute-done.2 = f32[8,1536]{1,0:T(8,128)S(1)} collective-permute-done((f32[8,1536]{1,0:T(8,128)S(1)}, f32[8,1536]{1,0:T(8,128)S(1)}, u32[]{:S(2)}, u32[]{:S(2)}) %collective-permute-start.2) | collective-permute-done | bytes 49184 | tf_op jit(solution)/shard_map/ppermute | solution.py:358
  13.7 2.3 %collective-permute-start.5 = (f32[8,1536]{1,0:T(8,128)S(1)}, f32[8,1536]{1,0:T(8,128)S(1)}, u32[]{:S(2)}, u32[]{:S(2)}) collective-permute-start(f32[8,1536]{1,0:T(8,128)S(1)} %add.20), channel_id=1, source_target_pairs={{0,6},{1,7},{2,4},{3,5},{4,2},{5,3},{6,0},{7,1},{8,14},{9,15},{10,... | collective-permute-start | bytes 147464 | tf_op jit(solution)/shard_map/ppermute | solution.py:358
  15.9 0.0 collective-permute-start.4
  15.9 1.0 %collective-permute-start.3 = (f32[8,1536]{1,0:T(8,128)S(1)}, f32[8,1536]{1,0:T(8,128)S(1)}, u32[]{:S(2)}, u32[]{:S(2)}) collective-permute-start(f32[8,1536]{1,0:T(8,128)S(1)} %add.20), channel_id=1, source_target_pairs={{0,5},{1,4},{2,7},{3,6},{4,1},{5,0},{6,3},{7,2},{8,13},{9,12},{10,... | collective-permute-start | bytes 147464 | tf_op jit(solution)/shard_map/ppermute | solution.py:358
  16.9 0.0 collective-permute-done.7.outer_ref
  16.9 0.0 collective-permute-done.6.inner_ref
  16.9 0.8 %channels.1.shifted_ref = bf16[192,2176]{1,0:T(8,128)(2,1)S(1)} custom-call(f32[24,2048]{1,0:T(8,128)S(1)} %get-tuple-element.42.strain_ref, f32[16,2048]{1,0:T(8,128)S(1)} %collective-permute-done.6.inner_ref, f32[16,2048]{1,0:T(8,128)S(1)} %collective-permute-done.7.outer_ref, bf16[24,168]{1,0:T(8,128)(2,1)S(1)} %get-tuple-element.45.space_matrix_ref, ...), custom_call_target="tpu_custom_call" | custom-call | tf_op jit(solution)/shard_map/channels/pallas_call | solution.py:393
  17.8 1.2 %collective-permute-done.5 = f32[8,1536]{1,0:T(8,128)S(1)} collective-permute-done((f32[8,1536]{1,0:T(8,128)S(1)}, f32[8,1536]{1,0:T(8,128)S(1)}, u32[]{:S(2)}, u32[]{:S(2)}) %collective-permute-start.5) | collective-permute-done | bytes 49184 | tf_op jit(solution)/shard_map/ppermute | solution.py:358
  19.0 1.1 %collective-permute-done.4 = f32[8,1536]{1,0:T(8,128)S(1)} collective-permute-done((f32[8,1536]{1,0:T(8,128)S(1)}, f32[8,1536]{1,0:T(8,128)S(1)}, u32[]{:S(2)}, u32[]{:S(2)}) %collective-permute-start.4) | collective-permute-done | bytes 49184 | tf_op jit(solution)/shard_map/ppermute | solution.py:358
  20.0 0.0 collective-permute-done.3
  20.0 0.4 %norm.1.normed_ref = bf16[16,1024]{1,0:T(8,128)(2,1)S(1)} custom-call(f32[8,1536]{1,0:T(8,128)S(1)} %add_add_fusion.total_ref, bf16[256,256]{1,0:T(8,128)(2,1)S(1)} %get-tuple-element.46.both_ref, bf16[128,256]{1,0:T(8,128)(2,1)S(1)} %get-tuple-element.47.low_ref, bf16[256,384]{1,0:T(8,128)(2,1)S(1)} %get-tuple-element.48.window_ref), custom_call_target="tpu_custom_call" | custom-call | tf_op jit(solution)/shard_map/norm/pallas_call | solution.py:405
  20.4 0.2 collective-permute-start.8
  20.6 0.7 %first.1.sums_ref = f32[6,24,256]{2,1,0:T(8,128)S(1)} custom-call(bf16[16,1024]{1,0:T(8,128)(2,1)S(1)} %norm.1.normed_ref, bf16[192,2176]{1,0:T(8,128)(2,1)S(1)} %channels.1.shifted_ref), custom_call_target="tpu_custom_call" | custom-call | tf_op jit(solution)/shard_map/first/pallas_call | solution.py:415
  21.3 0.4 %collective-permute-done.8.normed_ref = bf16[16,1024]{1,0:T(8,128)(2,1)S(1)} collective-permute-done((bf16[16,1024]{1,0:T(8,128)(2,1)S(1)}, bf16[16,1024]{1,0:T(8,128)(2,1)S(1)}, u32[]{:S(2)}, u32[]{:S(2)}) %collective-permute-start.8) | collective-permute-done | bytes 32800 | tf_op jit(solution)/shard_map/ppermute | solution.py:358
  21.7 1.4 %second.1 = f32[12,24,256]{2,1,0:T(8,128)} custom-call(bf16[16,1024]{1,0:T(8,128)(2,1)S(1)} %collective-permute-done.8.normed_ref, bf16[192,2176]{1,0:T(8,128)(2,1)S(1)} %channels.1.shifted_ref, f32[6,24,256]{2,1,0:T(8,128)S(1)} %first.1.sums_ref), custom_call_target="tpu_custom_call" | custom-call | tf_op jit(solution)/shard_map/second/pallas_call | solution.py:423
  (4 shorter events, 0.0 us)
Async XLA Ops:
  1.2 1.4 %collective-permute-start = (f32[8,1536]{1,0:T(8,128)S(1)}, f32[8,1536]{1,0:T(8,128)S(1)}, u32[]{:S(2)}, u32[]{:S(2)}) collective-permute-start(f32[8,1536]{1,0:T(8,128)S(1)} %get-tuple-element.29), channel_id=1, source_target_pairs={{0,1},{1,0},{2,3},{3,2},{4,5},{5,4},{6,7},{7,6},{8,9},{9,8},{10,11... | collective-permute-start | bytes 147464 | tf_op jit(solution)/shard_map/ppermute | solution.py:358
  2.6 7.0 %collective-permute-start.1 = (f32[8,1536]{1,0:T(8,128)S(1)}, f32[8,1536]{1,0:T(8,128)S(1)}, u32[]{:S(2)}, u32[]{:S(2)}) collective-permute-start(f32[8,1536]{1,0:T(8,128)S(1)} %add.18), channel_id=1, source_target_pairs={{0,17},{1,16},{2,19},{3,18},{4,21},{5,20},{6,23},{7,22},{8,25},{9,... | collective-permute-start | bytes 147464 | tf_op jit(solution)/shard_map/ppermute | solution.py:358
  6.3 10.6 %collective-permute-start.7 = (f32[16,2048]{1,0:T(8,128)S(1)}, f32[16,2048]{1,0:T(8,128)S(1)}, u32[]{:S(2)}, u32[]{:S(2)}) collective-permute-start(f32[16,2048]{1,0:T(8,128)S(1)} %get-tuple-element.44), channel_id=1, source_target_pairs={{1,2},{3,4},{5,6},{7,8},{9,10},{11,12},{13,14},{15,16},{17,18},{19... | collective-permute-start | bytes 393224 | tf_op jit(solution)/shard_map/ppermute | solution.py:370
  9.6 7.4 %collective-permute-start.6 = (f32[16,2048]{1,0:T(8,128)S(1)}, f32[16,2048]{1,0:T(8,128)S(1)}, u32[]{:S(2)}, u32[]{:S(2)}) collective-permute-start(f32[16,2048]{1,0:T(8,128)S(1)} %get-tuple-element.43), channel_id=1, source_target_pairs={{0,1},{1,0},{2,3},{3,2},{4,5},{5,4},{6,7},{7,6},{8,9},{9,8},{10,11... | collective-permute-start | bytes 393224 | tf_op jit(solution)/shard_map/ppermute | solution.py:358
  9.6 4.1 %collective-permute-start.2 = (f32[8,1536]{1,0:T(8,128)S(1)}, f32[8,1536]{1,0:T(8,128)S(1)}, u32[]{:S(2)}, u32[]{:S(2)}) collective-permute-start(f32[8,1536]{1,0:T(8,128)S(1)} %add.19), channel_id=1, source_target_pairs={{0,9},{1,8},{2,11},{3,10},{4,13},{5,12},{6,15},{7,14},{8,1},{9,0},... | collective-permute-start | bytes 147464 | tf_op jit(solution)/shard_map/ppermute | solution.py:358
  13.7 5.3 %collective-permute-start.5 = (f32[8,1536]{1,0:T(8,128)S(1)}, f32[8,1536]{1,0:T(8,128)S(1)}, u32[]{:S(2)}, u32[]{:S(2)}) collective-permute-start(f32[8,1536]{1,0:T(8,128)S(1)} %add.20), channel_id=1, source_target_pairs={{0,6},{1,7},{2,4},{3,5},{4,2},{5,3},{6,0},{7,1},{8,14},{9,15},{10,... | collective-permute-start | bytes 147464 | tf_op jit(solution)/shard_map/ppermute | solution.py:358
  15.9 4.1 %collective-permute-start.4 = (f32[8,1536]{1,0:T(8,128)S(1)}, f32[8,1536]{1,0:T(8,128)S(1)}, u32[]{:S(2)}, u32[]{:S(2)}) collective-permute-start(f32[8,1536]{1,0:T(8,128)S(1)} %add.20), channel_id=1, source_target_pairs={{0,3},{1,2},{2,1},{3,0},{4,7},{5,6},{6,5},{7,4},{8,11},{9,10},{10,... | collective-permute-start | bytes 147464 | tf_op jit(solution)/shard_map/ppermute | solution.py:358
  15.9 4.1 %collective-permute-start.3 = (f32[8,1536]{1,0:T(8,128)S(1)}, f32[8,1536]{1,0:T(8,128)S(1)}, u32[]{:S(2)}, u32[]{:S(2)}) collective-permute-start(f32[8,1536]{1,0:T(8,128)S(1)} %add.20), channel_id=1, source_target_pairs={{0,5},{1,4},{2,7},{3,6},{4,1},{5,0},{6,3},{7,2},{8,13},{9,12},{10,... | collective-permute-start | bytes 147464 | tf_op jit(solution)/shard_map/ppermute | solution.py:358
  20.4 1.3 %collective-permute-start.8 = (bf16[16,1024]{1,0:T(8,128)(2,1)S(1)}, bf16[16,1024]{1,0:T(8,128)(2,1)S(1)}, u32[]{:S(2)}, u32[]{:S(2)}) collective-permute-start(bf16[16,1024]{1,0:T(8,128)(2,1)S(1)} %norm.1.normed_ref), channel_id=1, source_target_pairs={{0,1},{1,0},{2,3},{3,2},{4,5},{5,4},{6,7},{7,6},{8,9},{9,8},{10,11... | collective-permute-start | bytes 98312 | tf_op jit(solution)/shard_map/ppermute | solution.py:358

commit v5 on v4

--- a/solution.py
+++ b/solution.py
@@ -132,45 +132,49 @@
     return copies
 
 
-def share_kernel(
+def load_kernel(
     strain_hbm,
     space_hbm,
     sources_hbm,
-    keep_ref,
-    send_ref,
-    inner_ref,
+    near_ref,
     outer_ref,
-    strain_ref,
+    part_ref,
+    matrix_ref,
     space_ref,
     sources_ref,
     sems,
 ):
     copies = fetch(
-        [(sources_hbm, sources_ref), (space_hbm, space_ref), (strain_hbm, strain_ref)], sems
-    )
-    channels = strain_ref.shape[0]
+        [(sources_hbm, sources_ref), (space_hbm, space_ref), (strain_hbm, near_ref)], sems
+    )
+    channels = near_ref.shape[0]
     me = lax.axis_index(AXES)
-    mine = parity(me)
+    half = parity(me)
     half_span = (space_ref.shape[0] - 1) // 2
+    copies[0].wait()
+    shape = (16, 2 * channels)
+    row = lax.broadcasted_iota(jnp.int32, shape, 0)
+    lane = lax.broadcasted_iota(jnp.int32, shape, 1)
+    source = jnp.full(shape, -(1 << 20), jnp.int32)
+    for k in range(HALF_ROWS):
+        number = half * HALF_ROWS + k
+        source = jnp.where(row == k, sources_ref[number // SRC, number % SRC], source)
+    copies[1].wait()
+    matrix = taps_at(space_ref, lane + (me - me % 2) * channels - source + half_span)
     even = me % 2 == 0
-    copies[0].wait()
-    row = lax.broadcasted_iota(jnp.int32, (16, channels), 0)
-    lane = lax.broadcasted_iota(jnp.int32, (16, channels), 1)
-    source = jnp.full((16, channels), -(1 << 20), jnp.int32)
-    for k in range(ROWS):
-        half = mine if k < HALF_ROWS else 1 - mine
-        number = half * HALF_ROWS + k % HALF_ROWS
-        place = k if k < HALF_ROWS else k - HALF_ROWS + 8
-        source = jnp.where(row == place, sources_ref[number // SRC, number % SRC], source)
-    copies[1].wait()
-    matrix = taps_at(space_ref, lane + me * channels - source + half_span)
+    own = jnp.where(even, matrix[:, :channels], matrix[:, channels:])
+    other = jnp.where(even, matrix[:, channels:], matrix[:, :channels])
+    matrix_ref[...] = split_columns(other)
     copies[2].wait()
-    x = strain_ref[...]
-    inner_ref[...] = jnp.where(even, x[channels - HALO :], x[:HALO])
+    x = near_ref[...]
     outer_ref[...] = jnp.where(even, x[:HALO], x[channels - HALO :])
-    share = jnp.dot(split_columns(matrix), split_rows(x), preferred_element_type=F32)
-    keep_ref[...] = pack(share[:HALF_ROWS])
-    send_ref[...] = pack(share[8 : 8 + HALF_ROWS])
+    part = jnp.dot(split_columns(own), split_rows(x), preferred_element_type=F32)
+    part_ref[...] = pack(part[:HALF_ROWS])
+
+
+def share_kernel(other_ref, part_ref, matrix_ref, total_ref):
+    part = jnp.dot(matrix_ref[...], split_rows(other_ref[...]), preferred_element_type=F32)
+    total_ref[...] = part_ref[...] + pack(part[:HALF_ROWS])
 
 
 def tables_kernel(
@@ -192,7 +196,7 @@
 
 def channels_kernel(
     strain_ref,
-    inner_ref,
+    other_ref,
     outer_ref,
     space_matrix_ref,
     both_ref,
@@ -203,9 +207,10 @@
     channels, samples = strain_ref.shape
     me = lax.axis_index(AXES)
     even = me % 2 == 0
-    inner, outer = inner_ref[...], outer_ref[...]
+    other, outer = other_ref[...], outer_ref[...]
     outer = jnp.where((me == 0) | (me == lax.axis_size(AXES) - 1), 0.0, outer)
-    before, after = jnp.where(even, outer, inner), jnp.where(even, inner, outer)
+    before = jnp.where(even, outer, other[channels - HALO :])
+    after = jnp.where(even, other[:HALO], outer)
     x = jnp.concatenate([before, strain_ref[...], after], axis=0)
     spaced = jnp.dot(space_matrix_ref[...], split_rows(x), preferred_element_type=F32)
     normed = filter_and_norm(spaced, both_ref[...], low_ref[...], window_ref[...])
@@ -337,35 +342,49 @@
 def local(strain, fir_taps, space_taps, sources):
     channels, samples = strain.shape
     devices = lax.axis_size(AXES)
+
+    def partner(x, mask):
+        return lax.ppermute(x, AXES, [(i, i ^ mask) for i in range(devices)])
+
+    beside = partner(strain, 1)
     packed = jax.ShapeDtypeStruct((8, samples * 3 // 4), F32)
-    edge = jax.ShapeDtypeStruct((HALO, samples), F32)
-    near = jax.ShapeDtypeStruct(strain.shape, F32)
-    keep, send, inner, outer, near = pl.pallas_call(
-        share_kernel,
-        out_shape=[packed, packed, edge, edge, near],
+    near, outer, part, matrix = pl.pallas_call(
+        load_kernel,
+        out_shape=[
+            jax.ShapeDtypeStruct(strain.shape, F32),
+            jax.ShapeDtypeStruct((HALO, samples), F32),
+            packed,
+            jax.ShapeDtypeStruct((16, 3 * channels), BF16),
+        ],
         in_specs=[HBM] * 3,
-        out_specs=[VMEM] * 5,
+        out_specs=[VMEM] * 4,
         scratch_shapes=[
             pltpu.SMEM(space_taps.shape, F32),
             pltpu.SMEM(sources.shape, jnp.int32),
             pltpu.SemaphoreType.DMA((3,)),
         ],
         compiler_params=SMALL,
+        name="load",
+    )(*[in_hbm(x) for x in (strain, space_taps, sources)])
+    total = pl.pallas_call(
+        share_kernel,
+        out_shape=packed,
+        in_specs=[VMEM] * 3,
+        out_specs=VMEM,
+        compiler_params=SMALL,
         name="share",
-    )(*[in_hbm(x) for x in (strain, space_taps, sources)])
-
-    def partner(x, distance):
-        return lax.ppermute(x, AXES, [(i, i ^ distance) for i in range(devices)])
-
-    total = keep + partner(send, 1)
-    across = [(i, i + 1) for i in range(1, devices - 1, 2)] + [(0, devices - 1)]
-    across = across + [(j, i) for i, j in across]
+    )(beside, part, matrix)
+    across = [(0, 2), (2, 1), (1, 0)]
+    across += [(devices - 1, devices - 3), (devices - 3, devices - 2), (devices - 2, devices - 1)]
+    for k in range(3, devices - 4, 2):
+        across += [(k, k + 1), (k + 1, k)]
+    me = lax.axis_index(AXES)
+    outer = jnp.where(me == 0, beside[channels - HALO :], outer)
+    outer = jnp.where(me == devices - 1, beside[:HALO], outer)
     steps = [1 << k for k in range(1, devices.bit_length() - 1)]
     order = [(distance + 1,) for distance in steps[:1:-1]] + [(5, 3, 6)]
     for place, masks in enumerate(order):
         if place == 0:
-            total, inner = lax.optimization_barrier((total, inner))
-            inner = partner(inner, 1)
             total, outer = lax.optimization_barrier((total, outer))
             outer = lax.ppermute(outer, AXES, across)
         if place == 1:
@@ -399,7 +418,7 @@
                 out_specs=VMEM,
                 compiler_params=SMALL,
                 name="channels",
-            )(near, inner, outer, *tables)
+            )(near, beside, outer, *tables)
         total = sum([partner(total, mask) for mask in masks], total)
     total, shifted = lax.optimization_barrier((total, shifted))
     mine = pl.pallas_call(

time: 23.2 us -> 21.7 us (0.935)
  waiting for transfers between devices: 5.82 us -> 4.49 us
  starting transfers between devices: 11.8 us -> 11.4 us
    ppermute x1, starting transfers between devices: 3.25 us -> 1.52 us  [local(): outer = lax.ppermute(outer, AXES, across)]
    ppermute x8 -> x7, starting transfers between devices: 8.52 us -> 9.87 us  [partner(): return lax.ppermute(x, AXES, [(i, i ^ mask) for i in range(devices)])]
    ppermute x8 -> x7, waiting for transfers between devices: 5.82 us -> 4.49 us  [partner(): return lax.ppermute(x, AXES, [(i, i ^ mask) for i in range(devices)])]
    pallas_call x1 -> x2, Pallas kernels: 1.19 us -> 1.35 us  [the longest x1 1.18 us: local(): pl.pallas_call(load_kernel, out_shape=[jax.ShapeDtypeStruct(strain.shape,...]
  transfers between devices with their start and end apart: 9 -> 8, of which waited for: 5 -> 6; matrix products, arithmetic and copies ran while one was open for 0% -> 0% of each run, Pallas kernels for 11% -> 17%
where the time goes in v5:
time: 21.7 us; the launch traced here: 21.6 us
  starting transfers between devices  11.4 us (53%)
  Pallas kernels  5.56 us (26%)
  waiting for transfers between devices  4.49 us (21%)
    ppermute x7, starting transfers between devices, partner(): return lax.ppermute(x, AXES, [(i, i ^ mask) for i in range(devices)])  9.87 us
    ppermute x7, waiting for transfers between devices, partner(): return lax.ppermute(x, AXES, [(i, i ^ mask) for i in range(devices)])  4.49 us
    ppermute x1, starting transfers between devices, local(): outer = lax.ppermute(outer, AXES, across)  1.52 us
    pallas_call x1, Pallas kernels, local(): pl.pallas_call(second_kernel, out_shape=jax.ShapeDtypeStruct((ROWS, chann...  1.38 us
    pallas_call x1, Pallas kernels, local(): pl.pallas_call(load_kernel, out_shape=[jax.ShapeDtypeStruct(strain.shape,...  1.18 us
    pallas_call x1, Pallas kernels, local(): pl.pallas_call(tables_kernel, out_shape=[jax.ShapeDtypeStruct((channels,...  0.94 us
    pallas_call x1, Pallas kernels, local(): pl.pallas_call(channels_kernel, out_shape=jax.ShapeDtypeStruct((LAGS // S...  0.81 us
    pallas_call x1, Pallas kernels, local(): pl.pallas_call(first_kernel, out_shape=sums, in_specs=[VMEM] * 2, out_spe...  0.7 us
  transfers between devices with their start and end apart: 8, of which 6 were waited for; matrix products, arithmetic and copies ran while one was open for 0% of the time, Pallas kernels for 17%

profile of v5, /device:TPU:0, one launch (start us, length us, event | category | flops | bytes accessed | tf_op | source)
XLA Modules:
  0.0 21.6 jit_solution(3197750657560387184)
XLA Ops:
  0.0 0.5 %collective-permute-start = (f32[24,2048]{1,0:T(8,128)}, f32[24,2048]{1,0:T(8,128)S(1)}, u32[]{:S(2)}, u32[]{:S(2)}) collective-permute-start(f32[24,2048]{1,0:T(8,128)} %strain_hbm.1), channel_id=1, source_target_pairs={{0,1},{1,0},{2,3},{3,2},{4,5},{5,4},{6,7},{7,6},{8,9},{9,8},{10,11... | collective-permute-start | bytes 589832 | tf_op jit(solution)/shard_map/ppermute | solution.py:347
  0.5 1.2 %load.1 = (f32[24,2048]{1,0:T(8,128)S(1)}, f32[16,2048]{1,0:T(8,128)S(1)}, f32[8,1536]{1,0:T(8,128)S(1)}, bf16[16,72]{1,0:T(8,128)(2,1)S(1)}) custom-call(f32[24,2048]{1,0:T(8,128)} %strain_hbm.1, f32[31]{0:T(128)} %space_hbm.2, s32[3,4]{1,0:T(4,128)} %sources_hbm.1), custom_call_target="tpu_custom_call" | custom-call | tf_op jit(solution)/shard_map/load/pallas_call | solution.py:351
  1.6 0.1 collective-permute-done.other_ref
  1.7 0.2 share.1
  1.9 3.8 %collective-permute-start.1 = (f32[8,1536]{1,0:T(8,128)S(1)}, f32[8,1536]{1,0:T(8,128)S(1)}, u32[]{:S(2)}, u32[]{:S(2)}) collective-permute-start(f32[8,1536]{1,0:T(8,128)S(1)} %share.1), channel_id=1, source_target_pairs={{0,17},{1,16},{2,19},{3,18},{4,21},{5,20},{6,23},{7,22},{8,25},{9,... | collective-permute-start | bytes 147464 | tf_op jit(solution)/shard_map/ppermute | solution.py:347
  5.7 1.5 %collective-permute-start.6 = (f32[16,2048]{1,0:T(8,128)S(1)}, f32[16,2048]{1,0:T(8,128)S(1)}, u32[]{:S(2)}, u32[]{:S(2)}) collective-permute-start(f32[16,2048]{1,0:T(8,128)S(1)} %fusion), channel_id=1, source_target_pairs={{0,2},{2,1},{1,0},{31,29},{29,30},{30,31},{3,4},{4,3},{5,6},{6,5},... | collective-permute-start | bytes 393224 | tf_op jit(solution)/shard_map/ppermute | solution.py:389
  7.2 0.3 %collective-permute-done.1 = f32[8,1536]{1,0:T(8,128)S(1)} collective-permute-done((f32[8,1536]{1,0:T(8,128)S(1)}, f32[8,1536]{1,0:T(8,128)S(1)}, u32[]{:S(2)}, u32[]{:S(2)}) %collective-permute-start.1) | collective-permute-done | bytes 49184 | tf_op jit(solution)/shard_map/ppermute | solution.py:347
  7.5 2.2 %collective-permute-start.2 = (f32[8,1536]{1,0:T(8,128)S(1)}, f32[8,1536]{1,0:T(8,128)S(1)}, u32[]{:S(2)}, u32[]{:S(2)}) collective-permute-start(f32[8,1536]{1,0:T(8,128)S(1)} %add.19), channel_id=1, source_target_pairs={{0,9},{1,8},{2,11},{3,10},{4,13},{5,12},{6,15},{7,14},{8,1},{9,0},... | collective-permute-start | bytes 147464 | tf_op jit(solution)/shard_map/ppermute | solution.py:347
  9.7 0.9 %tables.1 = (bf16[24,168]{1,0:T(8,128)(2,1)S(1)}, bf16[256,256]{1,0:T(8,128)(2,1)S(1)}, bf16[128,256]{1,0:T(8,128)(2,1)S(1)}, bf16[256,384]{1,0:T(8,128)(2,1)S(1)}) custom-call(f32[64]{0:T(128)} %fir_hbm, f32[31]{0:T(128)} %space_hbm.2), custom_call_target="tpu_custom_call" | custom-call | tf_op jit(solution)/shard_map/tables/pallas_call | solution.py:392
  10.7 1.2 %collective-permute-done.2 = f32[8,1536]{1,0:T(8,128)S(1)} collective-permute-done((f32[8,1536]{1,0:T(8,128)S(1)}, f32[8,1536]{1,0:T(8,128)S(1)}, u32[]{:S(2)}, u32[]{:S(2)}) %collective-permute-start.2) | collective-permute-done | bytes 49184 | tf_op jit(solution)/shard_map/ppermute | solution.py:347
  11.9 2.2 %collective-permute-start.5 = (f32[8,1536]{1,0:T(8,128)S(1)}, f32[8,1536]{1,0:T(8,128)S(1)}, u32[]{:S(2)}, u32[]{:S(2)}) collective-permute-start(f32[8,1536]{1,0:T(8,128)S(1)} %add.20), channel_id=1, source_target_pairs={{0,6},{1,7},{2,4},{3,5},{4,2},{5,3},{6,0},{7,1},{8,14},{9,15},{10,... | collective-permute-start | bytes 147464 | tf_op jit(solution)/shard_map/ppermute | solution.py:347
  14.1 0.2 collective-permute-start.4
  14.3 0.9 %collective-permute-start.3 = (f32[8,1536]{1,0:T(8,128)S(1)}, f32[8,1536]{1,0:T(8,128)S(1)}, u32[]{:S(2)}, u32[]{:S(2)}) collective-permute-start(f32[8,1536]{1,0:T(8,128)S(1)} %add.20), channel_id=1, source_target_pairs={{0,5},{1,4},{2,7},{3,6},{4,1},{5,0},{6,3},{7,2},{8,13},{9,12},{10,... | collective-permute-start | bytes 147464 | tf_op jit(solution)/shard_map/ppermute | solution.py:347
  15.2 0.0 collective-permute-done.6.outer_ref
  15.2 0.8 %channels.1.shifted_ref = bf16[192,2176]{1,0:T(8,128)(2,1)S(1)} custom-call(f32[24,2048]{1,0:T(8,128)S(1)} %get-tuple-element.37.strain_ref, f32[24,2048]{1,0:T(8,128)S(1)} %collective-permute-done.other_ref, f32[16,2048]{1,0:T(8,128)S(1)} %collective-permute-done.6.outer_ref, bf16[24,168]{1,0:T(8,128)(2,1)S(1)} %get-tuple-element.39.space_matrix_ref, ...), custom_call_target="tpu_custom_call" | custom-call | tf_op jit(solution)/shard_map/channels/pallas_call | solution.py:412
  16.0 1.2 %collective-permute-done.5 = f32[8,1536]{1,0:T(8,128)S(1)} collective-permute-done((f32[8,1536]{1,0:T(8,128)S(1)}, f32[8,1536]{1,0:T(8,128)S(1)}, u32[]{:S(2)}, u32[]{:S(2)}) %collective-permute-start.5) | collective-permute-done | bytes 49184 | tf_op jit(solution)/shard_map/ppermute | solution.py:347
  17.2 1.3 %collective-permute-done.4 = f32[8,1536]{1,0:T(8,128)S(1)} collective-permute-done((f32[8,1536]{1,0:T(8,128)S(1)}, f32[8,1536]{1,0:T(8,128)S(1)}, u32[]{:S(2)}, u32[]{:S(2)}) %collective-permute-start.4) | collective-permute-done | bytes 49184 | tf_op jit(solution)/shard_map/ppermute | solution.py:347
  18.5 0.0 collective-permute-done.3
  18.5 0.4 %norm.1.normed_ref = bf16[16,1024]{1,0:T(8,128)(2,1)S(1)} custom-call(f32[8,1536]{1,0:T(8,128)S(1)} %add_add_fusion.total_ref, bf16[256,256]{1,0:T(8,128)(2,1)S(1)} %get-tuple-element.40.both_ref, bf16[128,256]{1,0:T(8,128)(2,1)S(1)} %get-tuple-element.41.low_ref, bf16[256,384]{1,0:T(8,128)(2,1)S(1)} %get-tuple-element.42.window_ref), custom_call_target="tpu_custom_call" | custom-call | tf_op jit(solution)/shard_map/norm/pallas_call | solution.py:424
  18.9 0.2 collective-permute-start.7
  19.1 0.7 %first.1.sums_ref = f32[6,24,256]{2,1,0:T(8,128)S(1)} custom-call(bf16[16,1024]{1,0:T(8,128)(2,1)S(1)} %norm.1.normed_ref, bf16[192,2176]{1,0:T(8,128)(2,1)S(1)} %channels.1.shifted_ref), custom_call_target="tpu_custom_call" | custom-call | tf_op jit(solution)/shard_map/first/pallas_call | solution.py:434
  19.8 0.4 %collective-permute-done.7.normed_ref = bf16[16,1024]{1,0:T(8,128)(2,1)S(1)} collective-permute-done((bf16[16,1024]{1,0:T(8,128)(2,1)S(1)}, bf16[16,1024]{1,0:T(8,128)(2,1)S(1)}, u32[]{:S(2)}, u32[]{:S(2)}) %collective-permute-start.7) | collective-permute-done | bytes 32800 | tf_op jit(solution)/shard_map/ppermute | solution.py:347
  20.2 1.4 %second.1 = f32[12,24,256]{2,1,0:T(8,128)} custom-call(bf16[16,1024]{1,0:T(8,128)(2,1)S(1)} %collective-permute-done.7.normed_ref, bf16[192,2176]{1,0:T(8,128)(2,1)S(1)} %channels.1.shifted_ref, f32[6,24,256]{2,1,0:T(8,128)S(1)} %first.1.sums_ref), custom_call_target="tpu_custom_call" | custom-call | tf_op jit(solution)/shard_map/second/pallas_call | solution.py:442
  (4 shorter events, 0.1 us)
Async XLA Ops:
  0.0 1.7 %collective-permute-start = (f32[24,2048]{1,0:T(8,128)}, f32[24,2048]{1,0:T(8,128)S(1)}, u32[]{:S(2)}, u32[]{:S(2)}) collective-permute-start(f32[24,2048]{1,0:T(8,128)} %strain_hbm.1), channel_id=1, source_target_pairs={{0,1},{1,0},{2,3},{3,2},{4,5},{5,4},{6,7},{7,6},{8,9},{9,8},{10,11... | collective-permute-start | bytes 589832 | tf_op jit(solution)/shard_map/ppermute | solution.py:347
  1.9 5.6 %collective-permute-start.1 = (f32[8,1536]{1,0:T(8,128)S(1)}, f32[8,1536]{1,0:T(8,128)S(1)}, u32[]{:S(2)}, u32[]{:S(2)}) collective-permute-start(f32[8,1536]{1,0:T(8,128)S(1)} %share.1), channel_id=1, source_target_pairs={{0,17},{1,16},{2,19},{3,18},{4,21},{5,20},{6,23},{7,22},{8,25},{9,... | collective-permute-start | bytes 147464 | tf_op jit(solution)/shard_map/ppermute | solution.py:347
  5.7 9.5 %collective-permute-start.6 = (f32[16,2048]{1,0:T(8,128)S(1)}, f32[16,2048]{1,0:T(8,128)S(1)}, u32[]{:S(2)}, u32[]{:S(2)}) collective-permute-start(f32[16,2048]{1,0:T(8,128)S(1)} %fusion), channel_id=1, source_target_pairs={{0,2},{2,1},{1,0},{31,29},{29,30},{30,31},{3,4},{4,3},{5,6},{6,5},... | collective-permute-start | bytes 393224 | tf_op jit(solution)/shard_map/ppermute | solution.py:389
  7.5 4.4 %collective-permute-start.2 = (f32[8,1536]{1,0:T(8,128)S(1)}, f32[8,1536]{1,0:T(8,128)S(1)}, u32[]{:S(2)}, u32[]{:S(2)}) collective-permute-start(f32[8,1536]{1,0:T(8,128)S(1)} %add.19), channel_id=1, source_target_pairs={{0,9},{1,8},{2,11},{3,10},{4,13},{5,12},{6,15},{7,14},{8,1},{9,0},... | collective-permute-start | bytes 147464 | tf_op jit(solution)/shard_map/ppermute | solution.py:347
  11.9 5.3 %collective-permute-start.5 = (f32[8,1536]{1,0:T(8,128)S(1)}, f32[8,1536]{1,0:T(8,128)S(1)}, u32[]{:S(2)}, u32[]{:S(2)}) collective-permute-start(f32[8,1536]{1,0:T(8,128)S(1)} %add.20), channel_id=1, source_target_pairs={{0,6},{1,7},{2,4},{3,5},{4,2},{5,3},{6,0},{7,1},{8,14},{9,15},{10,... | collective-permute-start | bytes 147464 | tf_op jit(solution)/shard_map/ppermute | solution.py:347
  14.1 4.4 %collective-permute-start.4 = (f32[8,1536]{1,0:T(8,128)S(1)}, f32[8,1536]{1,0:T(8,128)S(1)}, u32[]{:S(2)}, u32[]{:S(2)}) collective-permute-start(f32[8,1536]{1,0:T(8,128)S(1)} %add.20), channel_id=1, source_target_pairs={{0,3},{1,2},{2,1},{3,0},{4,7},{5,6},{6,5},{7,4},{8,11},{9,10},{10,... | collective-permute-start | bytes 147464 | tf_op jit(solution)/shard_map/ppermute | solution.py:347
  14.3 4.2 %collective-permute-start.3 = (f32[8,1536]{1,0:T(8,128)S(1)}, f32[8,1536]{1,0:T(8,128)S(1)}, u32[]{:S(2)}, u32[]{:S(2)}) collective-permute-start(f32[8,1536]{1,0:T(8,128)S(1)} %add.20), channel_id=1, source_target_pairs={{0,5},{1,4},{2,7},{3,6},{4,1},{5,0},{6,3},{7,2},{8,13},{9,12},{10,... | collective-permute-start | bytes 147464 | tf_op jit(solution)/shard_map/ppermute | solution.py:347
  18.9 1.3 %collective-permute-start.7 = (bf16[16,1024]{1,0:T(8,128)(2,1)S(1)}, bf16[16,1024]{1,0:T(8,128)(2,1)S(1)}, u32[]{:S(2)}, u32[]{:S(2)}) collective-permute-start(bf16[16,1024]{1,0:T(8,128)(2,1)S(1)} %norm.1.normed_ref), channel_id=1, source_target_pairs={{0,1},{1,0},{2,3},{3,2},{4,5},{5,4},{6,7},{7,6},{8,9},{9,8},{10,11... | collective-permute-start | bytes 98312 | tf_op jit(solution)/shard_map/ppermute | solution.py:347

commit v6 on v5

--- a/solution.py
+++ b/solution.py
@@ -29,14 +29,21 @@
     return high, (x - high.astype(F32)).astype(BF16)
 
 
-def split_rows(x):
+def thirds(x):
     high = x.astype(BF16).astype(F32)
-    return jnp.concatenate([high, x - high, high], axis=0).astype(BF16)
-
-
-def split_columns(x):
-    high = x.astype(BF16).astype(F32)
-    return jnp.concatenate([high, high, x - high], axis=1).astype(BF16)
+    rest = x - high
+    middle = rest.astype(BF16).astype(F32)
+    return high, middle, rest - middle
+
+
+def data_terms(x, axis):
+    high, middle, low = thirds(x)
+    return jnp.concatenate([high, high, middle, high, low, middle], axis=axis).astype(BF16)
+
+
+def tap_terms(x, axis):
+    high, middle, low = thirds(x)
+    return jnp.concatenate([high, middle, high, low, high, middle], axis=axis).astype(BF16)
 
 
 def taps_at(taps_ref, index):
@@ -81,11 +88,10 @@
     return jnp.concatenate([jnp.where(b, 1.0, 0.0).astype(BF16) for b in bands], axis=1)
 
 
-def filter_and_norm(x, fir_both, fir_low, window):
+def filter_and_norm(x, fir_terms, window):
     rows, samples = x.shape
-    high, low = split(to_blocks(x))
     dot = functools.partial(jnp.dot, preferred_element_type=F32)
-    full = dot(jnp.concatenate([high, low], axis=1), fir_both) + dot(high, fir_low)
+    full = dot(data_terms(to_blocks(x), 1), fir_terms)
     smooth = full[:, :LANES] + earlier(full[:, LANES:], rows)
     high, low = split(jnp.abs(smooth))
     sums = dot(jnp.concatenate([high, low], axis=1), window)
@@ -164,21 +170,21 @@
     even = me % 2 == 0
     own = jnp.where(even, matrix[:, :channels], matrix[:, channels:])
     other = jnp.where(even, matrix[:, channels:], matrix[:, :channels])
-    matrix_ref[...] = split_columns(other)
+    matrix_ref[...] = tap_terms(other, 1)
     copies[2].wait()
     x = near_ref[...]
     outer_ref[...] = jnp.where(even, x[:HALO], x[channels - HALO :])
-    part = jnp.dot(split_columns(own), split_rows(x), preferred_element_type=F32)
+    part = jnp.dot(tap_terms(own, 1), data_terms(x, 0), preferred_element_type=F32)
     part_ref[...] = pack(part[:HALF_ROWS])
 
 
 def share_kernel(other_ref, part_ref, matrix_ref, total_ref):
-    part = jnp.dot(matrix_ref[...], split_rows(other_ref[...]), preferred_element_type=F32)
+    part = jnp.dot(matrix_ref[...], data_terms(other_ref[...], 0), preferred_element_type=F32)
     total_ref[...] = part_ref[...] + pack(part[:HALF_ROWS])
 
 
 def tables_kernel(
-    fir_hbm, space_hbm, space_matrix_ref, both_ref, low_ref, window_ref, fir_ref, space_ref, sems
+    fir_hbm, space_hbm, space_matrix_ref, fir_matrix_ref, window_ref, fir_ref, space_ref, sems
 ):
     copies = fetch([(space_hbm, space_ref), (fir_hbm, fir_ref)], sems)
     window_ref[...] = window_bands()
@@ -187,11 +193,11 @@
     row = lax.broadcasted_iota(jnp.int32, (channels, channels + 2 * HALO), 0)
     column = lax.broadcasted_iota(jnp.int32, (channels, channels + 2 * HALO), 1)
     copies[0].wait()
-    space_matrix_ref[...] = split_columns(taps_at(space_ref, column - HALO - row + half_span))
+    space_matrix_ref[...] = tap_terms(
+        taps_at(space_ref, column - HALO - row + half_span), 1
+    )
     copies[1].wait()
-    high, low = split(fir_matrix(fir_ref))
-    both_ref[...] = jnp.concatenate([high, high], axis=0)
-    low_ref[...] = low
+    fir_matrix_ref[...] = tap_terms(fir_matrix(fir_ref), 0)
 
 
 def channels_kernel(
@@ -199,8 +205,7 @@
     other_ref,
     outer_ref,
     space_matrix_ref,
-    both_ref,
-    low_ref,
+    fir_matrix_ref,
     window_ref,
     shifted_ref,
 ):
@@ -212,8 +217,8 @@
     before = jnp.where(even, outer, other[channels - HALO :])
     after = jnp.where(even, other[:HALO], outer)
     x = jnp.concatenate([before, strain_ref[...], after], axis=0)
-    spaced = jnp.dot(space_matrix_ref[...], split_rows(x), preferred_element_type=F32)
-    normed = filter_and_norm(spaced, both_ref[...], low_ref[...], window_ref[...])
+    spaced = jnp.dot(space_matrix_ref[...], data_terms(x, 0), preferred_element_type=F32)
+    normed = filter_and_norm(spaced, fir_matrix_ref[...], window_ref[...])
     length = shifted_ref.shape[1]
     padded = jnp.concatenate(
         [
@@ -298,11 +303,11 @@
     return sums
 
 
-def norm_kernel(total_ref, both_ref, low_ref, window_ref, normed_ref):
+def norm_kernel(total_ref, fir_matrix_ref, window_ref, normed_ref):
     spaced = unpack(total_ref[...])
     samples = spaced.shape[1]
     spaced = jnp.concatenate([spaced, jnp.zeros((8 - HALF_ROWS, samples), F32)], axis=0)
-    normed = filter_and_norm(spaced, both_ref[...], low_ref[...], window_ref[...])
+    normed = filter_and_norm(spaced, fir_matrix_ref[...], window_ref[...])
     normed = jnp.concatenate([normed[:, : samples // 2], normed[:, samples // 2 :]], axis=0)
     normed_ref[...] = normed.astype(BF16)
 
@@ -354,7 +359,7 @@
             jax.ShapeDtypeStruct(strain.shape, F32),
             jax.ShapeDtypeStruct((HALO, samples), F32),
             packed,
-            jax.ShapeDtypeStruct((16, 3 * channels), BF16),
+            jax.ShapeDtypeStruct((16, 6 * channels), BF16),
         ],
         in_specs=[HBM] * 3,
         out_specs=[VMEM] * 4,
@@ -392,13 +397,12 @@
             tables = pl.pallas_call(
                 tables_kernel,
                 out_shape=[
-                    jax.ShapeDtypeStruct((channels, 3 * (channels + 2 * HALO)), BF16),
-                    jax.ShapeDtypeStruct((2 * LANES, 2 * LANES), BF16),
-                    jax.ShapeDtypeStruct((LANES, 2 * LANES), BF16),
+                    jax.ShapeDtypeStruct((channels, 6 * (channels + 2 * HALO)), BF16),
+                    jax.ShapeDtypeStruct((6 * LANES, 2 * LANES), BF16),
                     jax.ShapeDtypeStruct((2 * LANES, 3 * LANES), BF16),
                 ],
                 in_specs=[HBM] * 2,
-                out_specs=[VMEM] * 4,
+                out_specs=[VMEM] * 3,
                 scratch_shapes=[
                     pltpu.SMEM(fir_taps.shape, F32),
                     pltpu.SMEM(space_taps.shape, F32),
@@ -414,7 +418,7 @@
                 out_shape=jax.ShapeDtypeStruct(
                     (LAGS // STEP * channels, samples + LANES), BF16
                 ),
-                in_specs=[VMEM] * 7,
+                in_specs=[VMEM] * 6,
                 out_specs=VMEM,
                 compiler_params=SMALL,
                 name="channels",
@@ -424,7 +428,7 @@
     mine = pl.pallas_call(
         norm_kernel,
         out_shape=jax.ShapeDtypeStruct((16, samples // 2), BF16),
-        in_specs=[VMEM] * 4,
+        in_specs=[VMEM] * 3,
         out_specs=VMEM,
         compiler_params=SMALL,
         name="norm",

time: 21.7 us -> 21.8 us (level)
  Pallas kernels: 5.56 us -> 5.82 us
  transfers between devices with their start and end apart: 8 -> 8, of which waited for: 6 -> 6; matrix products, arithmetic and copies ran while one was open for 0% -> 0% of each run, Pallas kernels for 17% -> 18%
where the time goes in v6:
time: 21.8 us; the launch traced here: 21.6 us
  starting transfers between devices  11.4 us (52%)
  Pallas kernels  5.82 us (27%)
  waiting for transfers between devices  4.31 us (20%)
    ppermute x7, starting transfers between devices, partner(): return lax.ppermute(x, AXES, [(i, i ^ mask) for i in range(devices)])  9.88 us
    ppermute x7, waiting for transfers between devices, partner(): return lax.ppermute(x, AXES, [(i, i ^ mask) for i in range(devices)])  4.31 us
    ppermute x1, starting transfers between devices, local(): outer = lax.ppermute(outer, AXES, across)  1.52 us
    pallas_call x1, Pallas kernels, local(): pl.pallas_call(second_kernel, out_shape=jax.ShapeDtypeStruct((ROWS, chann...  1.38 us
    pallas_call x1, Pallas kernels, local(): pl.pallas_call(load_kernel, out_shape=[jax.ShapeDtypeStruct(strain.shape,...  1.21 us
    pallas_call x1, Pallas kernels, local(): pl.pallas_call(channels_kernel, out_shape=jax.ShapeDtypeStruct((LAGS // S...  0.97 us
    pallas_call x1, Pallas kernels, local(): pl.pallas_call(tables_kernel, out_shape=[jax.ShapeDtypeStruct((channels,...  0.95 us
    pallas_call x1, Pallas kernels, local(): pl.pallas_call(first_kernel, out_shape=sums, in_specs=[VMEM] * 2, out_spe...  0.69 us
  transfers between devices with their start and end apart: 8, of which 6 were waited for; matrix products, arithmetic and copies ran while one was open for 0% of the time, Pallas kernels for 18%

profile of v6, /device:TPU:0, one launch (start us, length us, event | category | flops | bytes accessed | tf_op | source)
XLA Modules:
  0.0 21.6 jit_solution(5602463117198651035)
XLA Ops:
  0.0 0.5 %collective-permute-start = (f32[24,2048]{1,0:T(8,128)}, f32[24,2048]{1,0:T(8,128)S(1)}, u32[]{:S(2)}, u32[]{:S(2)}) collective-permute-start(f32[24,2048]{1,0:T(8,128)} %strain_hbm.1), channel_id=1, source_target_pairs={{0,1},{1,0},{2,3},{3,2},{4,5},{5,4},{6,7},{7,6},{8,9},{9,8},{10,11... | collective-permute-start | bytes 589832 | tf_op jit(solution)/shard_map/ppermute | solution.py:352
  0.5 1.2 %load.1 = (f32[24,2048]{1,0:T(8,128)S(1)}, f32[16,2048]{1,0:T(8,128)S(1)}, f32[8,1536]{1,0:T(8,128)S(1)}, bf16[16,144]{1,0:T(8,128)(2,1)S(1)}) custom-call(f32[24,2048]{1,0:T(8,128)} %strain_hbm.1, f32[31]{0:T(128)} %space_hbm.2, s32[3,4]{1,0:T(4,128)} %sources_hbm.1), custom_call_target="tpu_custom_call" | custom-call | tf_op jit(solution)/shard_map/load/pallas_call | solution.py:356
  1.7 0.1 collective-permute-done.other_ref
  1.7 0.2 share.1
  2.0 3.8 %collective-permute-start.1 = (f32[8,1536]{1,0:T(8,128)S(1)}, f32[8,1536]{1,0:T(8,128)S(1)}, u32[]{:S(2)}, u32[]{:S(2)}) collective-permute-start(f32[8,1536]{1,0:T(8,128)S(1)} %share.1), channel_id=1, source_target_pairs={{0,17},{1,16},{2,19},{3,18},{4,21},{5,20},{6,23},{7,22},{8,25},{9,... | collective-permute-start | bytes 147464 | tf_op jit(solution)/shard_map/ppermute | solution.py:352
  5.7 1.5 %collective-permute-start.6 = (f32[16,2048]{1,0:T(8,128)S(1)}, f32[16,2048]{1,0:T(8,128)S(1)}, u32[]{:S(2)}, u32[]{:S(2)}) collective-permute-start(f32[16,2048]{1,0:T(8,128)S(1)} %fusion), channel_id=1, source_target_pairs={{0,2},{2,1},{1,0},{31,29},{29,30},{30,31},{3,4},{4,3},{5,6},{6,5},... | collective-permute-start | bytes 393224 | tf_op jit(solution)/shard_map/ppermute | solution.py:394
  7.3 0.3 %collective-permute-done.1 = f32[8,1536]{1,0:T(8,128)S(1)} collective-permute-done((f32[8,1536]{1,0:T(8,128)S(1)}, f32[8,1536]{1,0:T(8,128)S(1)}, u32[]{:S(2)}, u32[]{:S(2)}) %collective-permute-start.1) | collective-permute-done | bytes 49184 | tf_op jit(solution)/shard_map/ppermute | solution.py:352
  7.6 2.2 %collective-permute-start.2 = (f32[8,1536]{1,0:T(8,128)S(1)}, f32[8,1536]{1,0:T(8,128)S(1)}, u32[]{:S(2)}, u32[]{:S(2)}) collective-permute-start(f32[8,1536]{1,0:T(8,128)S(1)} %add.19), channel_id=1, source_target_pairs={{0,9},{1,8},{2,11},{3,10},{4,13},{5,12},{6,15},{7,14},{8,1},{9,0},... | collective-permute-start | bytes 147464 | tf_op jit(solution)/shard_map/ppermute | solution.py:352
  9.8 0.9 %tables.1 = (bf16[24,336]{1,0:T(8,128)(2,1)S(1)}, bf16[768,256]{1,0:T(8,128)(2,1)S(1)}, bf16[256,384]{1,0:T(8,128)(2,1)S(1)}) custom-call(f32[64]{0:T(128)} %fir_hbm, f32[31]{0:T(128)} %space_hbm.2), custom_call_target="tpu_custom_call" | custom-call | tf_op jit(solution)/shard_map/tables/pallas_call | solution.py:397
  10.7 1.2 %collective-permute-done.2 = f32[8,1536]{1,0:T(8,128)S(1)} collective-permute-done((f32[8,1536]{1,0:T(8,128)S(1)}, f32[8,1536]{1,0:T(8,128)S(1)}, u32[]{:S(2)}, u32[]{:S(2)}) %collective-permute-start.2) | collective-permute-done | bytes 49184 | tf_op jit(solution)/shard_map/ppermute | solution.py:352
  11.9 2.2 %collective-permute-start.5 = (f32[8,1536]{1,0:T(8,128)S(1)}, f32[8,1536]{1,0:T(8,128)S(1)}, u32[]{:S(2)}, u32[]{:S(2)}) collective-permute-start(f32[8,1536]{1,0:T(8,128)S(1)} %add.20), channel_id=1, source_target_pairs={{0,6},{1,7},{2,4},{3,5},{4,2},{5,3},{6,0},{7,1},{8,14},{9,15},{10,... | collective-permute-start | bytes 147464 | tf_op jit(solution)/shard_map/ppermute | solution.py:352
  14.1 0.2 collective-permute-start.4
  14.3 0.9 %collective-permute-start.3 = (f32[8,1536]{1,0:T(8,128)S(1)}, f32[8,1536]{1,0:T(8,128)S(1)}, u32[]{:S(2)}, u32[]{:S(2)}) collective-permute-start(f32[8,1536]{1,0:T(8,128)S(1)} %add.20), channel_id=1, source_target_pairs={{0,5},{1,4},{2,7},{3,6},{4,1},{5,0},{6,3},{7,2},{8,13},{9,12},{10,... | collective-permute-start | bytes 147464 | tf_op jit(solution)/shard_map/ppermute | solution.py:352
  15.2 0.0 collective-permute-done.6.outer_ref
  15.2 1.0 %channels.1.shifted_ref = bf16[192,2176]{1,0:T(8,128)(2,1)S(1)} custom-call(f32[24,2048]{1,0:T(8,128)S(1)} %get-tuple-element.34.strain_ref, f32[24,2048]{1,0:T(8,128)S(1)} %collective-permute-done.other_ref, f32[16,2048]{1,0:T(8,128)S(1)} %collective-permute-done.6.outer_ref, bf16[24,336]{1,0:T(8,128)(2,1)S(1)} %get-tuple-element.36.space_matrix_ref, ...), custom_call_target="tpu_custom_call" | custom-call | tf_op jit(solution)/shard_map/channels/pallas_call | solution.py:416
  16.2 1.0 %collective-permute-done.5 = f32[8,1536]{1,0:T(8,128)S(1)} collective-permute-done((f32[8,1536]{1,0:T(8,128)S(1)}, f32[8,1536]{1,0:T(8,128)S(1)}, u32[]{:S(2)}, u32[]{:S(2)}) %collective-permute-start.5) | collective-permute-done | bytes 49184 | tf_op jit(solution)/shard_map/ppermute | solution.py:352
  17.2 1.3 %collective-permute-done.4 = f32[8,1536]{1,0:T(8,128)S(1)} collective-permute-done((f32[8,1536]{1,0:T(8,128)S(1)}, f32[8,1536]{1,0:T(8,128)S(1)}, u32[]{:S(2)}, u32[]{:S(2)}) %collective-permute-start.4) | collective-permute-done | bytes 49184 | tf_op jit(solution)/shard_map/ppermute | solution.py:352
  18.5 0.0 collective-permute-done.3
  18.6 0.4 %norm.1.normed_ref = bf16[16,1024]{1,0:T(8,128)(2,1)S(1)} custom-call(f32[8,1536]{1,0:T(8,128)S(1)} %add_add_fusion.total_ref, bf16[768,256]{1,0:T(8,128)(2,1)S(1)} %get-tuple-element.37.fir_matrix_ref, bf16[256,384]{1,0:T(8,128)(2,1)S(1)} %get-tuple-element.38.window_ref), custom_call_target="tpu_custom_call" | custom-call | tf_op jit(solution)/shard_map/norm/pallas_call | solution.py:428
  19.0 0.2 collective-permute-start.7
  19.2 0.7 %first.1.sums_ref = f32[6,24,256]{2,1,0:T(8,128)S(1)} custom-call(bf16[16,1024]{1,0:T(8,128)(2,1)S(1)} %norm.1.normed_ref, bf16[192,2176]{1,0:T(8,128)(2,1)S(1)} %channels.1.shifted_ref), custom_call_target="tpu_custom_call" | custom-call | tf_op jit(solution)/shard_map/first/pallas_call | solution.py:438
  19.9 0.4 %collective-permute-done.7.normed_ref = bf16[16,1024]{1,0:T(8,128)(2,1)S(1)} collective-permute-done((bf16[16,1024]{1,0:T(8,128)(2,1)S(1)}, bf16[16,1024]{1,0:T(8,128)(2,1)S(1)}, u32[]{:S(2)}, u32[]{:S(2)}) %collective-permute-start.7) | collective-permute-done | bytes 32800 | tf_op jit(solution)/shard_map/ppermute | solution.py:352
  20.3 1.4 %second.1 = f32[12,24,256]{2,1,0:T(8,128)} custom-call(bf16[16,1024]{1,0:T(8,128)(2,1)S(1)} %collective-permute-done.7.normed_ref, bf16[192,2176]{1,0:T(8,128)(2,1)S(1)} %channels.1.shifted_ref, f32[6,24,256]{2,1,0:T(8,128)S(1)} %first.1.sums_ref), custom_call_target="tpu_custom_call" | custom-call | tf_op jit(solution)/shard_map/second/pallas_call | solution.py:446
  (4 shorter events, 0.1 us)
Async XLA Ops:
  0.0 1.7 %collective-permute-start = (f32[24,2048]{1,0:T(8,128)}, f32[24,2048]{1,0:T(8,128)S(1)}, u32[]{:S(2)}, u32[]{:S(2)}) collective-permute-start(f32[24,2048]{1,0:T(8,128)} %strain_hbm.1), channel_id=1, source_target_pairs={{0,1},{1,0},{2,3},{3,2},{4,5},{5,4},{6,7},{7,6},{8,9},{9,8},{10,11... | collective-permute-start | bytes 589832 | tf_op jit(solution)/shard_map/ppermute | solution.py:352
  2.0 5.6 %collective-permute-start.1 = (f32[8,1536]{1,0:T(8,128)S(1)}, f32[8,1536]{1,0:T(8,128)S(1)}, u32[]{:S(2)}, u32[]{:S(2)}) collective-permute-start(f32[8,1536]{1,0:T(8,128)S(1)} %share.1), channel_id=1, source_target_pairs={{0,17},{1,16},{2,19},{3,18},{4,21},{5,20},{6,23},{7,22},{8,25},{9,... | collective-permute-start | bytes 147464 | tf_op jit(solution)/shard_map/ppermute | solution.py:352
  5.7 9.5 %collective-permute-start.6 = (f32[16,2048]{1,0:T(8,128)S(1)}, f32[16,2048]{1,0:T(8,128)S(1)}, u32[]{:S(2)}, u32[]{:S(2)}) collective-permute-start(f32[16,2048]{1,0:T(8,128)S(1)} %fusion), channel_id=1, source_target_pairs={{0,2},{2,1},{1,0},{31,29},{29,30},{30,31},{3,4},{4,3},{5,6},{6,5},... | collective-permute-start | bytes 393224 | tf_op jit(solution)/shard_map/ppermute | solution.py:394
  7.6 4.4 %collective-permute-start.2 = (f32[8,1536]{1,0:T(8,128)S(1)}, f32[8,1536]{1,0:T(8,128)S(1)}, u32[]{:S(2)}, u32[]{:S(2)}) collective-permute-start(f32[8,1536]{1,0:T(8,128)S(1)} %add.19), channel_id=1, source_target_pairs={{0,9},{1,8},{2,11},{3,10},{4,13},{5,12},{6,15},{7,14},{8,1},{9,0},... | collective-permute-start | bytes 147464 | tf_op jit(solution)/shard_map/ppermute | solution.py:352
  11.9 5.3 %collective-permute-start.5 = (f32[8,1536]{1,0:T(8,128)S(1)}, f32[8,1536]{1,0:T(8,128)S(1)}, u32[]{:S(2)}, u32[]{:S(2)}) collective-permute-start(f32[8,1536]{1,0:T(8,128)S(1)} %add.20), channel_id=1, source_target_pairs={{0,6},{1,7},{2,4},{3,5},{4,2},{5,3},{6,0},{7,1},{8,14},{9,15},{10,... | collective-permute-start | bytes 147464 | tf_op jit(solution)/shard_map/ppermute | solution.py:352
  14.1 4.4 %collective-permute-start.4 = (f32[8,1536]{1,0:T(8,128)S(1)}, f32[8,1536]{1,0:T(8,128)S(1)}, u32[]{:S(2)}, u32[]{:S(2)}) collective-permute-start(f32[8,1536]{1,0:T(8,128)S(1)} %add.20), channel_id=1, source_target_pairs={{0,3},{1,2},{2,1},{3,0},{4,7},{5,6},{6,5},{7,4},{8,11},{9,10},{10,... | collective-permute-start | bytes 147464 | tf_op jit(solution)/shard_map/ppermute | solution.py:352
  14.3 4.2 %collective-permute-start.3 = (f32[8,1536]{1,0:T(8,128)S(1)}, f32[8,1536]{1,0:T(8,128)S(1)}, u32[]{:S(2)}, u32[]{:S(2)}) collective-permute-start(f32[8,1536]{1,0:T(8,128)S(1)} %add.20), channel_id=1, source_target_pairs={{0,5},{1,4},{2,7},{3,6},{4,1},{5,0},{6,3},{7,2},{8,13},{9,12},{10,... | collective-permute-start | bytes 147464 | tf_op jit(solution)/shard_map/ppermute | solution.py:352
  19.0 1.3 %collective-permute-start.7 = (bf16[16,1024]{1,0:T(8,128)(2,1)S(1)}, bf16[16,1024]{1,0:T(8,128)(2,1)S(1)}, u32[]{:S(2)}, u32[]{:S(2)}) collective-permute-start(bf16[16,1024]{1,0:T(8,128)(2,1)S(1)} %norm.1.normed_ref), channel_id=1, source_target_pairs={{0,1},{1,0},{2,3},{3,2},{4,5},{5,4},{6,7},{7,6},{8,9},{9,8},{10,11... | collective-permute-start | bytes 98312 | tf_op jit(solution)/shard_map/ppermute | solution.py:352

commit v7 on v6

--- a/solution.py
+++ b/solution.py
@@ -178,7 +178,18 @@
     part_ref[...] = pack(part[:HALF_ROWS])
 
 
-def share_kernel(other_ref, part_ref, matrix_ref, total_ref):
+def share_kernel(other_ref, part_ref, matrix_ref, outer_ref, total_ref, sent_ref):
+    del outer_ref
+    me, channels = lax.axis_index(AXES), other_ref.shape[0]
+
+    @pl.when(me == 0)
+    def _():
+        sent_ref[...] = other_ref[channels - HALO :, :]
+
+    @pl.when(me == lax.axis_size(AXES) - 1)
+    def _():
+        sent_ref[...] = other_ref[:HALO, :]
+
     part = jnp.dot(matrix_ref[...], data_terms(other_ref[...], 0), preferred_element_type=F32)
     total_ref[...] = part_ref[...] + pack(part[:HALF_ROWS])
 
@@ -281,9 +292,10 @@
     if short:
         result = jnp.concatenate([result, jnp.zeros((result.shape[0], short), F32)], axis=1)
     lane = lax.broadcasted_iota(jnp.int32, (channels, LANES), 1)
-    sums = [[None] * (LAGS // LANES) for _ in range(rows)]
-    for h in range(LAGS // LANES):
-        for tile in range(tiles):
+    for tile in range(tiles):
+        count = min(per_tile, rows - tile * per_tile)
+        sums = [[] for _ in range(count)]
+        for h in range(LAGS // LANES):
             parts = [
                 result[
                     (h * per_tile + q) * channels : (h * per_tile + q + 1) * channels,
@@ -297,14 +309,14 @@
                         parts[q], parts[q + distance] = swap(
                             parts[q], parts[q + distance], distance * STEP, lane
                         )
-            for q in range(per_tile):
-                if tile * per_tile + q < rows:
-                    sums[tile * per_tile + q][h] = parts[q]
-    return sums
-
-
-def norm_kernel(total_ref, fir_matrix_ref, window_ref, normed_ref):
-    spaced = unpack(total_ref[...])
+            for q in range(count):
+                sums[q].append(parts[q])
+        yield tile * per_tile, [jnp.concatenate(halves, axis=1) for halves in sums]
+
+
+def norm_kernel(*refs):
+    *parts, fir_matrix_ref, window_ref, normed_ref = refs
+    spaced = unpack(sum([ref[...] for ref in parts[1:]], parts[0][...]))
     samples = spaced.shape[1]
     spaced = jnp.concatenate([spaced, jnp.zeros((8 - HALF_ROWS, samples), F32)], axis=0)
     normed = filter_and_norm(spaced, fir_matrix_ref[...], window_ref[...])
@@ -318,9 +330,9 @@
 
 
 def first_kernel(normed_ref, shifted_ref, sums_ref):
-    for k, halves in enumerate(lag_sums(shifted_ref, rows_of(normed_ref))):
-        for h, part in enumerate(halves):
-            sums_ref[k, :, h * LANES : (h + 1) * LANES] = part
+    for start, group in lag_sums(shifted_ref, rows_of(normed_ref)):
+        for k, sums in enumerate(group):
+            sums_ref[start + k] = sums
 
 
 def second_kernel(normed_ref, shifted_ref, sums_ref, out_hbm, more_ref, sems):
@@ -329,15 +341,19 @@
         sums_ref, out_hbm.at[pl.ds(mine * HALF_ROWS, HALF_ROWS)], sems.at[0]
     )
     early.start()
-    for k, halves in enumerate(lag_sums(shifted_ref, rows_of(normed_ref))):
-        for h, part in enumerate(halves):
-            more_ref[k, :, h * LANES : (h + 1) * LANES] = part
-    late = pltpu.make_async_copy(
-        more_ref, out_hbm.at[pl.ds((1 - mine) * HALF_ROWS, HALF_ROWS)], sems.at[1]
-    )
-    late.start()
-    early.wait()
-    late.wait()
+    copies = [early]
+    for start, group in lag_sums(shifted_ref, rows_of(normed_ref)):
+        for k, sums in enumerate(group):
+            more_ref[start + k] = sums
+        late = pltpu.make_async_copy(
+            more_ref.at[pl.ds(start, len(group))],
+            out_hbm.at[pl.ds((1 - mine) * HALF_ROWS + start, len(group))],
+            sems.at[len(copies)],
+        )
+        late.start()
+        copies.append(late)
+    for copy in copies:
+        copy.wait()
 
 
 def in_hbm(x):
@@ -371,23 +387,21 @@
         compiler_params=SMALL,
         name="load",
     )(*[in_hbm(x) for x in (strain, space_taps, sources)])
-    total = pl.pallas_call(
+    total, outer = pl.pallas_call(
         share_kernel,
-        out_shape=packed,
-        in_specs=[VMEM] * 3,
-        out_specs=VMEM,
+        out_shape=[packed, jax.ShapeDtypeStruct(outer.shape, F32)],
+        in_specs=[VMEM] * 4,
+        out_specs=[VMEM] * 2,
+        input_output_aliases={3: 1},
         compiler_params=SMALL,
         name="share",
-    )(beside, part, matrix)
+    )(beside, part, matrix, outer)
     across = [(0, 2), (2, 1), (1, 0)]
     across += [(devices - 1, devices - 3), (devices - 3, devices - 2), (devices - 2, devices - 1)]
     for k in range(3, devices - 4, 2):
         across += [(k, k + 1), (k + 1, k)]
-    me = lax.axis_index(AXES)
-    outer = jnp.where(me == 0, beside[channels - HALO :], outer)
-    outer = jnp.where(me == devices - 1, beside[:HALO], outer)
     steps = [1 << k for k in range(1, devices.bit_length() - 1)]
-    order = [(distance + 1,) for distance in steps[:1:-1]] + [(5, 3, 6)]
+    order = [(distance + 1,) for distance in steps[:1:-1]] + [(6, 3, 5)]
     for place, masks in enumerate(order):
         if place == 0:
             total, outer = lax.optimization_barrier((total, outer))
@@ -423,18 +437,21 @@
                 compiler_params=SMALL,
                 name="channels",
             )(near, beside, outer, *tables)
-        total = sum([partner(total, mask) for mask in masks], total)
-    total, shifted = lax.optimization_barrier((total, shifted))
+        received = [partner(total, mask) for mask in masks]
+        if place < len(order) - 1:
+            total = sum(received, total)
+    received, shifted = lax.optimization_barrier((received, shifted))
     mine = pl.pallas_call(
         norm_kernel,
         out_shape=jax.ShapeDtypeStruct((16, samples // 2), BF16),
-        in_specs=[VMEM] * 3,
+        in_specs=[VMEM] * (3 + len(received)),
         out_specs=VMEM,
         compiler_params=SMALL,
         name="norm",
-    )(total, *tables[1:])
+    )(total, *received, *tables[1:])
     other = partner(mine, 1)
     sums = jax.ShapeDtypeStruct((HALF_ROWS, channels, LAGS), F32)
+    groups = -(-HALF_ROWS * STEP // LANES)
     first = pl.pallas_call(
         first_kernel,
         out_shape=sums,
@@ -448,7 +465,7 @@
         out_shape=jax.ShapeDtypeStruct((ROWS, channels, LAGS), F32),
         in_specs=[VMEM] * 3,
         out_specs=HBM,
-        scratch_shapes=[pltpu.VMEM(sums.shape, F32), pltpu.SemaphoreType.DMA((2,))],
+        scratch_shapes=[pltpu.VMEM(sums.shape, F32), pltpu.SemaphoreType.DMA((1 + groups,))],
         compiler_params=SMALL,
         name="second",
     )(other, shifted, first)

time: 21.8 us -> 21.8 us (level)
  no operation moved by 1% of the time
where the time goes in v7:
time: 21.8 us; the launch traced here: 21.6 us
  starting transfers between devices  11.4 us (52%)
  Pallas kernels  5.82 us (27%)
  waiting for transfers between devices  4.31 us (20%)
    ppermute x7, starting transfers between devices, partner(): return lax.ppermute(x, AXES, [(i, i ^ mask) for i in range(devices)])  9.87 us
    ppermute x7, waiting for transfers between devices, partner(): return lax.ppermute(x, AXES, [(i, i ^ mask) for i in range(devices)])  4.3 us
    ppermute x1, starting transfers between devices, local(): outer = lax.ppermute(outer, AXES, across)  1.52 us
    pallas_call x1, Pallas kernels, local(): pl.pallas_call(second_kernel, out_shape=jax.ShapeDtypeStruct((ROWS, chann...  1.37 us
    pallas_call x1, Pallas kernels, local(): pl.pallas_call(load_kernel, out_shape=[jax.ShapeDtypeStruct(strain.shape,...  1.21 us
    pallas_call x1, Pallas kernels, local(): pl.pallas_call(channels_kernel, out_shape=jax.ShapeDtypeStruct((LAGS // S...  0.97 us
    pallas_call x1, Pallas kernels, local(): pl.pallas_call(tables_kernel, out_shape=[jax.ShapeDtypeStruct((channels,...  0.95 us
    pallas_call x1, Pallas kernels, local(): pl.pallas_call(first_kernel, out_shape=sums, in_specs=[VMEM] * 2, out_spe...  0.7 us
  transfers between devices with their start and end apart: 8, of which 6 were waited for; matrix products, arithmetic and copies ran while one was open for 0% of the time, Pallas kernels for 18%

profile of v7, /device:TPU:0, one launch (start us, length us, event | category | flops | bytes accessed | tf_op | source)
XLA Modules:
  0.0 21.6 jit_solution(17442542535750144795)
XLA Ops:
  0.0 0.5 %collective-permute-start = (f32[24,2048]{1,0:T(8,128)}, f32[24,2048]{1,0:T(8,128)S(1)}, u32[]{:S(2)}, u32[]{:S(2)}) collective-permute-start(f32[24,2048]{1,0:T(8,128)} %strain_hbm.1), channel_id=1, source_target_pairs={{0,1},{1,0},{2,3},{3,2},{4,5},{5,4},{6,7},{7,6},{8,9},{9,8},{10,11... | collective-permute-start | bytes 589832 | tf_op jit(solution)/shard_map/ppermute | solution.py:368
  0.5 1.2 %load.1 = (f32[24,2048]{1,0:T(8,128)S(1)}, f32[16,2048]{1,0:T(8,128)S(1)}, f32[8,1536]{1,0:T(8,128)S(1)}, bf16[16,144]{1,0:T(8,128)(2,1)S(1)}) custom-call(f32[24,2048]{1,0:T(8,128)} %strain_hbm.1, f32[31]{0:T(128)} %space_hbm.2, s32[3,4]{1,0:T(4,128)} %sources_hbm.1), custom_call_target="tpu_custom_call" | custom-call | tf_op jit(solution)/shard_map/load/pallas_call | solution.py:372
  1.7 0.1 collective-permute-done.other_ref
  1.7 0.2 share.1
  1.9 3.8 %collective-permute-start.1 = (f32[8,1536]{1,0:T(8,128)S(1)}, f32[8,1536]{1,0:T(8,128)S(1)}, u32[]{:S(2)}, u32[]{:S(2)}) collective-permute-start(f32[8,1536]{1,0:T(8,128)S(1)} %get-tuple-element.28), channel_id=1, source_target_pairs={{0,17},{1,16},{2,19},{3,18},{4,21},{5,20},{6,23},{7,22},{8,25},{9,... | collective-permute-start | bytes 147464 | tf_op jit(solution)/shard_map/ppermute | solution.py:368
  5.7 1.5 %collective-permute-start.6 = (f32[16,2048]{1,0:T(8,128)S(1)}, f32[16,2048]{1,0:T(8,128)S(1)}, u32[]{:S(2)}, u32[]{:S(2)}) collective-permute-start(f32[16,2048]{1,0:T(8,128)S(1)} %get-tuple-element.37), channel_id=1, source_target_pairs={{0,2},{2,1},{1,0},{31,29},{29,30},{30,31},{3,4},{4,3},{5,6},{6,5},... | collective-permute-start | bytes 393224 | tf_op jit(solution)/shard_map/ppermute | solution.py:408
  7.2 0.3 %collective-permute-done.1 = f32[8,1536]{1,0:T(8,128)S(1)} collective-permute-done((f32[8,1536]{1,0:T(8,128)S(1)}, f32[8,1536]{1,0:T(8,128)S(1)}, u32[]{:S(2)}, u32[]{:S(2)}) %collective-permute-start.1) | collective-permute-done | bytes 49184 | tf_op jit(solution)/shard_map/ppermute | solution.py:368
  7.5 2.2 %collective-permute-start.2 = (f32[8,1536]{1,0:T(8,128)S(1)}, f32[8,1536]{1,0:T(8,128)S(1)}, u32[]{:S(2)}, u32[]{:S(2)}) collective-permute-start(f32[8,1536]{1,0:T(8,128)S(1)} %add.6), channel_id=1, source_target_pairs={{0,9},{1,8},{2,11},{3,10},{4,13},{5,12},{6,15},{7,14},{8,1},{9,0},... | collective-permute-start | bytes 147464 | tf_op jit(solution)/shard_map/ppermute | solution.py:368
  9.7 0.9 %tables.1 = (bf16[24,336]{1,0:T(8,128)(2,1)S(1)}, bf16[768,256]{1,0:T(8,128)(2,1)S(1)}, bf16[256,384]{1,0:T(8,128)(2,1)S(1)}) custom-call(f32[64]{0:T(128)} %fir_hbm, f32[31]{0:T(128)} %space_hbm.2), custom_call_target="tpu_custom_call" | custom-call | tf_op jit(solution)/shard_map/tables/pallas_call | solution.py:411
  10.7 1.2 %collective-permute-done.2 = f32[8,1536]{1,0:T(8,128)S(1)} collective-permute-done((f32[8,1536]{1,0:T(8,128)S(1)}, f32[8,1536]{1,0:T(8,128)S(1)}, u32[]{:S(2)}, u32[]{:S(2)}) %collective-permute-start.2) | collective-permute-done | bytes 49184 | tf_op jit(solution)/shard_map/ppermute | solution.py:368
  11.9 2.2 %collective-permute-start.3 = (f32[8,1536]{1,0:T(8,128)S(1)}, f32[8,1536]{1,0:T(8,128)S(1)}, u32[]{:S(2)}, u32[]{:S(2)}) collective-permute-start(f32[8,1536]{1,0:T(8,128)S(1)} %add.7.refs_0_), channel_id=1, source_target_pairs={{0,6},{1,7},{2,4},{3,5},{4,2},{5,3},{6,0},{7,1},{8,14},{9,15},{10,... | collective-permute-start | bytes 147464 | tf_op jit(solution)/shard_map/ppermute | solution.py:368
  14.1 0.2 collective-permute-start.4
  14.3 0.9 %collective-permute-start.5 = (f32[8,1536]{1,0:T(8,128)S(1)}, f32[8,1536]{1,0:T(8,128)S(1)}, u32[]{:S(2)}, u32[]{:S(2)}) collective-permute-start(f32[8,1536]{1,0:T(8,128)S(1)} %add.7.refs_0_), channel_id=1, source_target_pairs={{0,5},{1,4},{2,7},{3,6},{4,1},{5,0},{6,3},{7,2},{8,13},{9,12},{10,... | collective-permute-start | bytes 147464 | tf_op jit(solution)/shard_map/ppermute | solution.py:368
  15.2 0.0 collective-permute-done.6.outer_ref
  15.2 1.0 %channels.1.shifted_ref = bf16[192,2176]{1,0:T(8,128)(2,1)S(1)} custom-call(f32[24,2048]{1,0:T(8,128)S(1)} %get-tuple-element.36.strain_ref, f32[24,2048]{1,0:T(8,128)S(1)} %collective-permute-done.other_ref, f32[16,2048]{1,0:T(8,128)S(1)} %collective-permute-done.6.outer_ref, bf16[24,336]{1,0:T(8,128)(2,1)S(1)} %get-tuple-element.38.space_matrix_ref, ...), custom_call_target="tpu_custom_call" | custom-call | tf_op jit(solution)/shard_map/channels/pallas_call | solution.py:430
  16.1 1.0 %collective-permute-done.3.refs_1_ = f32[8,1536]{1,0:T(8,128)S(1)} collective-permute-done((f32[8,1536]{1,0:T(8,128)S(1)}, f32[8,1536]{1,0:T(8,128)S(1)}, u32[]{:S(2)}, u32[]{:S(2)}) %collective-permute-start.3) | collective-permute-done | bytes 49184 | tf_op jit(solution)/shard_map/ppermute | solution.py:368
  17.2 1.3 %collective-permute-done.4.refs_2_ = f32[8,1536]{1,0:T(8,128)S(1)} collective-permute-done((f32[8,1536]{1,0:T(8,128)S(1)}, f32[8,1536]{1,0:T(8,128)S(1)}, u32[]{:S(2)}, u32[]{:S(2)}) %collective-permute-start.4) | collective-permute-done | bytes 49184 | tf_op jit(solution)/shard_map/ppermute | solution.py:368
  18.5 0.0 collective-permute-done.5.refs_3_
  18.5 0.4 %norm.1.normed_ref = bf16[16,1024]{1,0:T(8,128)(2,1)S(1)} custom-call(f32[8,1536]{1,0:T(8,128)S(1)} %add.7.refs_0_, f32[8,1536]{1,0:T(8,128)S(1)} %collective-permute-done.3.refs_1_, f32[8,1536]{1,0:T(8,128)S(1)} %collective-permute-done.4.refs_2_, f32[8,1536]{1,0:T(8,128)S(1)} %collective-permute-done.5.refs_3_, ...), custom_call_target="tpu_custom_call" | custom-call | tf_op jit(solution)/shard_map/norm/pallas_call | solution.py:444
  18.9 0.2 collective-permute-start.7
  19.1 0.7 %first.1.sums_ref = f32[6,24,256]{2,1,0:T(8,128)S(1)} custom-call(bf16[16,1024]{1,0:T(8,128)(2,1)S(1)} %norm.1.normed_ref, bf16[192,2176]{1,0:T(8,128)(2,1)S(1)} %channels.1.shifted_ref), custom_call_target="tpu_custom_call" | custom-call | tf_op jit(solution)/shard_map/first/pallas_call | solution.py:455
  19.8 0.4 %collective-permute-done.7.normed_ref = bf16[16,1024]{1,0:T(8,128)(2,1)S(1)} collective-permute-done((bf16[16,1024]{1,0:T(8,128)(2,1)S(1)}, bf16[16,1024]{1,0:T(8,128)(2,1)S(1)}, u32[]{:S(2)}, u32[]{:S(2)}) %collective-permute-start.7) | collective-permute-done | bytes 32800 | tf_op jit(solution)/shard_map/ppermute | solution.py:368
  20.2 1.4 %second.1 = f32[12,24,256]{2,1,0:T(8,128)} custom-call(bf16[16,1024]{1,0:T(8,128)(2,1)S(1)} %collective-permute-done.7.normed_ref, bf16[192,2176]{1,0:T(8,128)(2,1)S(1)} %channels.1.shifted_ref, f32[6,24,256]{2,1,0:T(8,128)S(1)} %first.1.sums_ref), custom_call_target="tpu_custom_call" | custom-call | tf_op jit(solution)/shard_map/second/pallas_call | solution.py:463
  (2 shorter events, 0.0 us)
Async XLA Ops:
  0.0 1.7 %collective-permute-start = (f32[24,2048]{1,0:T(8,128)}, f32[24,2048]{1,0:T(8,128)S(1)}, u32[]{:S(2)}, u32[]{:S(2)}) collective-permute-start(f32[24,2048]{1,0:T(8,128)} %strain_hbm.1), channel_id=1, source_target_pairs={{0,1},{1,0},{2,3},{3,2},{4,5},{5,4},{6,7},{7,6},{8,9},{9,8},{10,11... | collective-permute-start | bytes 589832 | tf_op jit(solution)/shard_map/ppermute | solution.py:368
  1.9 5.6 %collective-permute-start.1 = (f32[8,1536]{1,0:T(8,128)S(1)}, f32[8,1536]{1,0:T(8,128)S(1)}, u32[]{:S(2)}, u32[]{:S(2)}) collective-permute-start(f32[8,1536]{1,0:T(8,128)S(1)} %get-tuple-element.28), channel_id=1, source_target_pairs={{0,17},{1,16},{2,19},{3,18},{4,21},{5,20},{6,23},{7,22},{8,25},{9,... | collective-permute-start | bytes 147464 | tf_op jit(solution)/shard_map/ppermute | solution.py:368
  5.7 9.5 %collective-permute-start.6 = (f32[16,2048]{1,0:T(8,128)S(1)}, f32[16,2048]{1,0:T(8,128)S(1)}, u32[]{:S(2)}, u32[]{:S(2)}) collective-permute-start(f32[16,2048]{1,0:T(8,128)S(1)} %get-tuple-element.37), channel_id=1, source_target_pairs={{0,2},{2,1},{1,0},{31,29},{29,30},{30,31},{3,4},{4,3},{5,6},{6,5},... | collective-permute-start | bytes 393224 | tf_op jit(solution)/shard_map/ppermute | solution.py:408
  7.5 4.4 %collective-permute-start.2 = (f32[8,1536]{1,0:T(8,128)S(1)}, f32[8,1536]{1,0:T(8,128)S(1)}, u32[]{:S(2)}, u32[]{:S(2)}) collective-permute-start(f32[8,1536]{1,0:T(8,128)S(1)} %add.6), channel_id=1, source_target_pairs={{0,9},{1,8},{2,11},{3,10},{4,13},{5,12},{6,15},{7,14},{8,1},{9,0},... | collective-permute-start | bytes 147464 | tf_op jit(solution)/shard_map/ppermute | solution.py:368
  11.9 5.3 %collective-permute-start.3 = (f32[8,1536]{1,0:T(8,128)S(1)}, f32[8,1536]{1,0:T(8,128)S(1)}, u32[]{:S(2)}, u32[]{:S(2)}) collective-permute-start(f32[8,1536]{1,0:T(8,128)S(1)} %add.7.refs_0_), channel_id=1, source_target_pairs={{0,6},{1,7},{2,4},{3,5},{4,2},{5,3},{6,0},{7,1},{8,14},{9,15},{10,... | collective-permute-start | bytes 147464 | tf_op jit(solution)/shard_map/ppermute | solution.py:368
  14.1 4.4 %collective-permute-start.4 = (f32[8,1536]{1,0:T(8,128)S(1)}, f32[8,1536]{1,0:T(8,128)S(1)}, u32[]{:S(2)}, u32[]{:S(2)}) collective-permute-start(f32[8,1536]{1,0:T(8,128)S(1)} %add.7.refs_0_), channel_id=1, source_target_pairs={{0,3},{1,2},{2,1},{3,0},{4,7},{5,6},{6,5},{7,4},{8,11},{9,10},{10,... | collective-permute-start | bytes 147464 | tf_op jit(solution)/shard_map/ppermute | solution.py:368
  14.3 4.2 %collective-permute-start.5 = (f32[8,1536]{1,0:T(8,128)S(1)}, f32[8,1536]{1,0:T(8,128)S(1)}, u32[]{:S(2)}, u32[]{:S(2)}) collective-permute-start(f32[8,1536]{1,0:T(8,128)S(1)} %add.7.refs_0_), channel_id=1, source_target_pairs={{0,5},{1,4},{2,7},{3,6},{4,1},{5,0},{6,3},{7,2},{8,13},{9,12},{10,... | collective-permute-start | bytes 147464 | tf_op jit(solution)/shard_map/ppermute | solution.py:368
  18.9 1.3 %collective-permute-start.7 = (bf16[16,1024]{1,0:T(8,128)(2,1)S(1)}, bf16[16,1024]{1,0:T(8,128)(2,1)S(1)}, u32[]{:S(2)}, u32[]{:S(2)}) collective-permute-start(bf16[16,1024]{1,0:T(8,128)(2,1)S(1)} %norm.1.normed_ref), channel_id=1, source_target_pairs={{0,1},{1,0},{2,3},{3,2},{4,5},{5,4},{6,7},{7,6},{8,9},{9,8},{10,11... | collective-permute-start | bytes 98312 | tf_op jit(solution)/shard_map/ppermute | solution.py:368

commit v8 on v7

--- a/solution.py
+++ b/solution.py
@@ -401,7 +401,7 @@
     for k in range(3, devices - 4, 2):
         across += [(k, k + 1), (k + 1, k)]
     steps = [1 << k for k in range(1, devices.bit_length() - 1)]
-    order = [(distance + 1,) for distance in steps[:1:-1]] + [(6, 3, 5)]
+    order = [(6, 3, 5)] + [(distance + 1,) for distance in steps[2:]]
     for place, masks in enumerate(order):
         if place == 0:
             total, outer = lax.optimization_barrier((total, outer))

time: 21.8 us -> 21.7 us (level)
  starting transfers between devices: 11.4 us -> 10.6 us
  waiting for transfers between devices: 4.31 us -> 4.94 us
    ppermute x7, starting transfers between devices: 9.87 us -> 8.66 us  [partner(): return lax.ppermute(x, AXES, [(i, i ^ mask) for i in range(devices)])]
    ppermute x7, waiting for transfers between devices: 4.3 us -> 4.94 us  [partner(): return lax.ppermute(x, AXES, [(i, i ^ mask) for i in range(devices)])]
    ppermute x1, starting transfers between devices: 1.52 us -> 1.92 us  [local(): outer = lax.ppermute(outer, AXES, across)]
  transfers between devices with their start and end apart: 8 -> 8, of which waited for: 6 -> 5; matrix products, arithmetic and copies ran while one was open for 0% -> 0% of each run, Pallas kernels for 18% -> 18%
where the time goes in v8:
time: 21.7 us; the launch traced here: 21.4 us
  starting transfers between devices  10.6 us (49%)
  Pallas kernels  5.81 us (27%)
  waiting for transfers between devices  4.94 us (23%)
    ppermute x7, starting transfers between devices, partner(): return lax.ppermute(x, AXES, [(i, i ^ mask) for i in range(devices)])  8.66 us
    ppermute x7, waiting for transfers between devices, partner(): return lax.ppermute(x, AXES, [(i, i ^ mask) for i in range(devices)])  4.94 us
    ppermute x1, starting transfers between devices, local(): outer = lax.ppermute(outer, AXES, across)  1.92 us
    pallas_call x1, Pallas kernels, local(): pl.pallas_call(second_kernel, out_shape=jax.ShapeDtypeStruct((ROWS, chann...  1.37 us
    pallas_call x1, Pallas kernels, local(): pl.pallas_call(load_kernel, out_shape=[jax.ShapeDtypeStruct(strain.shape,...  1.21 us
    pallas_call x1, Pallas kernels, local(): pl.pallas_call(channels_kernel, out_shape=jax.ShapeDtypeStruct((LAGS // S...  0.97 us
    pallas_call x1, Pallas kernels, local(): pl.pallas_call(tables_kernel, out_shape=[jax.ShapeDtypeStruct((channels,...  0.95 us
    pallas_call x1, Pallas kernels, local(): pl.pallas_call(first_kernel, out_shape=sums, in_specs=[VMEM] * 2, out_spe...  0.69 us
  transfers between devices with their start and end apart: 8, of which 5 were waited for; matrix products, arithmetic and copies ran while one was open for 0% of the time, Pallas kernels for 18%

profile of v8, /device:TPU:0, one launch (start us, length us, event | category | flops | bytes accessed | tf_op | source)
XLA Modules:
  0.0 21.4 jit_solution(16334334158269925699)
XLA Ops:
  0.0 0.5 %collective-permute-start = (f32[24,2048]{1,0:T(8,128)}, f32[24,2048]{1,0:T(8,128)S(1)}, u32[]{:S(2)}, u32[]{:S(2)}) collective-permute-start(f32[24,2048]{1,0:T(8,128)} %strain_hbm.1), channel_id=1, source_target_pairs={{0,1},{1,0},{2,3},{3,2},{4,5},{5,4},{6,7},{7,6},{8,9},{9,8},{10,11... | collective-permute-start | bytes 589832 | tf_op jit(solution)/shard_map/ppermute | solution.py:368
  0.5 1.2 %load.1 = (f32[24,2048]{1,0:T(8,128)S(1)}, f32[16,2048]{1,0:T(8,128)S(1)}, f32[8,1536]{1,0:T(8,128)S(1)}, bf16[16,144]{1,0:T(8,128)(2,1)S(1)}) custom-call(f32[24,2048]{1,0:T(8,128)} %strain_hbm.1, f32[31]{0:T(128)} %space_hbm.2, s32[3,4]{1,0:T(4,128)} %sources_hbm.1), custom_call_target="tpu_custom_call" | custom-call | tf_op jit(solution)/shard_map/load/pallas_call | solution.py:372
  1.7 0.1 collective-permute-done.other_ref
  1.7 0.2 share.1
  1.9 3.9 %collective-permute-start.1 = (f32[8,1536]{1,0:T(8,128)S(1)}, f32[8,1536]{1,0:T(8,128)S(1)}, u32[]{:S(2)}, u32[]{:S(2)}) collective-permute-start(f32[8,1536]{1,0:T(8,128)S(1)} %get-tuple-element.26), channel_id=1, source_target_pairs={{0,6},{1,7},{2,4},{3,5},{4,2},{5,3},{6,0},{7,1},{8,14},{9,15},{10,... | collective-permute-start | bytes 147464 | tf_op jit(solution)/shard_map/ppermute | solution.py:368
  5.8 0.0 collective-permute-start.2
  5.8 0.4 %collective-permute-start.3 = (f32[8,1536]{1,0:T(8,128)S(1)}, f32[8,1536]{1,0:T(8,128)S(1)}, u32[]{:S(2)}, u32[]{:S(2)}) collective-permute-start(f32[8,1536]{1,0:T(8,128)S(1)} %get-tuple-element.26), channel_id=1, source_target_pairs={{0,5},{1,4},{2,7},{3,6},{4,1},{5,0},{6,3},{7,2},{8,13},{9,12},{10,... | collective-permute-start | bytes 147464 | tf_op jit(solution)/shard_map/ppermute | solution.py:368
  6.2 1.9 %collective-permute-start.6 = (f32[16,2048]{1,0:T(8,128)S(1)}, f32[16,2048]{1,0:T(8,128)S(1)}, u32[]{:S(2)}, u32[]{:S(2)}) collective-permute-start(f32[16,2048]{1,0:T(8,128)S(1)} %get-tuple-element.35), channel_id=1, source_target_pairs={{0,2},{2,1},{1,0},{31,29},{29,30},{30,31},{3,4},{4,3},{5,6},{6,5},... | collective-permute-start | bytes 393224 | tf_op jit(solution)/shard_map/ppermute | solution.py:408
  8.1 0.0 collective-permute-done.1
  8.1 1.7 %collective-permute-done.2 = f32[8,1536]{1,0:T(8,128)S(1)} collective-permute-done((f32[8,1536]{1,0:T(8,128)S(1)}, f32[8,1536]{1,0:T(8,128)S(1)}, u32[]{:S(2)}, u32[]{:S(2)}) %collective-permute-start.2) | collective-permute-done | bytes 49184 | tf_op jit(solution)/shard_map/ppermute | solution.py:368
  9.8 0.0 collective-permute-done.3
  9.8 1.4 %collective-permute-start.4 = (f32[8,1536]{1,0:T(8,128)S(1)}, f32[8,1536]{1,0:T(8,128)S(1)}, u32[]{:S(2)}, u32[]{:S(2)}) collective-permute-start(f32[8,1536]{1,0:T(8,128)S(1)} %add_add_fusion), channel_id=1, source_target_pairs={{0,9},{1,8},{2,11},{3,10},{4,13},{5,12},{6,15},{7,14},{8,1},{9,0},... | collective-permute-start | bytes 147464 | tf_op jit(solution)/shard_map/ppermute | solution.py:368
  11.2 0.9 %tables.1 = (bf16[24,336]{1,0:T(8,128)(2,1)S(1)}, bf16[768,256]{1,0:T(8,128)(2,1)S(1)}, bf16[256,384]{1,0:T(8,128)(2,1)S(1)}) custom-call(f32[64]{0:T(128)} %fir_hbm, f32[31]{0:T(128)} %space_hbm.2), custom_call_target="tpu_custom_call" | custom-call | tf_op jit(solution)/shard_map/tables/pallas_call | solution.py:411
  12.2 1.5 %collective-permute-done.4 = f32[8,1536]{1,0:T(8,128)S(1)} collective-permute-done((f32[8,1536]{1,0:T(8,128)S(1)}, f32[8,1536]{1,0:T(8,128)S(1)}, u32[]{:S(2)}, u32[]{:S(2)}) %collective-permute-start.4) | collective-permute-done | bytes 49184 | tf_op jit(solution)/shard_map/ppermute | solution.py:368
  13.6 2.4 %collective-permute-start.5 = (f32[8,1536]{1,0:T(8,128)S(1)}, f32[8,1536]{1,0:T(8,128)S(1)}, u32[]{:S(2)}, u32[]{:S(2)}) collective-permute-start(f32[8,1536]{1,0:T(8,128)S(1)} %add.15.refs_0_), channel_id=1, source_target_pairs={{0,17},{1,16},{2,19},{3,18},{4,21},{5,20},{6,23},{7,22},{8,25},{9,... | collective-permute-start | bytes 147464 | tf_op jit(solution)/shard_map/ppermute | solution.py:368
  16.0 0.0 collective-permute-done.6.outer_ref
  16.0 1.0 %channels.1.shifted_ref = bf16[192,2176]{1,0:T(8,128)(2,1)S(1)} custom-call(f32[24,2048]{1,0:T(8,128)S(1)} %get-tuple-element.34.strain_ref, f32[24,2048]{1,0:T(8,128)S(1)} %collective-permute-done.other_ref, f32[16,2048]{1,0:T(8,128)S(1)} %collective-permute-done.6.outer_ref, bf16[24,336]{1,0:T(8,128)(2,1)S(1)} %get-tuple-element.36.space_matrix_ref, ...), custom_call_target="tpu_custom_call" | custom-call | tf_op jit(solution)/shard_map/channels/pallas_call | solution.py:430
  17.0 1.3 %collective-permute-done.5.refs_1_ = f32[8,1536]{1,0:T(8,128)S(1)} collective-permute-done((f32[8,1536]{1,0:T(8,128)S(1)}, f32[8,1536]{1,0:T(8,128)S(1)}, u32[]{:S(2)}, u32[]{:S(2)}) %collective-permute-start.5) | collective-permute-done | bytes 49184 | tf_op jit(solution)/shard_map/ppermute | solution.py:368
  18.3 0.4 %norm.1.normed_ref = bf16[16,1024]{1,0:T(8,128)(2,1)S(1)} custom-call(f32[8,1536]{1,0:T(8,128)S(1)} %add.15.refs_0_, f32[8,1536]{1,0:T(8,128)S(1)} %collective-permute-done.5.refs_1_, bf16[768,256]{1,0:T(8,128)(2,1)S(1)} %get-tuple-element.37.fir_matrix_ref.refs_2_, bf16[256,384]{1,0:T(8,128)(2,1)S(1)} %get-tuple-element.38.window_ref.refs_3_), custom_call_target="tpu_custom_call" | custom-call | tf_op jit(solution)/shard_map/norm/pallas_call | solution.py:444
  18.8 0.2 collective-permute-start.7
  19.0 0.7 %first.1.sums_ref = f32[6,24,256]{2,1,0:T(8,128)S(1)} custom-call(bf16[16,1024]{1,0:T(8,128)(2,1)S(1)} %norm.1.normed_ref, bf16[192,2176]{1,0:T(8,128)(2,1)S(1)} %channels.1.shifted_ref), custom_call_target="tpu_custom_call" | custom-call | tf_op jit(solution)/shard_map/first/pallas_call | solution.py:455
  19.7 0.4 %collective-permute-done.7.normed_ref = bf16[16,1024]{1,0:T(8,128)(2,1)S(1)} collective-permute-done((bf16[16,1024]{1,0:T(8,128)(2,1)S(1)}, bf16[16,1024]{1,0:T(8,128)(2,1)S(1)}, u32[]{:S(2)}, u32[]{:S(2)}) %collective-permute-start.7) | collective-permute-done | bytes 32800 | tf_op jit(solution)/shard_map/ppermute | solution.py:368
  20.0 1.4 %second.1 = f32[12,24,256]{2,1,0:T(8,128)} custom-call(bf16[16,1024]{1,0:T(8,128)(2,1)S(1)} %collective-permute-done.7.normed_ref, bf16[192,2176]{1,0:T(8,128)(2,1)S(1)} %channels.1.shifted_ref, f32[6,24,256]{2,1,0:T(8,128)S(1)} %first.1.sums_ref), custom_call_target="tpu_custom_call" | custom-call | tf_op jit(solution)/shard_map/second/pallas_call | solution.py:463
  (2 shorter events, 0.0 us)
Async XLA Ops:
  0.0 1.7 %collective-permute-start = (f32[24,2048]{1,0:T(8,128)}, f32[24,2048]{1,0:T(8,128)S(1)}, u32[]{:S(2)}, u32[]{:S(2)}) collective-permute-start(f32[24,2048]{1,0:T(8,128)} %strain_hbm.1), channel_id=1, source_target_pairs={{0,1},{1,0},{2,3},{3,2},{4,5},{5,4},{6,7},{7,6},{8,9},{9,8},{10,11... | collective-permute-start | bytes 589832 | tf_op jit(solution)/shard_map/ppermute | solution.py:368
  1.9 6.2 %collective-permute-start.1 = (f32[8,1536]{1,0:T(8,128)S(1)}, f32[8,1536]{1,0:T(8,128)S(1)}, u32[]{:S(2)}, u32[]{:S(2)}) collective-permute-start(f32[8,1536]{1,0:T(8,128)S(1)} %get-tuple-element.26), channel_id=1, source_target_pairs={{0,6},{1,7},{2,4},{3,5},{4,2},{5,3},{6,0},{7,1},{8,14},{9,15},{10,... | collective-permute-start | bytes 147464 | tf_op jit(solution)/shard_map/ppermute | solution.py:368
  5.8 4.0 %collective-permute-start.2 = (f32[8,1536]{1,0:T(8,128)S(1)}, f32[8,1536]{1,0:T(8,128)S(1)}, u32[]{:S(2)}, u32[]{:S(2)}) collective-permute-start(f32[8,1536]{1,0:T(8,128)S(1)} %get-tuple-element.26), channel_id=1, source_target_pairs={{0,3},{1,2},{2,1},{3,0},{4,7},{5,6},{6,5},{7,4},{8,11},{9,10},{10,... | collective-permute-start | bytes 147464 | tf_op jit(solution)/shard_map/ppermute | solution.py:368
  5.8 4.0 %collective-permute-start.3 = (f32[8,1536]{1,0:T(8,128)S(1)}, f32[8,1536]{1,0:T(8,128)S(1)}, u32[]{:S(2)}, u32[]{:S(2)}) collective-permute-start(f32[8,1536]{1,0:T(8,128)S(1)} %get-tuple-element.26), channel_id=1, source_target_pairs={{0,5},{1,4},{2,7},{3,6},{4,1},{5,0},{6,3},{7,2},{8,13},{9,12},{10,... | collective-permute-start | bytes 147464 | tf_op jit(solution)/shard_map/ppermute | solution.py:368
  6.2 9.9 %collective-permute-start.6 = (f32[16,2048]{1,0:T(8,128)S(1)}, f32[16,2048]{1,0:T(8,128)S(1)}, u32[]{:S(2)}, u32[]{:S(2)}) collective-permute-start(f32[16,2048]{1,0:T(8,128)S(1)} %get-tuple-element.35), channel_id=1, source_target_pairs={{0,2},{2,1},{1,0},{31,29},{29,30},{30,31},{3,4},{4,3},{5,6},{6,5},... | collective-permute-start | bytes 393224 | tf_op jit(solution)/shard_map/ppermute | solution.py:408
  9.8 3.8 %collective-permute-start.4 = (f32[8,1536]{1,0:T(8,128)S(1)}, f32[8,1536]{1,0:T(8,128)S(1)}, u32[]{:S(2)}, u32[]{:S(2)}) collective-permute-start(f32[8,1536]{1,0:T(8,128)S(1)} %add_add_fusion), channel_id=1, source_target_pairs={{0,9},{1,8},{2,11},{3,10},{4,13},{5,12},{6,15},{7,14},{8,1},{9,0},... | collective-permute-start | bytes 147464 | tf_op jit(solution)/shard_map/ppermute | solution.py:368
  13.6 4.7 %collective-permute-start.5 = (f32[8,1536]{1,0:T(8,128)S(1)}, f32[8,1536]{1,0:T(8,128)S(1)}, u32[]{:S(2)}, u32[]{:S(2)}) collective-permute-start(f32[8,1536]{1,0:T(8,128)S(1)} %add.15.refs_0_), channel_id=1, source_target_pairs={{0,17},{1,16},{2,19},{3,18},{4,21},{5,20},{6,23},{7,22},{8,25},{9,... | collective-permute-start | bytes 147464 | tf_op jit(solution)/shard_map/ppermute | solution.py:368
  18.8 1.3 %collective-permute-start.7 = (bf16[16,1024]{1,0:T(8,128)(2,1)S(1)}, bf16[16,1024]{1,0:T(8,128)(2,1)S(1)}, u32[]{:S(2)}, u32[]{:S(2)}) collective-permute-start(bf16[16,1024]{1,0:T(8,128)(2,1)S(1)} %norm.1.normed_ref), channel_id=1, source_target_pairs={{0,1},{1,0},{2,3},{3,2},{4,5},{5,4},{6,7},{7,6},{8,9},{9,8},{10,11... | collective-permute-start | bytes 98312 | tf_op jit(solution)/shard_map/ppermute | solution.py:368

commit v9 on v8

--- a/solution.py
+++ b/solution.py
@@ -104,8 +104,8 @@
     where = lax.broadcasted_iota(jnp.int32, shape, 0) // rows * LANES
     where = where + lax.broadcasted_iota(jnp.int32, shape, 1)
     count = jnp.minimum(where, RUN) + jnp.minimum(samples - 1 - where, RUN) + 1
-    level = total / count.astype(F32)
-    return from_blocks(smooth / (level + 1e-5), rows)
+    scale = count.astype(F32)
+    return from_blocks(smooth * scale / (total + 1e-5 * scale), rows)
 
 
 def pack(x):

time: 21.7 us -> 21.7 us (level)
  no operation moved by 1% of the time
where the time goes in v9:
time: 21.7 us; the launch traced here: 21.4 us
  starting transfers between devices  10.6 us (49%)
  Pallas kernels  5.81 us (27%)
  waiting for transfers between devices  4.94 us (23%)
    ppermute x7, starting transfers between devices, partner(): return lax.ppermute(x, AXES, [(i, i ^ mask) for i in range(devices)])  8.66 us
    ppermute x7, waiting for transfers between devices, partner(): return lax.ppermute(x, AXES, [(i, i ^ mask) for i in range(devices)])  4.94 us
    ppermute x1, starting transfers between devices, local(): outer = lax.ppermute(outer, AXES, across)  1.92 us
    pallas_call x1, Pallas kernels, local(): pl.pallas_call(second_kernel, out_shape=jax.ShapeDtypeStruct((ROWS, chann...  1.37 us
    pallas_call x1, Pallas kernels, local(): pl.pallas_call(load_kernel, out_shape=[jax.ShapeDtypeStruct(strain.shape,...  1.21 us
    pallas_call x1, Pallas kernels, local(): pl.pallas_call(channels_kernel, out_shape=jax.ShapeDtypeStruct((LAGS // S...  0.97 us
    pallas_call x1, Pallas kernels, local(): pl.pallas_call(tables_kernel, out_shape=[jax.ShapeDtypeStruct((channels,...  0.95 us
    pallas_call x1, Pallas kernels, local(): pl.pallas_call(first_kernel, out_shape=sums, in_specs=[VMEM] * 2, out_spe...  0.69 us
  transfers between devices with their start and end apart: 8, of which 5 were waited for; matrix products, arithmetic and copies ran while one was open for 0% of the time, Pallas kernels for 18%

profile of v9, /device:TPU:0, one launch (start us, length us, event | category | flops | bytes accessed | tf_op | source)
XLA Modules:
  0.0 21.4 jit_solution(10826412289224446764)
XLA Ops:
  0.0 0.5 %collective-permute-start = (f32[24,2048]{1,0:T(8,128)}, f32[24,2048]{1,0:T(8,128)S(1)}, u32[]{:S(2)}, u32[]{:S(2)}) collective-permute-start(f32[24,2048]{1,0:T(8,128)} %strain_hbm.1), channel_id=1, source_target_pairs={{0,1},{1,0},{2,3},{3,2},{4,5},{5,4},{6,7},{7,6},{8,9},{9,8},{10,11... | collective-permute-start | bytes 589832 | tf_op jit(solution)/shard_map/ppermute | solution.py:368
  0.5 1.2 %load.1 = (f32[24,2048]{1,0:T(8,128)S(1)}, f32[16,2048]{1,0:T(8,128)S(1)}, f32[8,1536]{1,0:T(8,128)S(1)}, bf16[16,144]{1,0:T(8,128)(2,1)S(1)}) custom-call(f32[24,2048]{1,0:T(8,128)} %strain_hbm.1, f32[31]{0:T(128)} %space_hbm.2, s32[3,4]{1,0:T(4,128)} %sources_hbm.1), custom_call_target="tpu_custom_call" | custom-call | tf_op jit(solution)/shard_map/load/pallas_call | solution.py:372
  1.7 0.1 collective-permute-done.other_ref
  1.7 0.2 share.1
  1.9 3.9 %collective-permute-start.1 = (f32[8,1536]{1,0:T(8,128)S(1)}, f32[8,1536]{1,0:T(8,128)S(1)}, u32[]{:S(2)}, u32[]{:S(2)}) collective-permute-start(f32[8,1536]{1,0:T(8,128)S(1)} %get-tuple-element.26), channel_id=1, source_target_pairs={{0,6},{1,7},{2,4},{3,5},{4,2},{5,3},{6,0},{7,1},{8,14},{9,15},{10,... | collective-permute-start | bytes 147464 | tf_op jit(solution)/shard_map/ppermute | solution.py:368
  5.8 0.0 collective-permute-start.2
  5.8 0.4 %collective-permute-start.3 = (f32[8,1536]{1,0:T(8,128)S(1)}, f32[8,1536]{1,0:T(8,128)S(1)}, u32[]{:S(2)}, u32[]{:S(2)}) collective-permute-start(f32[8,1536]{1,0:T(8,128)S(1)} %get-tuple-element.26), channel_id=1, source_target_pairs={{0,5},{1,4},{2,7},{3,6},{4,1},{5,0},{6,3},{7,2},{8,13},{9,12},{10,... | collective-permute-start | bytes 147464 | tf_op jit(solution)/shard_map/ppermute | solution.py:368
  6.2 1.9 %collective-permute-start.6 = (f32[16,2048]{1,0:T(8,128)S(1)}, f32[16,2048]{1,0:T(8,128)S(1)}, u32[]{:S(2)}, u32[]{:S(2)}) collective-permute-start(f32[16,2048]{1,0:T(8,128)S(1)} %get-tuple-element.35), channel_id=1, source_target_pairs={{0,2},{2,1},{1,0},{31,29},{29,30},{30,31},{3,4},{4,3},{5,6},{6,5},... | collective-permute-start | bytes 393224 | tf_op jit(solution)/shard_map/ppermute | solution.py:408
  8.1 0.0 collective-permute-done.1
  8.1 1.7 %collective-permute-done.2 = f32[8,1536]{1,0:T(8,128)S(1)} collective-permute-done((f32[8,1536]{1,0:T(8,128)S(1)}, f32[8,1536]{1,0:T(8,128)S(1)}, u32[]{:S(2)}, u32[]{:S(2)}) %collective-permute-start.2) | collective-permute-done | bytes 49184 | tf_op jit(solution)/shard_map/ppermute | solution.py:368
  9.8 0.0 collective-permute-done.3
  9.8 1.4 %collective-permute-start.4 = (f32[8,1536]{1,0:T(8,128)S(1)}, f32[8,1536]{1,0:T(8,128)S(1)}, u32[]{:S(2)}, u32[]{:S(2)}) collective-permute-start(f32[8,1536]{1,0:T(8,128)S(1)} %add_add_fusion), channel_id=1, source_target_pairs={{0,9},{1,8},{2,11},{3,10},{4,13},{5,12},{6,15},{7,14},{8,1},{9,0},... | collective-permute-start | bytes 147464 | tf_op jit(solution)/shard_map/ppermute | solution.py:368
  11.2 0.9 %tables.1 = (bf16[24,336]{1,0:T(8,128)(2,1)S(1)}, bf16[768,256]{1,0:T(8,128)(2,1)S(1)}, bf16[256,384]{1,0:T(8,128)(2,1)S(1)}) custom-call(f32[64]{0:T(128)} %fir_hbm, f32[31]{0:T(128)} %space_hbm.2), custom_call_target="tpu_custom_call" | custom-call | tf_op jit(solution)/shard_map/tables/pallas_call | solution.py:411
  12.2 1.5 %collective-permute-done.4 = f32[8,1536]{1,0:T(8,128)S(1)} collective-permute-done((f32[8,1536]{1,0:T(8,128)S(1)}, f32[8,1536]{1,0:T(8,128)S(1)}, u32[]{:S(2)}, u32[]{:S(2)}) %collective-permute-start.4) | collective-permute-done | bytes 49184 | tf_op jit(solution)/shard_map/ppermute | solution.py:368
  13.6 2.4 %collective-permute-start.5 = (f32[8,1536]{1,0:T(8,128)S(1)}, f32[8,1536]{1,0:T(8,128)S(1)}, u32[]{:S(2)}, u32[]{:S(2)}) collective-permute-start(f32[8,1536]{1,0:T(8,128)S(1)} %add.15.refs_0_), channel_id=1, source_target_pairs={{0,17},{1,16},{2,19},{3,18},{4,21},{5,20},{6,23},{7,22},{8,25},{9,... | collective-permute-start | bytes 147464 | tf_op jit(solution)/shard_map/ppermute | solution.py:368
  16.0 0.0 collective-permute-done.6.outer_ref
  16.0 1.0 %channels.1.shifted_ref = bf16[192,2176]{1,0:T(8,128)(2,1)S(1)} custom-call(f32[24,2048]{1,0:T(8,128)S(1)} %get-tuple-element.34.strain_ref, f32[24,2048]{1,0:T(8,128)S(1)} %collective-permute-done.other_ref, f32[16,2048]{1,0:T(8,128)S(1)} %collective-permute-done.6.outer_ref, bf16[24,336]{1,0:T(8,128)(2,1)S(1)} %get-tuple-element.36.space_matrix_ref, ...), custom_call_target="tpu_custom_call" | custom-call | tf_op jit(solution)/shard_map/channels/pallas_call | solution.py:430
  17.0 1.3 %collective-permute-done.5.refs_1_ = f32[8,1536]{1,0:T(8,128)S(1)} collective-permute-done((f32[8,1536]{1,0:T(8,128)S(1)}, f32[8,1536]{1,0:T(8,128)S(1)}, u32[]{:S(2)}, u32[]{:S(2)}) %collective-permute-start.5) | collective-permute-done | bytes 49184 | tf_op jit(solution)/shard_map/ppermute | solution.py:368
  18.3 0.4 %norm.1.normed_ref = bf16[16,1024]{1,0:T(8,128)(2,1)S(1)} custom-call(f32[8,1536]{1,0:T(8,128)S(1)} %add.15.refs_0_, f32[8,1536]{1,0:T(8,128)S(1)} %collective-permute-done.5.refs_1_, bf16[768,256]{1,0:T(8,128)(2,1)S(1)} %get-tuple-element.37.fir_matrix_ref.refs_2_, bf16[256,384]{1,0:T(8,128)(2,1)S(1)} %get-tuple-element.38.window_ref.refs_3_), custom_call_target="tpu_custom_call" | custom-call | tf_op jit(solution)/shard_map/norm/pallas_call | solution.py:444
  18.8 0.2 collective-permute-start.7
  19.0 0.7 %first.1.sums_ref = f32[6,24,256]{2,1,0:T(8,128)S(1)} custom-call(bf16[16,1024]{1,0:T(8,128)(2,1)S(1)} %norm.1.normed_ref, bf16[192,2176]{1,0:T(8,128)(2,1)S(1)} %channels.1.shifted_ref), custom_call_target="tpu_custom_call" | custom-call | tf_op jit(solution)/shard_map/first/pallas_call | solution.py:455
  19.7 0.4 %collective-permute-done.7.normed_ref = bf16[16,1024]{1,0:T(8,128)(2,1)S(1)} collective-permute-done((bf16[16,1024]{1,0:T(8,128)(2,1)S(1)}, bf16[16,1024]{1,0:T(8,128)(2,1)S(1)}, u32[]{:S(2)}, u32[]{:S(2)}) %collective-permute-start.7) | collective-permute-done | bytes 32800 | tf_op jit(solution)/shard_map/ppermute | solution.py:368
  20.0 1.4 %second.1 = f32[12,24,256]{2,1,0:T(8,128)} custom-call(bf16[16,1024]{1,0:T(8,128)(2,1)S(1)} %collective-permute-done.7.normed_ref, bf16[192,2176]{1,0:T(8,128)(2,1)S(1)} %channels.1.shifted_ref, f32[6,24,256]{2,1,0:T(8,128)S(1)} %first.1.sums_ref), custom_call_target="tpu_custom_call" | custom-call | tf_op jit(solution)/shard_map/second/pallas_call | solution.py:463
  (2 shorter events, 0.0 us)
Async XLA Ops:
  0.0 1.7 %collective-permute-start = (f32[24,2048]{1,0:T(8,128)}, f32[24,2048]{1,0:T(8,128)S(1)}, u32[]{:S(2)}, u32[]{:S(2)}) collective-permute-start(f32[24,2048]{1,0:T(8,128)} %strain_hbm.1), channel_id=1, source_target_pairs={{0,1},{1,0},{2,3},{3,2},{4,5},{5,4},{6,7},{7,6},{8,9},{9,8},{10,11... | collective-permute-start | bytes 589832 | tf_op jit(solution)/shard_map/ppermute | solution.py:368
  1.9 6.2 %collective-permute-start.1 = (f32[8,1536]{1,0:T(8,128)S(1)}, f32[8,1536]{1,0:T(8,128)S(1)}, u32[]{:S(2)}, u32[]{:S(2)}) collective-permute-start(f32[8,1536]{1,0:T(8,128)S(1)} %get-tuple-element.26), channel_id=1, source_target_pairs={{0,6},{1,7},{2,4},{3,5},{4,2},{5,3},{6,0},{7,1},{8,14},{9,15},{10,... | collective-permute-start | bytes 147464 | tf_op jit(solution)/shard_map/ppermute | solution.py:368
  5.8 4.0 %collective-permute-start.2 = (f32[8,1536]{1,0:T(8,128)S(1)}, f32[8,1536]{1,0:T(8,128)S(1)}, u32[]{:S(2)}, u32[]{:S(2)}) collective-permute-start(f32[8,1536]{1,0:T(8,128)S(1)} %get-tuple-element.26), channel_id=1, source_target_pairs={{0,3},{1,2},{2,1},{3,0},{4,7},{5,6},{6,5},{7,4},{8,11},{9,10},{10,... | collective-permute-start | bytes 147464 | tf_op jit(solution)/shard_map/ppermute | solution.py:368
  5.8 4.0 %collective-permute-start.3 = (f32[8,1536]{1,0:T(8,128)S(1)}, f32[8,1536]{1,0:T(8,128)S(1)}, u32[]{:S(2)}, u32[]{:S(2)}) collective-permute-start(f32[8,1536]{1,0:T(8,128)S(1)} %get-tuple-element.26), channel_id=1, source_target_pairs={{0,5},{1,4},{2,7},{3,6},{4,1},{5,0},{6,3},{7,2},{8,13},{9,12},{10,... | collective-permute-start | bytes 147464 | tf_op jit(solution)/shard_map/ppermute | solution.py:368
  6.2 9.9 %collective-permute-start.6 = (f32[16,2048]{1,0:T(8,128)S(1)}, f32[16,2048]{1,0:T(8,128)S(1)}, u32[]{:S(2)}, u32[]{:S(2)}) collective-permute-start(f32[16,2048]{1,0:T(8,128)S(1)} %get-tuple-element.35), channel_id=1, source_target_pairs={{0,2},{2,1},{1,0},{31,29},{29,30},{30,31},{3,4},{4,3},{5,6},{6,5},... | collective-permute-start | bytes 393224 | tf_op jit(solution)/shard_map/ppermute | solution.py:408
  9.8 3.8 %collective-permute-start.4 = (f32[8,1536]{1,0:T(8,128)S(1)}, f32[8,1536]{1,0:T(8,128)S(1)}, u32[]{:S(2)}, u32[]{:S(2)}) collective-permute-start(f32[8,1536]{1,0:T(8,128)S(1)} %add_add_fusion), channel_id=1, source_target_pairs={{0,9},{1,8},{2,11},{3,10},{4,13},{5,12},{6,15},{7,14},{8,1},{9,0},... | collective-permute-start | bytes 147464 | tf_op jit(solution)/shard_map/ppermute | solution.py:368
  13.6 4.7 %collective-permute-start.5 = (f32[8,1536]{1,0:T(8,128)S(1)}, f32[8,1536]{1,0:T(8,128)S(1)}, u32[]{:S(2)}, u32[]{:S(2)}) collective-permute-start(f32[8,1536]{1,0:T(8,128)S(1)} %add.15.refs_0_), channel_id=1, source_target_pairs={{0,17},{1,16},{2,19},{3,18},{4,21},{5,20},{6,23},{7,22},{8,25},{9,... | collective-permute-start | bytes 147464 | tf_op jit(solution)/shard_map/ppermute | solution.py:368
  18.8 1.3 %collective-permute-start.7 = (bf16[16,1024]{1,0:T(8,128)(2,1)S(1)}, bf16[16,1024]{1,0:T(8,128)(2,1)S(1)}, u32[]{:S(2)}, u32[]{:S(2)}) collective-permute-start(bf16[16,1024]{1,0:T(8,128)(2,1)S(1)} %norm.1.normed_ref), channel_id=1, source_target_pairs={{0,1},{1,0},{2,3},{3,2},{4,5},{5,4},{6,7},{7,6},{8,9},{9,8},{10,11... | collective-permute-start | bytes 98312 | tf_op jit(solution)/shard_map/ppermute | solution.py:368
